TPU v7x, 512 devices: a whole 4x8x8 slice. The times are simulated.
512 devices in a mesh: section: 16 (over y, x_lo), expert: 32 (over z, x_hi, core).
Axes of the slice: x: 4 (x_hi: 2, x_lo: 2; x = x_hi * 2 + x_lo), y: 8, z: 8, core: 2. Of those that a mesh axis runs over, the one named last changes fastest.
Arguments:
- left_x: bfloat16 [16, 2048, 3584], P('section', 'expert'), may hold values from -6 to 6
- left_cot: bfloat16 [16, 2048, 3584], P('section', 'expert'), may hold values from -6 to 6
- left_experts: int32 [16, 2048, 8], P('section', 'expert'), may hold values from 0 to 127, all different within a row; in each aligned block of 64 rows (0 to 63, 64 to 127, ..., all dimensions but the last counted through in order) at most 6 rows name the same one
- left_gates: float32 [16, 2048, 8], P('section', 'expert'), may hold values from 0.1 to 1
- right_x: bfloat16 [16, 2048, 3584], P('section', 'expert'), may hold values from -6 to 6
- right_cot: bfloat16 [16, 2048, 3584], P('section', 'expert'), may hold values from -6 to 6
- right_experts: int32 [16, 2048, 8], P('section', 'expert'), may hold values from 0 to 127, all different within a row; in each aligned block of 64 rows (0 to 63, 64 to 127, ..., all dimensions but the last counted through in order) at most 6 rows name the same one
- right_gates: float32 [16, 2048, 8], P('section', 'expert'), may hold values from 0.1 to 1
- up_weight: bfloat16 [16, 3584, 2048], P('section', None, 'expert'), may hold values from -0.09375 to 0.09375
- down_weight: bfloat16 [16, 3584, 2048], P('section', None, 'expert'), may hold values from -0.1875 to 0.1875
Outputs:
- left_grad_in: bfloat16 [16, 2048, 3584], P('section', 'expert')
- right_grad_in: bfloat16 [16, 2048, 3584], P('section', 'expert')
- layer_grad: bfloat16 [16, 3584, 4096], P('section', None, 'expert')
Inputs may be any that keep to these rules, and one draw needn't show every extreme that they name: `left_experts`: in each device's 64 tokens no expert is named by more than 6 assignments, a bound that some block reaches; a token's 8 experts differ. `right_experts`: as for left_experts.
All inputs are finite; a program needn't handle non-finite values.
Results may differ from a plain program's by a relative error of at most 0.013.
Values may be sent and summed in bfloat16 or wider, within the bound.
No kernel may reach another device: no remote copies, remote signals or barrier semaphores. Data moves between devices by JAX's collectives and lax.ppermute only.
A program may use at most 64 MiB of HBM per device.

v0:
```python
import jax
import jax.numpy as jnp
from jax import lax
from jax.sharding import PartitionSpec as P

EXPERTS = 2
CAP = 6


def partner(value, axis, bit):
    mask = 2**bit
    pairs = [(source, source ^ mask) for source in range(lax.axis_size(axis))]
    return lax.ppermute(value, axis, pairs)


def shifted(block, axis, distance):
    devices = range(lax.axis_size(axis))
    route = [(i - distance, i) for i in devices if i - distance in devices]
    return lax.ppermute(block, axis, route)


def slot_tables(experts, gates, n_exp, cap):
    tok, top = experts.shape
    flat = experts.reshape(-1)
    onehot = (flat[:, None] == jnp.arange(n_exp, dtype=jnp.int32)[None, :]).astype(jnp.int32)
    earlier = jnp.cumsum(onehot, axis=0) - onehot
    rank = jnp.sum(earlier * onehot, axis=1)
    position = (flat * cap + rank).reshape(tok, top)
    slots = jnp.arange(n_exp * cap, dtype=jnp.int32)
    hit = position[None, :, :] == slots[:, None, None]
    placed = jnp.sum(hit.astype(jnp.float32), axis=2)
    weighted = jnp.sum(jnp.where(hit, gates[None, :, :], jnp.float32(0.0)), axis=2)
    return (placed, weighted)


def mirror(block):
    moved = block
    for bit in range(lax.axis_size("section").bit_length() - 1):
        moved = partner(moved, "section", bit)
    return moved


def expert_backward(got_x, got_g, packed):
    sources, cap, width = got_x.shape
    part = packed.shape[1] // 2
    w_up = packed[:, :part]
    w_down = packed[:, part:]
    inputs = got_x.reshape(sources * cap, width)
    scaled = got_g.reshape(sources * cap, width)
    act = jnp.dot(inputs, w_up, preferred_element_type=jnp.float32)
    sig = jax.nn.sigmoid(act)
    hid = (act * sig).astype(jnp.bfloat16)
    back_h = jnp.dot(scaled, w_down, preferred_element_type=jnp.float32)
    d_act = (back_h * sig * (1.0 + act * (1.0 - sig))).astype(jnp.bfloat16)
    grad_up = lax.dot_general(
        inputs, d_act, (((0,), (0,)), ((), ())), preferred_element_type=jnp.float32
    )
    grad_down = lax.dot_general(
        scaled, hid, (((0,), (0,)), ((), ())), preferred_element_type=jnp.float32
    )
    grad = jnp.concatenate([grad_up, grad_down], 1).astype(jnp.bfloat16)
    d_part = lax.dot_general(
        d_act, w_up, (((1,), (1,)), ((), ())), preferred_element_type=jnp.float32
    )
    return (d_part.astype(jnp.bfloat16).reshape(sources, cap, width), grad)


def prepare(tokens, cot, experts, gates, groups):
    width = tokens.shape[1]
    placed, weighted = slot_tables(experts, gates, EXPERTS, CAP)
    sent_x = jnp.dot(
        placed.astype(jnp.bfloat16), tokens, preferred_element_type=jnp.float32
    ).astype(jnp.bfloat16)
    sent_g = jnp.dot(weighted, cot.astype(jnp.float32), precision=lax.Precision.HIGHEST).astype(
        jnp.bfloat16
    )
    sent_x = jnp.repeat(sent_x.reshape(EXPERTS, CAP, width), groups, axis=0)
    sent_g = jnp.repeat(sent_g.reshape(EXPERTS, CAP, width), groups, axis=0)
    return (placed, sent_x, sent_g)


def finish(placed, cot, returned, groups):
    width = cot.shape[1]
    summed = jnp.sum(returned.reshape(EXPERTS, groups, CAP, width).astype(jnp.float32), axis=1)
    summed = summed.reshape(EXPERTS * CAP, width)
    total = cot.astype(jnp.float32) + jnp.dot(placed.T, summed, precision=lax.Precision.HIGHEST)
    return total.astype(jnp.bfloat16)


def on_device(
    left_x,
    left_cot,
    left_experts,
    left_gates,
    right_x,
    right_cot,
    right_experts,
    right_gates,
    up_weight,
    down_weight,
):
    groups = lax.axis_size("expert") // EXPERTS
    near = jnp.concatenate([up_weight[0], down_weight[0]], 1)
    far = mirror(near)
    left_in = (left_x[0], left_cot[0], left_experts[0], left_gates[0])
    right_in = (right_x[0], right_cot[0], right_experts[0], right_gates[0])

    def one_stream(stream, packed):
        placed, sent_x, sent_g = prepare(stream[0], stream[1], stream[2], stream[3], groups)
        got_x, got_g = (
            lax.all_to_all(sent_x, "expert", split_axis=0, concat_axis=0, tiled=True),
            lax.all_to_all(sent_g, "expert", split_axis=0, concat_axis=0, tiled=True),
        )
        d_part, grad = expert_backward(got_x, got_g, packed)
        returned = lax.all_to_all(d_part, "expert", split_axis=0, concat_axis=0, tiled=True)
        return (finish(placed, stream[1], returned, groups), grad)

    dx_left, near_grad = one_stream(left_in, near)
    dx_right, far_grad = one_stream(right_in, far)
    left_grad_in = shifted(dx_left[None], "section", -1)
    right_grad_in = shifted(dx_right[None], "section", 1)
    mirrored = mirror(far_grad)
    layer_grad = (near_grad.astype(jnp.float32) + mirrored.astype(jnp.float32)).astype(jnp.bfloat16)
    return (left_grad_in, right_grad_in, layer_grad[None])


def solution(mesh):
    return jax.shard_map(
        on_device,
        mesh=mesh,
        in_specs=(
            P("section", "expert", None),
            P("section", "expert", None),
            P("section", "expert", None),
            P("section", "expert", None),
            P("section", "expert", None),
            P("section", "expert", None),
            P("section", "expert", None),
            P("section", "expert", None),
            P("section", None, "expert"),
            P("section", None, "expert"),
        ),
        out_specs=(
            P("section", "expert", None),
            P("section", "expert", None),
            P("section", None, "expert"),
        ),
        check_vma=False,
    )
```

profile of v0, /device:TPU:15, one launch (start us, length us, event | category | flops | bytes accessed | tf_op | source)
XLA Modules:
  0.0 452.4 jit_solution(9083672934565059912)
XLA Ops:
  0.6 0.8 copy.43
  1.7 0.6 reduce-window.16
  2.9 0.7 add_bitcast_fusion
  3.6 0.7 select_reduce_fusion
  4.6 1.4 broadcast_in_dim.56
  6.0 13.9 %all-to-all-start.4 = ((bf16[32,6,3584]{2,1,0:T(8,128)(2,1)}), bf16[32,6,3584]{2,1,0:T(8,128)(2,1)S(1)}, u32[]{:S(2)}, u32[]{:S(2)}) async-start(bf16[32,6,3584]{2,1,0:T(8,128)(2,1)} %bitcast.101), calls=%async_computation.4 | async-start | bytes 3670016 | tf_op jit(solution)/shard_map/all_to_all | solution.py:111
  20.2 0.6 reduce-window.14
  21.7 42.7 %all-to-all-done.4 = bf16[32,6,3584]{2,1,0:T(8,128)(2,1)S(1)} async-done(((bf16[32,6,3584]{2,1,0:T(8,128)(2,1)}), bf16[32,6,3584]{2,1,0:T(8,128)(2,1)S(1)}, u32[]{:S(2)}, u32[]{:S(2)}) %all-to-all-start.4) | async-done | bytes 1376288 | tf_op jit(solution)/shard_map/all_to_all | solution.py:111
  64.4 1.5 broadcast_in_dim.51
  65.9 0.3 copy-done.1
  66.3 6.3 %all-to-all-start.1 = ((bf16[32,6,3584]{2,1,0:T(8,128)(2,1)}), bf16[32,6,3584]{2,1,0:T(8,128)(2,1)}, u32[]{:S(2)}, u32[]{:S(2)}) async-start(bf16[32,6,3584]{2,1,0:T(8,128)(2,1)} %bitcast.103), calls=%async_computation.1 | async-start | bytes 3670016 | tf_op jit(solution)/shard_map/all_to_all | solution.py:111
  72.5 0.3 convolution_convert_fusion.9
  72.9 44.3 %all-to-all-done.1 = bf16[32,6,3584]{2,1,0:T(8,128)(2,1)} async-done(((bf16[32,6,3584]{2,1,0:T(8,128)(2,1)}), bf16[32,6,3584]{2,1,0:T(8,128)(2,1)}, u32[]{:S(2)}, u32[]{:S(2)}) %all-to-all-start.1) | async-done | bytes 1376288 | tf_op jit(solution)/shard_map/all_to_all | solution.py:111
  117.2 1.4 broadcast_in_dim.50
  118.5 6.3 %all-to-all-start = ((bf16[32,6,3584]{2,1,0:T(8,128)(2,1)}), bf16[32,6,3584]{2,1,0:T(8,128)(2,1)S(1)}, u32[]{:S(2)}, u32[]{:S(2)}) async-start(bf16[32,6,3584]{2,1,0:T(8,128)(2,1)} %bitcast.102), calls=%async_computation | async-start | bytes 3670016 | tf_op jit(solution)/shard_map/all_to_all | solution.py:112
  124.9 1.0 pad_maximum_fusion
  125.9 2.4 collective-permute-start.1
  128.4 0.3 convolution_convert_fusion.7
  128.7 40.7 %all-to-all-done = bf16[32,6,3584]{2,1,0:T(8,128)(2,1)S(1)} async-done(((bf16[32,6,3584]{2,1,0:T(8,128)(2,1)}), bf16[32,6,3584]{2,1,0:T(8,128)(2,1)S(1)}, u32[]{:S(2)}, u32[]{:S(2)}) %all-to-all-start) | async-done | bytes 1376288 | tf_op jit(solution)/shard_map/all_to_all | solution.py:112
  169.5 1.5 broadcast_in_dim.55
  171.3 6.3 %all-to-all-start.3 = ((bf16[32,6,3584]{2,1,0:T(8,128)(2,1)}), bf16[32,6,3584]{2,1,0:T(8,128)(2,1)}, u32[]{:S(2)}, u32[]{:S(2)}) async-start(bf16[32,6,3584]{2,1,0:T(8,128)(2,1)} %bitcast.100), calls=%async_computation.3 | async-start | bytes 3670016 | tf_op jit(solution)/shard_map/all_to_all | solution.py:112
  177.6 2.1 collective-permute-start.2
  179.7 21.7 %collective-permute-done.2 = bf16[3584,128]{0,1:T(8,128)(2,1)} collective-permute-done((bf16[3584,128]{0,1:T(8,128)(2,1)}, bf16[3584,128]{0,1:T(8,128)(2,1)}, u32[]{:S(2)}, u32[]{:S(2)}) %collective-permute-start.2) | collective-permute-done | bytes 917536 | tf_op jit(solution)/shard_map/ppermute | solution.py:13
  201.3 4.2 collective-permute-start.3
  205.6 2.5 reshape.102
  208.0 2.5 reshape.99
  210.5 2.0 fusion.30
  212.5 0.6 fusion.6
  213.1 32.4 %collective-permute-done.3 = bf16[3584,128]{0,1:T(8,128)(2,1)} collective-permute-done((bf16[3584,128]{0,1:T(8,128)(2,1)}, bf16[3584,128]{0,1:T(8,128)(2,1)}, u32[]{:S(2)}, u32[]{:S(2)}) %collective-permute-start.3) | collective-permute-done | bytes 917536 | tf_op jit(solution)/shard_map/ppermute | solution.py:13
  245.5 4.0 collective-permute-start.4
  249.5 0.5 convolution_convert_fusion.1
  250.0 1.5 reshape.103
  251.6 11.1 %all-to-all-start.2 = ((bf16[32,6,3584]{2,1,0:T(8,128)(2,1)}), bf16[32,6,3584]{2,1,0:T(8,128)(2,1)}, u32[]{:S(2)}, u32[]{:S(2)}) async-start(bf16[32,6,3584]{2,1,0:T(8,128)(2,1)} %reshape.103), calls=%async_computation.2 | async-start | bytes 3670016 | tf_op jit(solution)/shard_map/all_to_all | solution.py:115
  262.7 2.5 reshape.111
  265.1 3.5 reshape.108
  268.7 5.1 %collective-permute-done.4 = bf16[3584,128]{0,1:T(8,128)(2,1)} collective-permute-done((bf16[3584,128]{0,1:T(8,128)(2,1)}, bf16[3584,128]{0,1:T(8,128)(2,1)}, u32[]{:S(2)}, u32[]{:S(2)}) %collective-permute-start.4) | collective-permute-done | bytes 917536 | tf_op jit(solution)/shard_map/ppermute | solution.py:13
  273.8 1.6 fusion.15
  275.3 1.6 fusion.7
  276.9 0.4 convolution_convert_fusion.3
  277.3 0.4 convolution_convert_fusion.2
  277.7 1.0 pad_maximum_fusion.1
  278.7 2.4 collective-permute-start.6
  281.1 1.6 convolution_convert_fusion
  282.7 1.5 reshape.112
  284.2 23.1 %all-to-all-done.2 = bf16[32,6,3584]{2,1,0:T(8,128)(2,1)} async-done(((bf16[32,6,3584]{2,1,0:T(8,128)(2,1)}), bf16[32,6,3584]{2,1,0:T(8,128)(2,1)}, u32[]{:S(2)}, u32[]{:S(2)}) %all-to-all-start.2) | async-done | bytes 1376288 | tf_op jit(solution)/shard_map/all_to_all | solution.py:115
  307.3 6.3 %all-to-all-start.5 = ((bf16[32,6,3584]{2,1,0:T(8,128)(2,1)}), bf16[32,6,3584]{2,1,0:T(8,128)(2,1)}, u32[]{:S(2)}, u32[]{:S(2)}) async-start(bf16[32,6,3584]{2,1,0:T(8,128)(2,1)} %reshape.112), calls=%async_computation.5 | async-start | bytes 3670016 | tf_op jit(solution)/shard_map/all_to_all | solution.py:115
  313.6 11.6 %collective-permute-start.7 = (bf16[3584,128]{0,1:T(8,128)(2,1)}, bf16[3584,128]{0,1:T(8,128)(2,1)}, u32[]{:S(2)}, u32[]{:S(2)}) collective-permute-start(bf16[3584,128]{0,1:T(8,128)(2,1)} %collective-permute-done.6), channel_id=1, source_target_pairs={{0,64},{32,96},{64,0},{96,32},{128,192},{160,224},{192,128},{224,1... | collective-permute-start | bytes 2752520 | tf_op jit(solution)/shard_map/ppermute | solution.py:13
  325.3 14.5 %collective-permute-done.7 = bf16[3584,128]{0,1:T(8,128)(2,1)} collective-permute-done((bf16[3584,128]{0,1:T(8,128)(2,1)}, bf16[3584,128]{0,1:T(8,128)(2,1)}, u32[]{:S(2)}, u32[]{:S(2)}) %collective-permute-start.7) | collective-permute-done | bytes 917536 | tf_op jit(solution)/shard_map/ppermute | solution.py:13
  339.8 10.3 %collective-permute-start.8 = (bf16[3584,128]{0,1:T(8,128)(2,1)}, bf16[3584,128]{0,1:T(8,128)(2,1)}, u32[]{:S(2)}, u32[]{:S(2)}) collective-permute-start(bf16[3584,128]{0,1:T(8,128)(2,1)} %collective-permute-done.7), channel_id=1, source_target_pairs={{0,128},{32,160},{64,192},{96,224},{128,0},{160,32},{192,64},{224,... | collective-permute-start | bytes 2752520 | tf_op jit(solution)/shard_map/ppermute | solution.py:13
  350.1 1.9 convert_reduce_fusion.1
  352.0 38.1 %collective-permute-done.8 = bf16[3584,128]{0,1:T(8,128)(2,1)} collective-permute-done((bf16[3584,128]{0,1:T(8,128)(2,1)}, bf16[3584,128]{0,1:T(8,128)(2,1)}, u32[]{:S(2)}, u32[]{:S(2)}) %collective-permute-start.8) | collective-permute-done | bytes 917536 | tf_op jit(solution)/shard_map/ppermute | solution.py:13
  390.1 5.2 %collective-permute-start.9 = (bf16[3584,128]{0,1:T(8,128)(2,1)}, bf16[3584,128]{0,1:T(8,128)(2,1)}, u32[]{:S(2)}, u32[]{:S(2)}) collective-permute-start(bf16[3584,128]{0,1:T(8,128)(2,1)} %collective-permute-done.8), channel_id=1, source_target_pairs={{0,256},{32,288},{64,320},{96,352},{128,384},{160,416},{192,448},{... | collective-permute-start | bytes 2752520 | tf_op jit(solution)/shard_map/ppermute | solution.py:13
  395.2 1.7 fusion.3
  397.0 2.1 collective-permute-start
  399.1 1.9 convert_reduce_fusion
  401.0 0.9 fusion.2
  402.0 4.2 collective-permute-start.5
  406.2 0.4 convolution_convert_fusion.5
  406.6 0.4 convolution_convert_fusion.4
  406.9 41.2 %collective-permute-done = bf16[1,64,3584]{2,1,0:T(8,128)(2,1)S(1)} collective-permute-done((bf16[1,64,3584]{2,1,0:T(8,128)(2,1)}, bf16[1,64,3584]{2,1,0:T(8,128)(2,1)S(1)}, u32[]{:S(2)}, u32[]{:S(2)}) %collective-permute-start) | collective-permute-done | bytes 458784 | tf_op jit(solution)/shard_map/ppermute | solution.py:19
  448.2 1.4 fusion.8
  449.6 1.3 copy.46
  450.8 0.8 copy.53
  451.6 0.8 copy.54
  (68 shorter events, 2.7 us)
Async XLA Ops:
  0.6 3.7 copy-start
  6.0 13.9 %copy-start.15 = (s32[1,64,8]{1,2,0:T(8,128)S(1)}, s32[1,64,8]{1,2,0:T(8,128)}, u32[]{:S(2)}) copy-start(s32[1,64,8]{1,2,0:T(8,128)} %param.12) | copy-start | bytes 6148
  6.0 15.5 %copy-start.16 = (f32[1,64,8]{1,2,0:T(8,128)S(1)}, f32[1,64,8]{1,2,0:T(8,128)}, u32[]{:S(2)}) copy-start(f32[1,64,8]{1,2,0:T(8,128)} %param.13) | copy-start | bytes 6148
  6.0 15.5 %copy-start.14 = (bf16[1,64,3584]{2,1,0:T(8,128)(2,1)S(1)}, bf16[1,64,3584]{2,1,0:T(8,128)(2,1)}, u32[]{:S(2)}) copy-start(bf16[1,64,3584]{2,1,0:T(8,128)(2,1)} %param.10) | copy-start | bytes 1376260
  6.0 58.5 %all-to-all-start.4 = ((bf16[32,6,3584]{2,1,0:T(8,128)(2,1)}), bf16[32,6,3584]{2,1,0:T(8,128)(2,1)S(1)}, u32[]{:S(2)}, u32[]{:S(2)}) async-start(bf16[32,6,3584]{2,1,0:T(8,128)(2,1)} %bitcast.101), calls=%async_computation.4 | async-start | bytes 3670016 | tf_op jit(solution)/shard_map/all_to_all | solution.py:111
  64.4 1.8 copy-start.1
  65.9 6.6 %copy-start.8 = (bf16[1,64,3584]{2,1,0:T(8,128)(2,1)S(1)}, bf16[1,64,3584]{2,1,0:T(8,128)(2,1)}, u32[]{:S(2)}) copy-start(bf16[1,64,3584]{2,1,0:T(8,128)(2,1)} %param.11) | copy-start | bytes 1376260
  66.3 50.9 %all-to-all-start.1 = ((bf16[32,6,3584]{2,1,0:T(8,128)(2,1)}), bf16[32,6,3584]{2,1,0:T(8,128)(2,1)}, u32[]{:S(2)}, u32[]{:S(2)}) async-start(bf16[32,6,3584]{2,1,0:T(8,128)(2,1)} %bitcast.103), calls=%async_computation.1 | async-start | bytes 3670016 | tf_op jit(solution)/shard_map/all_to_all | solution.py:111
  118.5 6.4 %copy-start.6 = (bf16[1,3584,64]{1,2,0:T(8,128)(2,1)S(1)}, bf16[1,3584,64]{1,2,0:T(8,128)(2,1)}, u32[]{:S(2)}) copy-start(bf16[1,3584,64]{1,2,0:T(8,128)(2,1)} %param.18) | copy-start | bytes 1376260
  118.5 6.4 %copy-start.12 = (bf16[1,3584,64]{1,2,0:T(8,128)(2,1)S(1)}, bf16[1,3584,64]{1,2,0:T(8,128)(2,1)}, u32[]{:S(2)}) copy-start(bf16[1,3584,64]{1,2,0:T(8,128)(2,1)} %param.19) | copy-start | bytes 1376260
  118.5 50.9 %all-to-all-start = ((bf16[32,6,3584]{2,1,0:T(8,128)(2,1)}), bf16[32,6,3584]{2,1,0:T(8,128)(2,1)S(1)}, u32[]{:S(2)}, u32[]{:S(2)}) async-start(bf16[32,6,3584]{2,1,0:T(8,128)(2,1)} %bitcast.102), calls=%async_computation | async-start | bytes 3670016 | tf_op jit(solution)/shard_map/all_to_all | solution.py:112
  124.9 3.5 copy-start.10
  125.9 51.7 %collective-permute-start.1 = (bf16[3584,128]{0,1:T(8,128)(2,1)}, bf16[3584,128]{0,1:T(8,128)(2,1)}, u32[]{:S(2)}, u32[]{:S(2)}) collective-permute-start(bf16[3584,128]{0,1:T(8,128)(2,1)} %pad_maximum_fusion), channel_id=1, source_target_pairs={{0,32},{32,0},{64,96},{96,64},{128,160},{160,128},{192,224},{224,1... | collective-permute-start | bytes 2752520 | tf_op jit(solution)/shard_map/ppermute | solution.py:13
  169.5 1.8 copy-start.2
  171.3 80.3 %all-to-all-start.3 = ((bf16[32,6,3584]{2,1,0:T(8,128)(2,1)}), bf16[32,6,3584]{2,1,0:T(8,128)(2,1)}, u32[]{:S(2)}, u32[]{:S(2)}) async-start(bf16[32,6,3584]{2,1,0:T(8,128)(2,1)} %bitcast.100), calls=%async_computation.3 | async-start | bytes 3670016 | tf_op jit(solution)/shard_map/all_to_all | solution.py:112
  177.6 23.8 %collective-permute-start.2 = (bf16[3584,128]{0,1:T(8,128)(2,1)}, bf16[3584,128]{0,1:T(8,128)(2,1)}, u32[]{:S(2)}, u32[]{:S(2)}) collective-permute-start(bf16[3584,128]{0,1:T(8,128)(2,1)} %collective-permute-done.1), channel_id=1, source_target_pairs={{0,64},{32,96},{64,0},{96,32},{128,192},{160,224},{192,128},{224,1... | collective-permute-start | bytes 2752520 | tf_op jit(solution)/shard_map/ppermute | solution.py:13
  201.3 44.1 %collective-permute-start.3 = (bf16[3584,128]{0,1:T(8,128)(2,1)}, bf16[3584,128]{0,1:T(8,128)(2,1)}, u32[]{:S(2)}, u32[]{:S(2)}) collective-permute-start(bf16[3584,128]{0,1:T(8,128)(2,1)} %collective-permute-done.2), channel_id=1, source_target_pairs={{0,128},{32,160},{64,192},{96,224},{128,0},{160,32},{192,64},{224,... | collective-permute-start | bytes 2752520 | tf_op jit(solution)/shard_map/ppermute | solution.py:13
  210.5 2.6 copy-start.3
  210.5 2.0 copy-start.13
  212.5 37.0 %copy-start.7 = (bf16[1,3584,64]{1,2,0:T(8,128)(2,1)S(1)}, bf16[1,3584,64]{1,2,0:T(8,128)(2,1)}, u32[]{:S(2)}) copy-start(bf16[1,3584,64]{1,2,0:T(8,128)(2,1)} %param.18) | copy-start | bytes 1376260
  245.5 28.3 %collective-permute-start.4 = (bf16[3584,128]{0,1:T(8,128)(2,1)}, bf16[3584,128]{0,1:T(8,128)(2,1)}, u32[]{:S(2)}, u32[]{:S(2)}) collective-permute-start(bf16[3584,128]{0,1:T(8,128)(2,1)} %collective-permute-done.3), channel_id=1, source_target_pairs={{0,256},{32,288},{64,320},{96,352},{128,384},{160,416},{192,448},{... | collective-permute-start | bytes 2752520 | tf_op jit(solution)/shard_map/ppermute | solution.py:13
  251.6 55.7 %all-to-all-start.2 = ((bf16[32,6,3584]{2,1,0:T(8,128)(2,1)}), bf16[32,6,3584]{2,1,0:T(8,128)(2,1)}, u32[]{:S(2)}, u32[]{:S(2)}) async-start(bf16[32,6,3584]{2,1,0:T(8,128)(2,1)} %reshape.103), calls=%async_computation.2 | async-start | bytes 3670016 | tf_op jit(solution)/shard_map/all_to_all | solution.py:115
  268.7 6.7 %copy-start.5 = (bf16[192,3584]{1,0:T(8,128)(2,1)S(1)}, bf16[192,3584]{1,0:T(8,128)(2,1)}, u32[]{:S(2)}) copy-start(bf16[192,3584]{1,0:T(8,128)(2,1)} %reshape.108) | copy-start | bytes 4128772
  278.7 34.9 %collective-permute-start.6 = (bf16[3584,128]{0,1:T(8,128)(2,1)}, bf16[3584,128]{0,1:T(8,128)(2,1)}, u32[]{:S(2)}, u32[]{:S(2)}) collective-permute-start(bf16[3584,128]{0,1:T(8,128)(2,1)} %pad_maximum_fusion.1), channel_id=1, source_target_pairs={{0,32},{32,0},{64,96},{96,64},{128,160},{160,128},{192,224},{224,1... | collective-permute-start | bytes 2752520 | tf_op jit(solution)/shard_map/ppermute | solution.py:13
  307.3 91.8 %all-to-all-start.5 = ((bf16[32,6,3584]{2,1,0:T(8,128)(2,1)}), bf16[32,6,3584]{2,1,0:T(8,128)(2,1)}, u32[]{:S(2)}, u32[]{:S(2)}) async-start(bf16[32,6,3584]{2,1,0:T(8,128)(2,1)} %reshape.112), calls=%async_computation.5 | async-start | bytes 3670016 | tf_op jit(solution)/shard_map/all_to_all | solution.py:115
  313.6 81.7 %copy-start.9 = (bf16[1,64,3584]{2,1,0:T(8,128)(2,1)S(1)}, bf16[1,64,3584]{2,1,0:T(8,128)(2,1)}, u32[]{:S(2)}) copy-start(bf16[1,64,3584]{2,1,0:T(8,128)(2,1)} %param.11) | copy-start | bytes 1376260
  313.6 26.2 %collective-permute-start.7 = (bf16[3584,128]{0,1:T(8,128)(2,1)}, bf16[3584,128]{0,1:T(8,128)(2,1)}, u32[]{:S(2)}, u32[]{:S(2)}) collective-permute-start(bf16[3584,128]{0,1:T(8,128)(2,1)} %collective-permute-done.6), channel_id=1, source_target_pairs={{0,64},{32,96},{64,0},{96,32},{128,192},{160,224},{192,128},{224,1... | collective-permute-start | bytes 2752520 | tf_op jit(solution)/shard_map/ppermute | solution.py:13
  339.8 50.3 %collective-permute-start.8 = (bf16[3584,128]{0,1:T(8,128)(2,1)}, bf16[3584,128]{0,1:T(8,128)(2,1)}, u32[]{:S(2)}, u32[]{:S(2)}) collective-permute-start(bf16[3584,128]{0,1:T(8,128)(2,1)} %collective-permute-done.7), channel_id=1, source_target_pairs={{0,128},{32,160},{64,192},{96,224},{128,0},{160,32},{192,64},{224,... | collective-permute-start | bytes 2752520 | tf_op jit(solution)/shard_map/ppermute | solution.py:13
  390.1 58.1 %collective-permute-start.9 = (bf16[3584,128]{0,1:T(8,128)(2,1)}, bf16[3584,128]{0,1:T(8,128)(2,1)}, u32[]{:S(2)}, u32[]{:S(2)}) collective-permute-start(bf16[3584,128]{0,1:T(8,128)(2,1)} %collective-permute-done.8), channel_id=1, source_target_pairs={{0,256},{32,288},{64,320},{96,352},{128,384},{160,416},{192,448},{... | collective-permute-start | bytes 2752520 | tf_op jit(solution)/shard_map/ppermute | solution.py:13
  397.0 4.1 copy-start.11
  397.0 51.2 %collective-permute-start = (bf16[1,64,3584]{2,1,0:T(8,128)(2,1)}, bf16[1,64,3584]{2,1,0:T(8,128)(2,1)S(1)}, u32[]{:S(2)}, u32[]{:S(2)}) collective-permute-start(bf16[1,64,3584]{2,1,0:T(8,128)(2,1)} %fusion.3), channel_id=1, source_target_pairs={{32,0},{64,32},{96,64},{128,96},{160,128},{192,160},{224,192},{256... | collective-permute-start | bytes 1376264 | tf_op jit(solution)/shard_map/ppermute | solution.py:19
  401.0 5.5 %copy-start.4 = (bf16[192,3584]{1,0:T(8,128)(2,1)S(1)}, bf16[192,3584]{1,0:T(8,128)(2,1)}, u32[]{:S(2)}) copy-start(bf16[192,3584]{1,0:T(8,128)(2,1)} %copy-done.3) | copy-start | bytes 4128772
  402.0 46.2 %collective-permute-start.5 = (bf16[1,64,3584]{2,1,0:T(8,128)(2,1)S(1)}, bf16[1,64,3584]{2,1,0:T(8,128)(2,1)S(1)}, u32[]{:S(2)}, u32[]{:S(2)}) collective-permute-start(bf16[1,64,3584]{2,1,0:T(8,128)(2,1)S(1)} %fusion.2), channel_id=1, source_target_pairs={{0,32},{32,64},{64,96},{96,128},{128,160},{160,192},{192,224},{224... | collective-permute-start | bytes 1376264 | tf_op jit(solution)/shard_map/ppermute | solution.py:19
where the time goes:
time: 454 us; the launch traced here: 452 us
  waiting for transfers between devices  304 us (67%)
  starting transfers between devices  98.6 us (22%)
  local copies, waits for them, and re-layouts  25.4 us (6%)
  matrix products  12.8 us (3%)
  other arithmetic  10.4 us (2%)
    ppermute x8, waiting for transfers between devices, partner(): return lax.ppermute(value, axis, pairs)  112 us
    all_to_all x2, waiting for transfers between devices, one_stream(): lax.all_to_all(sent_x, 'expert', split_axis=0, concat_axis=0, tiled=True)  87 us
    ppermute x8, starting transfers between devices, partner(): return lax.ppermute(value, axis, pairs)  42.3 us
    ppermute x2, waiting for transfers between devices, shifted(): return lax.ppermute(block, axis, route)  41.2 us
    all_to_all x2, waiting for transfers between devices, one_stream(): lax.all_to_all(sent_g, 'expert', split_axis=0, concat_axis=0, tiled=True)  40.8 us
    all_to_all x2, waiting for transfers between devices, one_stream(): lax.all_to_all(d_part, 'expert', split_axis=0, concat_axis=0, tiled=True)  23.1 us
    all_to_all x2, starting transfers between devices, one_stream(): lax.all_to_all(sent_x, 'expert', split_axis=0, concat_axis=0, tiled=True)  20.1 us
    all_to_all x2, starting transfers between devices, one_stream(): lax.all_to_all(d_part, 'expert', split_axis=0, concat_axis=0, tiled=True)  17.4 us
  transfers between devices with their start and end apart: 16, of which 10 were waited for; matrix products, arithmetic and copies ran while one was open for 8% of the time, Pallas kernels for 0%

commit v1 on v0

v1 whole, which is shorter than its diff:
```python
import jax
import jax.numpy as jnp
from jax import lax
from jax.sharding import PartitionSpec as P

EXPERTS = 2
CAP = 6
BOTH = ("section", "expert")


def send(value, axis, route):
    size = lax.axis_size(axis)
    pairs = [(i, route(i)) for i in range(size)]
    return lax.ppermute(value, axis, [(a, b) for a, b in pairs if 0 <= b < size])


def slot_table(experts, order):
    hit = (experts[:, :, None] == order[None, None, :]).astype(jnp.float32)
    named = jnp.sum(hit, axis=1)
    rank = jnp.cumsum(named, axis=0) - named
    slots = jnp.arange(CAP, dtype=jnp.float32)
    table = named[:, :, None] * (rank[:, :, None] == slots).astype(jnp.float32)
    return hit, table


def dispatch(tokens, cot, experts, gates, order):
    half = tokens.shape[1] // 2
    hit, table = slot_table(experts, order)
    gate = jnp.sum(hit * gates[:, :, None], axis=1)
    slot_gate = jnp.sum(table * gate[:, :, None], axis=0)
    pick = table.astype(jnp.bfloat16)
    xs = jnp.einsum("ter,td->erd", pick, tokens, preferred_element_type=jnp.float32)
    cs = jnp.einsum("ter,td->erd", pick, cot, preferred_element_type=jnp.float32)
    xs = xs.astype(jnp.bfloat16)
    gs = (cs * slot_gate[:, :, None]).astype(jnp.bfloat16)
    kinds = [xs[..., :half], gs[..., :half], xs[..., half:], gs[..., half:]]
    return jnp.stack(kinds, axis=1)


def on_device(
    left_x,
    left_cot,
    left_experts,
    left_gates,
    right_x,
    right_cot,
    right_experts,
    right_gates,
    up_weight,
    down_weight,
):
    n_sec = lax.axis_size("section")
    n_exp = lax.axis_size("expert")
    groups = n_exp // EXPERTS
    width = left_x.shape[2]
    half = width // 2
    part = up_weight.shape[2]
    place = lax.axis_index("expert")
    own = place // groups
    core = place % 2
    order = jnp.stack([own, 1 - own]).astype(jnp.int32)

    left = dispatch(left_x[0], left_cot[0], left_experts[0], left_gates[0], order)
    right = dispatch(right_x[0], right_cot[0], right_experts[0], right_gates[0], order)

    def far(i):
        return (n_sec - 1 - i // n_exp) * n_exp + (i % n_exp + groups) % n_exp

    left_far = send(left[1], "expert", lambda j: (j + groups) % n_exp)
    right_near = send(right[0], "section", lambda s: n_sec - 1 - s)
    right_far = send(right[1], BOTH, far)

    next_cot = send(left_cot[0], "section", lambda s: s - 1)
    last_cot = send(right_cot[0], "section", lambda s: s + 1)
    next_experts = send(left_experts[0], "section", lambda s: s - 1)
    last_experts = send(right_experts[0], "section", lambda s: s + 1)

    shard = jnp.stack([left[0], right_near, left_far, right_far], axis=1)
    shard = shard.reshape(16 * CAP, half)
    same = [list(range(e * groups, (e + 1) * groups)) for e in range(EXPERTS)]
    rows = lax.all_gather(shard, "expert", axis=0, tiled=True, axis_index_groups=same)

    up, down = up_weight[0], down_weight[0]
    weights = jnp.concatenate([up[:half], down[:half], up[half:], down[half:]], axis=1)
    both = jnp.dot(rows, weights, preferred_element_type=jnp.float32)
    both = both.reshape(groups, 4, 4 * CAP, 4 * part)
    act = both[:, 0, :, :part] + both[:, 2, :, 2 * part : 3 * part]
    back_h = both[:, 1, :, part : 2 * part] + both[:, 3, :, 3 * part :]
    sig = jax.nn.sigmoid(act)
    hid = (act * sig).astype(jnp.bfloat16)
    d_act = (back_h * sig * (1.0 + act * (1.0 - sig))).astype(jnp.bfloat16)
    none = jnp.zeros_like(hid)
    spread = jnp.stack(
        [
            jnp.concatenate([d_act, none, none, none], axis=2),
            jnp.concatenate([none, hid, none, none], axis=2),
            jnp.concatenate([none, none, d_act, none], axis=2),
            jnp.concatenate([none, none, none, hid], axis=2),
        ],
        axis=1,
    ).reshape(groups * 16 * CAP, 4 * part)
    grad = lax.dot_general(
        rows, spread, (((0,), (0,)), ((), ())), preferred_element_type=jnp.float32
    ).astype(jnp.bfloat16)
    grad = jnp.concatenate([grad[:, : 2 * part], grad[:, 2 * part :]], axis=0)

    slots = lax.dot_general(
        d_act.reshape(-1, part), up, (((1,), (1,)), ((), ())), preferred_element_type=jnp.float32
    ).astype(jnp.bfloat16)
    slots = slots.reshape(groups // 2, 2, 4 * CAP, width)
    kept = lax.dynamic_index_in_dim(slots, core, 1, keepdims=False)
    given = lax.dynamic_index_in_dim(slots, 1 - core, 1, keepdims=False)
    got = send(given, "expert", lambda j: j ^ 1)
    summed = (kept.astype(jnp.float32) + got.astype(jnp.float32)).astype(jnp.bfloat16)
    summed = summed.reshape(groups // 2, 2, 2 * CAP, 2, half).transpose(1, 0, 3, 2, 4)
    summed = jnp.where(own == 0, summed, summed[::-1])
    summed = summed.reshape(groups * 4 * CAP, half)
    cores = [list(range(c, n_exp, 2)) for c in range(2)]
    back = lax.all_to_all(
        summed, "expert", split_axis=0, concat_axis=0, tiled=True, axis_index_groups=cores
    )
    back = back.reshape(EXPERTS, groups // 2, 2, 2, CAP, half).astype(jnp.float32)
    back = jnp.sum(back, axis=1).astype(jnp.bfloat16)
    back = back.transpose(2, 0, 3, 1, 4).reshape(2, EXPERTS * CAP, width)

    next_slots = send(back[0], "section", lambda s: s - 1)
    last_slots = send(back[1], "section", lambda s: n_sec - s)

    def finish(cot, experts, slots):
        _, table = slot_table(experts, jnp.arange(EXPERTS, dtype=jnp.int32))
        table = table.reshape(-1, EXPERTS * CAP).astype(jnp.bfloat16)
        added = jnp.dot(table, slots, preferred_element_type=jnp.float32)
        return (cot.astype(jnp.float32) + added).astype(jnp.bfloat16)[None]

    left_grad_in = finish(next_cot, next_experts, next_slots)
    right_grad_in = finish(last_cot, last_experts, last_slots)
    return left_grad_in, right_grad_in, grad[None]


def solution(mesh):
    return jax.shard_map(
        on_device,
        mesh=mesh,
        in_specs=(
            P("section", "expert", None),
            P("section", "expert", None),
            P("section", "expert", None),
            P("section", "expert", None),
            P("section", "expert", None),
            P("section", "expert", None),
            P("section", "expert", None),
            P("section", "expert", None),
            P("section", None, "expert"),
            P("section", None, "expert"),
        ),
        out_specs=(
            P("section", "expert", None),
            P("section", "expert", None),
            P("section", None, "expert"),
        ),
        check_vma=False,
    )
```

time: 454 us -> 182 us (0.40)
  the two profiles are of different devices: /device:TPU:15 before, /device:TPU:26 now
where the time goes in v1:
time: 182 us
  waiting for transfers between devices  83.4 us (46%)
  starting transfers between devices  51.6 us (28%)
  matrix products  15.4 us (8%)
  between operations  14.6 us (8%)
  local copies, waits for them, and re-layouts  9.06 us (5%)
  other arithmetic  7.51 us (4%)
    all_gather x1, waiting for transfers between devices, on_device(): lax.all_gather(shard, 'expert', axis=0, tiled=True, axis_index_groups=same)  44.9 us
    ppermute x10, starting transfers between devices, send(): lax.ppermute(value, axis, [(a, b) for a, b in pairs if 0 <= b < size])  44.6 us
    ppermute x10, waiting for transfers between devices, send(): lax.ppermute(value, axis, [(a, b) for a, b in pairs if 0 <= b < size])  20.8 us
    all_to_all x1, waiting for transfers between devices, on_device(): lax.all_to_all(summed, 'expert', split_axis=0, concat_axis=0, tiled=True,...  17.7 us
    all_to_all x1, starting transfers between devices, on_device(): lax.all_to_all(summed, 'expert', split_axis=0, concat_axis=0, tiled=True,...  7 us
    dot_general x2, matrix products, finish(): added = jnp.dot(table, slots, preferred_element_type=jnp.float32)  4.31 us
    dot_general x1, matrix products, on_device(): both = jnp.dot(rows, weights, preferred_element_type=jnp.float32)  4.31 us
    dot_general x1, matrix products, on_device(): lax.dot_general(rows, spread, (((0,), (0,)), ((), ())), preferred_element...  4.2 us
  transfers between devices with their start and end apart: 12, of which 6 were waited for; matrix products, arithmetic and copies ran while one was open for 5% of the time, Pallas kernels for 0%

profile of v1, /device:TPU:26, one launch (start us, length us, event | category | flops | bytes accessed | tf_op | source)
XLA Modules:
  0.0 181.6 jit_solution(7734052797139265479)
XLA Ops:
  7.3 0.1 pad_add_fusion
  7.3 0.9 fusion.27
  8.2 0.1 copy.113
  8.3 0.1 reduce_window_sum.23
  8.4 0.1 copy.115
  8.5 0.1 copy.117
  8.6 0.1 reduce_window_sum.27
  8.7 0.1 copy.119
  8.8 0.1 fusion.31
  8.9 1.2 fusion
  10.1 0.2 convolution_convert_fusion.2
  10.4 0.1 pad_maximum_fusion.2
  10.4 10.9 %collective-permute-start.3 = (bf16[4,6,1792]{2,1,0:T(8,128)(2,1)S(1)}, bf16[4,6,1792]{2,1,0:T(8,128)(2,1)S(1)}, u32[]{:S(2)}, u32[]{:S(2)}) collective-permute-start(bf16[4,6,1792]{2,1,0:T(8,128)(2,1)S(1)} %get-tuple-element.18), channel_id=1, source_target_pairs={{0,16},{1,17},{2,18},{3,19},{4,20},{5,21},{6,22},{7,23},{8,24},{9,... | collective-permute-start | bytes 258056 | tf_op jit(solution)/shard_map/ppermute | solution.py:14
  21.4 0.2 fusion.1
  21.6 0.2 convolution_convert_fusion.1
  21.9 4.8 %collective-permute-start.2 = (bf16[4,6,1792]{2,1,0:T(8,128)(2,1)S(1)}, bf16[4,6,1792]{2,1,0:T(8,128)(2,1)S(1)}, u32[]{:S(2)}, u32[]{:S(2)}) collective-permute-start(bf16[4,6,1792]{2,1,0:T(8,128)(2,1)S(1)} %get-tuple-element.19), channel_id=1, source_target_pairs={{0,480},{32,448},{64,416},{96,384},{128,352},{160,320},{192,288},{... | collective-permute-start | bytes 258056 | tf_op jit(solution)/shard_map/ppermute | solution.py:14
  26.7 2.7 %collective-permute-start.4 = (bf16[4,6,1792]{2,1,0:T(8,128)(2,1)S(1)}, bf16[4,6,1792]{2,1,0:T(8,128)(2,1)S(1)}, u32[]{:S(2)}, u32[]{:S(2)}) collective-permute-start(bf16[4,6,1792]{2,1,0:T(8,128)(2,1)S(1)} %get-tuple-element.20), channel_id=1, source_target_pairs={{0,496},{1,497},{2,498},{3,499},{4,500},{5,501},{6,502},{7,503},{8... | collective-permute-start | bytes 258056 | tf_op jit(solution)/shard_map/ppermute | solution.py:14
  29.5 5.4 %collective-permute-done.2 = bf16[4,6,1792]{2,1,0:T(8,128)(2,1)S(1)} collective-permute-done((bf16[4,6,1792]{2,1,0:T(8,128)(2,1)S(1)}, bf16[4,6,1792]{2,1,0:T(8,128)(2,1)S(1)}, u32[]{:S(2)}, u32[]{:S(2)}) %collective-permute-start.2) | collective-permute-done | bytes 86048 | tf_op jit(solution)/shard_map/ppermute | solution.py:14
  34.9 8.4 %collective-permute-done.4 = bf16[4,6,1792]{2,1,0:T(8,128)(2,1)S(1)} collective-permute-done((bf16[4,6,1792]{2,1,0:T(8,128)(2,1)S(1)}, bf16[4,6,1792]{2,1,0:T(8,128)(2,1)S(1)}, u32[]{:S(2)}, u32[]{:S(2)}) %collective-permute-start.4) | collective-permute-done | bytes 86048 | tf_op jit(solution)/shard_map/ppermute | solution.py:14
  43.3 0.1 pad_maximum_fusion.1
  43.5 0.8 reshape.107
  44.5 44.9 %all-gather.2.cloned.1.call-done = bf16[1536,1792]{1,0:T(8,128)(2,1)} async-done(((bf16[96,1792]{1,0:T(8,128)(2,1)}), bf16[1536,1792]{1,0:T(8,128)(2,1)}) %all-gather.2.cloned.1.call-update) | async-done | bytes 5505040 | tf_op jit(solution)/shard_map/all_gather | solution.py:81
  89.3 4.3 %fusion.3 = f32[1536,256]{1,0:T(8,128)S(1)} fusion(bf16[1536,1792]{1,0:T(8,128)(2,1)} %all-gather.2.cloned.1.call-done, bf16[1792,64]{0,1:T(8,128)(2,1)S(1)} %get-tuple-element.16, bf16[1792,64]{0,1:T(8,128)(2,1)S(1)} %get-tuple-element.37, bf16[1792,64]{0,1:T(8,128)(2,1)S(1)} %get-tuple-element.15, bf16[1792,64]{0,1:T(8,128)(2,1)S(1)} %get-tuple-element.38), kind=kOutput, calls=%fused_computation.13 | convolution fusion | flops 1412956160 | bytes 7995392 | tf_op jit(solution)/shard_map/dot_general | solution.py:85
  93.7 0.2 multiply_convert_fusion
  93.9 0.9 convolution_convert_fusion
  94.7 0.1 copy-done.3
  94.8 1.2 dynamic-slice_bitcast_fusion
  96.1 2.1 %collective-permute-start.5 = (bf16[8,24,3584]{2,1,0:T(8,128)(2,1)}, bf16[8,24,3584]{2,1,0:T(8,128)(2,1)}, u32[]{:S(2)}, u32[]{:S(2)}) collective-permute-start(bf16[8,24,3584]{2,1,0:T(8,128)(2,1)} %dynamic-slice_bitcast_fusion), channel_id=1, source_target_pairs={{0,1},{1,0},{2,3},{3,2},{4,5},{5,4},{6,7},{7,6},{8,9},{9,8},{10,11... | collective-permute-start | bytes 4128776 | tf_op jit(solution)/shard_map/ppermute | solution.py:14
  98.2 3.2 %collective-permute-done.5 = bf16[8,24,3584]{2,1,0:T(8,128)(2,1)} collective-permute-done((bf16[8,24,3584]{2,1,0:T(8,128)(2,1)}, bf16[8,24,3584]{2,1,0:T(8,128)(2,1)}, u32[]{:S(2)}, u32[]{:S(2)}) %collective-permute-start.5) | collective-permute-done | bytes 1376288 | tf_op jit(solution)/shard_map/ppermute | solution.py:14
  101.4 2.8 %fusion.2 = bf16[8,24,3584]{2,1,0:T(8,128)(2,1)} fusion(bf16[8,24,3584]{2,1,0:T(8,128)(2,1)} %collective-permute-done.5, bf16[8,2,24,3584]{3,2,1,0:T(8,128)(2,1)S(1)} %bitcast.188, s32[]{:T(128)S(6)} %select_n.29), kind=kLoop, calls=%fused_computation.8 | loop fusion | flops 2752512 | bytes 4128772 | tf_op jit(solution)/shard_map/convert_element_type | solution.py:114
  104.3 3.2 %reshape.110 = bf16[8,2,12,2,1792]{4,3,2,1,0:T(2,128)(2,1)S(1)} reshape(bf16[8,24,3584]{2,1,0:T(8,128)(2,1)} %fusion.2) | data formatting | bytes 2752512 | tf_op jit(solution)/shard_map/reshape | solution.py:115
  107.5 1.1 broadcast_select_fusion
  108.6 0.4 copy.128
  109.0 1.5 copy.129
  110.5 7.0 %all-to-all-start = ((bf16[16,24,1792]{2,1,0:T(8,128)(2,1)}), bf16[16,24,1792]{2,1,0:T(8,128)(2,1)S(1)}, u32[]{:S(2)}, u32[]{:S(2)}) async-start(bf16[16,24,1792]{2,1,0:T(8,128)(2,1)} %copy.129), calls=%async_computation | async-start | bytes 2752512 | tf_op jit(solution)/shard_map/all_to_all | solution.py:119
  117.5 5.4 %collective-permute-start.8 = (s32[64,8]{0,1:T(8,128)S(1)}, s32[64,8]{0,1:T(8,128)S(1)}, u32[]{:S(2)}, u32[]{:S(2)}) collective-permute-start(s32[64,8]{0,1:T(8,128)S(1)} %bitcast.210), channel_id=1, source_target_pairs={{0,32},{32,64},{64,96},{96,128},{128,160},{160,192},{192,224},{224... | collective-permute-start | bytes 6152 | tf_op jit(solution)/shard_map/ppermute | solution.py:14
  122.9 1.9 %collective-permute-start.1 = (s32[64,8]{0,1:T(8,128)S(1)}, s32[64,8]{0,1:T(8,128)S(1)}, u32[]{:S(2)}, u32[]{:S(2)}) collective-permute-start(s32[64,8]{0,1:T(8,128)S(1)} %bitcast.212), channel_id=1, source_target_pairs={{32,0},{64,32},{96,64},{128,96},{160,128},{192,160},{224,192},{256... | collective-permute-start | bytes 6152 | tf_op jit(solution)/shard_map/ppermute | solution.py:14
  124.8 6.0 %collective-permute-start.7 = (bf16[64,3584]{1,0:T(8,128)(2,1)}, bf16[64,3584]{1,0:T(8,128)(2,1)}, u32[]{:S(2)}, u32[]{:S(2)}) collective-permute-start(bf16[64,3584]{1,0:T(8,128)(2,1)} %bitcast.197), channel_id=1, source_target_pairs={{0,32},{32,64},{64,96},{96,128},{128,160},{160,192},{192,224},{224... | collective-permute-start | bytes 1376264 | tf_op jit(solution)/shard_map/ppermute | solution.py:14
  130.9 1.9 %collective-permute-start = (bf16[64,3584]{1,0:T(8,128)(2,1)}, bf16[64,3584]{1,0:T(8,128)(2,1)}, u32[]{:S(2)}, u32[]{:S(2)}) collective-permute-start(bf16[64,3584]{1,0:T(8,128)(2,1)} %bitcast.198), channel_id=1, source_target_pairs={{32,0},{64,32},{96,64},{128,96},{160,128},{192,160},{224,192},{256... | collective-permute-start | bytes 1376264 | tf_op jit(solution)/shard_map/ppermute | solution.py:14
  132.8 0.1 eq.129
  132.9 0.1 copy.132
  133.0 0.1 reduce_window_sum.32
  133.1 0.1 copy.134
  133.3 0.1 copy.110
  133.4 0.1 reduce_window_sum.22
  133.5 0.1 copy.112
  133.6 0.2 fusion.25
  133.8 0.2 maximum_bitcast_fusion.1
  134.1 0.1 pad_maximum_fusion
  134.2 4.2 %convolution_convert_fusion.3 = bf16[1792,256]{1,0:T(8,128)(2,1)S(1)} fusion(bf16[1536,1792]{1,0:T(8,128)(2,1)} %all-gather.2.cloned.1.call-done, bf16[1536,256]{1,0:T(8,128)(2,1)S(1)} %bitcast.193), kind=kOutput, calls=%fused_computation.10 | convolution fusion | flops 1409744896 | bytes 7208960 | tf_op jit(solution)/shard_map/dot_general | solution.py:102
  138.4 17.7 %all-to-all-done = bf16[16,24,1792]{2,1,0:T(8,128)(2,1)S(1)} async-done(((bf16[16,24,1792]{2,1,0:T(8,128)(2,1)}), bf16[16,24,1792]{2,1,0:T(8,128)(2,1)S(1)}, u32[]{:S(2)}, u32[]{:S(2)}) %all-to-all-start) | async-done | bytes 1376288 | tf_op jit(solution)/shard_map/all_to_all | solution.py:119
  156.1 0.2 bitcast_reduce_fusion
  156.3 0.1 copy.138
  156.5 0.1 fusion.59
  156.6 0.1 copy.135
  156.7 0.1 pad.33
  156.8 5.9 %collective-permute-start.9 = (bf16[12,3584]{1,0:T(8,128)(2,1)S(1)}, bf16[12,3584]{1,0:T(8,128)(2,1)S(1)}, u32[]{:S(2)}, u32[]{:S(2)}) collective-permute-start(bf16[12,3584]{1,0:T(8,128)(2,1)S(1)} %bitcast.205), channel_id=1, source_target_pairs={{32,480},{64,448},{96,416},{128,384},{160,352},{192,320},{224,288}... | collective-permute-start | bytes 258056 | tf_op jit(solution)/shard_map/ppermute | solution.py:14
  162.7 1.0 maximum_bitcast_fusion
  163.6 0.1 copy.131
  163.7 0.1 pad.32
  163.8 2.8 %collective-permute-start.6 = (bf16[12,3584]{1,0:T(8,128)(2,1)S(1)}, bf16[12,3584]{1,0:T(8,128)(2,1)S(1)}, u32[]{:S(2)}, u32[]{:S(2)}) collective-permute-start(bf16[12,3584]{1,0:T(8,128)(2,1)S(1)} %bitcast.206), channel_id=1, source_target_pairs={{32,0},{64,32},{96,64},{128,96},{160,128},{192,160},{224,192},{256... | collective-permute-start | bytes 258056 | tf_op jit(solution)/shard_map/ppermute | solution.py:14
  166.7 2.2 %fusion.12 = bf16[1,64,3584]{2,1,0:T(8,128)(2,1)} fusion(bf16[64,3584]{1,0:T(8,128)(2,1)} %collective-permute-done.7, bf16[12,3584]{1,0:T(8,128)(2,1)S(1)} %collective-permute-done.9, bf16[64,12]{0,1:T(8,128)(2,1)S(1)} %mul.137, f32[64,12]{0,1:T(8,128)S(1)} %eq.149, f32[12]{0:T(128)S(1)} %eq.129), kind=kOutput, calls=%fused_computation.26 | convolution fusion | flops 6194688 | bytes 1008176 | tf_op jit(solution)/shard_map/dot_general | solution.py:132
  168.9 3.8 %collective-permute-done.6 = bf16[12,3584]{1,0:T(8,128)(2,1)S(1)} collective-permute-done((bf16[12,3584]{1,0:T(8,128)(2,1)S(1)}, bf16[12,3584]{1,0:T(8,128)(2,1)S(1)}, u32[]{:S(2)}, u32[]{:S(2)}) %collective-permute-start.6) | collective-permute-done | bytes 86048 | tf_op jit(solution)/shard_map/ppermute | solution.py:14
  172.6 2.2 %fusion.11 = bf16[1,64,3584]{2,1,0:T(8,128)(2,1)} fusion(bf16[64,3584]{1,0:T(8,128)(2,1)} %collective-permute-done, bf16[12,3584]{1,0:T(8,128)(2,1)S(1)} %collective-permute-done.6, bf16[64,12]{0,1:T(8,128)(2,1)S(1)} %mul.113, f32[64,12]{0,1:T(8,128)S(1)} %eq.127, f32[12]{0:T(128)S(1)} %eq.129), kind=kOutput, calls=%fused_computation.25 | convolution fusion | flops 6194688 | bytes 1008176 | tf_op jit(solution)/shard_map/dot_general | solution.py:132
  (56 shorter events, 0.6 us)
Async XLA Ops:
  7.2 3.0 %copy-start = (bf16[1,64,3584]{2,1,0:T(8,128)(2,1)S(1)}, bf16[1,64,3584]{2,1,0:T(8,128)(2,1)}, u32[]{:S(2)}) copy-start(bf16[1,64,3584]{2,1,0:T(8,128)(2,1)} %param.10) | copy-start | bytes 1376260
  7.2 14.2 %copy-start.7 = (bf16[1,64,3584]{2,1,0:T(8,128)(2,1)S(1)}, bf16[1,64,3584]{2,1,0:T(8,128)(2,1)}, u32[]{:S(2)}) copy-start(bf16[1,64,3584]{2,1,0:T(8,128)(2,1)} %param.15) | copy-start | bytes 1376260
  7.2 82.2 %all-gather.2.cloned.1.call-start = ((), (), s32[]{:S(2)}) async-start(), calls=%async_computation.1 | async-start | bytes 5849088 | tf_op jit(solution)/shard_map/all_gather | solution.py:81
  8.4 13.2 %copy-start.6 = (bf16[1,64,3584]{2,1,0:T(8,128)(2,1)S(1)}, bf16[1,64,3584]{2,1,0:T(8,128)(2,1)}, u32[]{:S(2)}) copy-start(bf16[1,64,3584]{2,1,0:T(8,128)(2,1)} %param.14) | copy-start | bytes 1376260
  10.4 19.0 %collective-permute-start.3 = (bf16[4,6,1792]{2,1,0:T(8,128)(2,1)S(1)}, bf16[4,6,1792]{2,1,0:T(8,128)(2,1)S(1)}, u32[]{:S(2)}, u32[]{:S(2)}) collective-permute-start(bf16[4,6,1792]{2,1,0:T(8,128)(2,1)S(1)} %get-tuple-element.18), channel_id=1, source_target_pairs={{0,16},{1,17},{2,18},{3,19},{4,20},{5,21},{6,22},{7,23},{8,24},{9,... | collective-permute-start | bytes 258056 | tf_op jit(solution)/shard_map/ppermute | solution.py:14
  21.9 22.5 %copy-start.1 = (bf16[1,3584,64]{1,2,0:T(8,128)(2,1)S(1)}, bf16[1,3584,64]{1,2,0:T(8,128)(2,1)}, u32[]{:S(2)}) copy-start(bf16[1,3584,64]{1,2,0:T(8,128)(2,1)} %param.18) | copy-start | bytes 1376260
  21.9 22.5 %copy-start.5 = (bf16[1,3584,64]{1,2,0:T(8,128)(2,1)S(1)}, bf16[1,3584,64]{1,2,0:T(8,128)(2,1)}, u32[]{:S(2)}) copy-start(bf16[1,3584,64]{1,2,0:T(8,128)(2,1)} %param.19) | copy-start | bytes 1376260
  21.9 13.0 %collective-permute-start.2 = (bf16[4,6,1792]{2,1,0:T(8,128)(2,1)S(1)}, bf16[4,6,1792]{2,1,0:T(8,128)(2,1)S(1)}, u32[]{:S(2)}, u32[]{:S(2)}) collective-permute-start(bf16[4,6,1792]{2,1,0:T(8,128)(2,1)S(1)} %get-tuple-element.19), channel_id=1, source_target_pairs={{0,480},{32,448},{64,416},{96,384},{128,352},{160,320},{192,288},{... | collective-permute-start | bytes 258056 | tf_op jit(solution)/shard_map/ppermute | solution.py:14
  26.7 16.6 %collective-permute-start.4 = (bf16[4,6,1792]{2,1,0:T(8,128)(2,1)S(1)}, bf16[4,6,1792]{2,1,0:T(8,128)(2,1)S(1)}, u32[]{:S(2)}, u32[]{:S(2)}) collective-permute-start(bf16[4,6,1792]{2,1,0:T(8,128)(2,1)S(1)} %get-tuple-element.20), channel_id=1, source_target_pairs={{0,496},{1,497},{2,498},{3,499},{4,500},{5,501},{6,502},{7,503},{8... | collective-permute-start | bytes 258056 | tf_op jit(solution)/shard_map/ppermute | solution.py:14
  89.3 4.5 %copy-start.2 = (bf16[1,3584,64]{1,2,0:T(8,128)(2,1)S(1)}, bf16[1,3584,64]{1,2,0:T(8,128)(2,1)}, u32[]{:S(2)}) copy-start(bf16[1,3584,64]{1,2,0:T(8,128)(2,1)} %param.18) | copy-start | bytes 1376260
  93.7 1.2 copy-start.3
  96.1 5.4 %collective-permute-start.5 = (bf16[8,24,3584]{2,1,0:T(8,128)(2,1)}, bf16[8,24,3584]{2,1,0:T(8,128)(2,1)}, u32[]{:S(2)}, u32[]{:S(2)}) collective-permute-start(bf16[8,24,3584]{2,1,0:T(8,128)(2,1)} %dynamic-slice_bitcast_fusion), channel_id=1, source_target_pairs={{0,1},{1,0},{2,3},{3,2},{4,5},{5,4},{6,7},{7,6},{8,9},{9,8},{10,11... | collective-permute-start | bytes 4128776 | tf_op jit(solution)/shard_map/ppermute | solution.py:14
  110.5 7.0 %copy-start.8 = (s32[1,64,8]{1,2,0:T(8,128)S(1)}, s32[1,64,8]{1,2,0:T(8,128)}, u32[]{:S(2)}) copy-start(s32[1,64,8]{1,2,0:T(8,128)} %param.16) | copy-start | bytes 6148
  110.5 12.4 %copy-start.9 = (s32[1,64,8]{1,2,0:T(8,128)S(1)}, s32[1,64,8]{1,2,0:T(8,128)}, u32[]{:S(2)}) copy-start(s32[1,64,8]{1,2,0:T(8,128)} %param.12) | copy-start | bytes 6148
  110.5 23.1 %copy-start.4 = (f32[1536,256]{1,0:T(8,128)S(1)}, f32[1536,256]{1,0:T(8,128)}, u32[]{:S(2)}) copy-start(f32[1536,256]{1,0:T(8,128)} %copy-done.3) | copy-start | bytes 4718596
  110.5 45.6 %all-to-all-start = ((bf16[16,24,1792]{2,1,0:T(8,128)(2,1)}), bf16[16,24,1792]{2,1,0:T(8,128)(2,1)S(1)}, u32[]{:S(2)}, u32[]{:S(2)}) async-start(bf16[16,24,1792]{2,1,0:T(8,128)(2,1)} %copy.129), calls=%async_computation | async-start | bytes 2752512 | tf_op jit(solution)/shard_map/all_to_all | solution.py:119
  117.5 15.4 %collective-permute-start.8 = (s32[64,8]{0,1:T(8,128)S(1)}, s32[64,8]{0,1:T(8,128)S(1)}, u32[]{:S(2)}, u32[]{:S(2)}) collective-permute-start(s32[64,8]{0,1:T(8,128)S(1)} %bitcast.210), channel_id=1, source_target_pairs={{0,32},{32,64},{64,96},{96,128},{128,160},{160,192},{192,224},{224... | collective-permute-start | bytes 6152 | tf_op jit(solution)/shard_map/ppermute | solution.py:14
  122.9 10.3 %collective-permute-start.1 = (s32[64,8]{0,1:T(8,128)S(1)}, s32[64,8]{0,1:T(8,128)S(1)}, u32[]{:S(2)}, u32[]{:S(2)}) collective-permute-start(s32[64,8]{0,1:T(8,128)S(1)} %bitcast.212), channel_id=1, source_target_pairs={{32,0},{64,32},{96,64},{128,96},{160,128},{192,160},{224,192},{256... | collective-permute-start | bytes 6152 | tf_op jit(solution)/shard_map/ppermute | solution.py:14
  124.8 41.8 %collective-permute-start.7 = (bf16[64,3584]{1,0:T(8,128)(2,1)}, bf16[64,3584]{1,0:T(8,128)(2,1)}, u32[]{:S(2)}, u32[]{:S(2)}) collective-permute-start(bf16[64,3584]{1,0:T(8,128)(2,1)} %bitcast.197), channel_id=1, source_target_pairs={{0,32},{32,64},{64,96},{96,128},{128,160},{160,192},{192,224},{224... | collective-permute-start | bytes 1376264 | tf_op jit(solution)/shard_map/ppermute | solution.py:14
  130.9 38.0 %collective-permute-start = (bf16[64,3584]{1,0:T(8,128)(2,1)}, bf16[64,3584]{1,0:T(8,128)(2,1)}, u32[]{:S(2)}, u32[]{:S(2)}) collective-permute-start(bf16[64,3584]{1,0:T(8,128)(2,1)} %bitcast.198), channel_id=1, source_target_pairs={{32,0},{64,32},{96,64},{128,96},{160,128},{192,160},{224,192},{256... | collective-permute-start | bytes 1376264 | tf_op jit(solution)/shard_map/ppermute | solution.py:14
  156.8 9.9 %collective-permute-start.9 = (bf16[12,3584]{1,0:T(8,128)(2,1)S(1)}, bf16[12,3584]{1,0:T(8,128)(2,1)S(1)}, u32[]{:S(2)}, u32[]{:S(2)}) collective-permute-start(bf16[12,3584]{1,0:T(8,128)(2,1)S(1)} %bitcast.205), channel_id=1, source_target_pairs={{32,480},{64,448},{96,416},{128,384},{160,352},{192,320},{224,288}... | collective-permute-start | bytes 258056 | tf_op jit(solution)/shard_map/ppermute | solution.py:14
  163.8 8.8 %collective-permute-start.6 = (bf16[12,3584]{1,0:T(8,128)(2,1)S(1)}, bf16[12,3584]{1,0:T(8,128)(2,1)S(1)}, u32[]{:S(2)}, u32[]{:S(2)}) collective-permute-start(bf16[12,3584]{1,0:T(8,128)(2,1)S(1)} %bitcast.206), channel_id=1, source_target_pairs={{32,0},{64,32},{96,64},{128,96},{160,128},{192,160},{224,192},{256... | collective-permute-start | bytes 258056 | tf_op jit(solution)/shard_map/ppermute | solution.py:14
Sparse Core Ops, SparseCore 0:
  44.5 44.7 all-gather.1

commit v2 on v1

v2 whole, which is shorter than its diff:
```python
import functools

import jax
import jax.numpy as jnp
from jax import lax
from jax.experimental import pallas as pl
from jax.experimental.pallas import tpu as pltpu
from jax.sharding import PartitionSpec as P

EXPERTS = 2
CAP = 6
KINDS = 4
NEAR = 4
RING = 8
BLOCK = KINDS * CAP
ROWS = RING * BLOCK
KIND_ROWS = RING * CAP
VMEM = pl.BlockSpec(memory_space=pltpu.VMEM)
SMEM = pl.BlockSpec(memory_space=pltpu.SMEM)
PARAMS = pltpu.CompilerParams(vmem_limit_bytes=48 * 1024 * 1024)


def send(value, axis, route):
    size = lax.axis_size(axis)
    pairs = [(i, route(i)) for i in range(size)]
    return lax.ppermute(value, axis, [(a, b) for a, b in pairs if 0 <= b < size])


def iota(shape, dim):
    return lax.broadcasted_iota(jnp.int32, shape, dim)


def nn(a, b):
    return jnp.dot(a, b, preferred_element_type=jnp.float32)


def nt(a, b):
    return lax.dot_general(a, b, (((1,), (1,)), ((), ())), preferred_element_type=jnp.float32)


def tn(a, b):
    return lax.dot_general(a, b, (((0,), (0,)), ((), ())), preferred_element_type=jnp.float32)


def one_hot(mask):
    return jnp.where(mask, 1.0, 0.0).astype(jnp.bfloat16)


def slot_table(experts, expert_of, slot_of):
    tokens = experts.shape[1]
    named = [
        jnp.sum(jnp.where(experts == e, 1.0, 0.0), axis=0, keepdims=True) for e in range(EXPERTS)
    ]
    named = jnp.where(expert_of == 0, named[0], named[1])
    before = one_hot(iota((tokens, tokens), 0) < iota((tokens, tokens), 1))
    rank = nn(named.astype(jnp.bfloat16), before)
    return jnp.where(rank == slot_of.astype(jnp.float32), named, 0.0)


def prepare_kernel(copies, x_ref, c_ref, e_ref, g_ref, o_ref):
    half = x_ref.shape[1] // 2
    experts, gates = e_ref[...], g_ref[...]
    shape = (EXPERTS * BLOCK, experts.shape[1])
    row = iota(shape, 0)
    expert_of, kind, slot_of = row // BLOCK, (row // CAP) % KINDS, row % CAP
    table = slot_table(experts, expert_of, slot_of)
    gate = [
        jnp.sum(jnp.where(experts == e, gates, 0.0), axis=0, keepdims=True) for e in range(EXPERTS)
    ]
    gate = jnp.sum(table * jnp.where(expert_of == 0, gate[0], gate[1]), axis=1, keepdims=True)
    scale = jnp.where(kind[:, :1] % 2 == 1, gate, 1.0)
    total = None
    sources = (x_ref[:, :half], c_ref[:, :half], x_ref[:, half:], c_ref[:, half:])
    for k, source in enumerate(sources):
        part = nn(jnp.where(kind == k, table, 0.0).astype(jnp.bfloat16), source)
        total = part if total is None else total + part
    out = (total * scale).astype(jnp.bfloat16)
    if copies == 1:
        o_ref[...] = out
    else:
        for e in range(EXPERTS):
            one = (total[e * BLOCK : (e + 1) * BLOCK] * scale[e * BLOCK : (e + 1) * BLOCK]).astype(
                jnp.bfloat16
            )
            two = jnp.concatenate([one, one], axis=0)
            for i in range(copies // 2):
                start = (e * copies + 2 * i) * BLOCK
                o_ref[start : start + 2 * BLOCK, :] = two


def prepare(x, cot, experts, gates, copies):
    return pl.pallas_call(
        functools.partial(prepare_kernel, copies),
        out_shape=jax.ShapeDtypeStruct((EXPERTS * copies * BLOCK, x.shape[1] // 2), jnp.bfloat16),
        in_specs=[VMEM] * 4,
        out_specs=VMEM,
        compiler_params=PARAMS,
        name="prepare",
    )(x, cot, experts, gates)


def work(rows, weights, aligned_ref, da_ref, hid_ref):
    half = rows.shape[1]
    part = weights.shape[0] // (2 * NEAR)
    out, src = iota((ROWS, ROWS), 0), iota((ROWS, ROWS), 1)
    within = out % KIND_ROWS
    wanted = (within // CAP) * BLOCK + (out // KIND_ROWS) * CAP + out % CAP
    aligned = nn(one_hot(src == wanted), rows).astype(jnp.bfloat16)
    aligned_ref[...] = aligned
    x0, g0, x1, g1 = (aligned[k * KIND_ROWS : (k + 1) * KIND_ROWS] for k in range(KINDS))
    up = jnp.concatenate([weights[2 * k * part : (2 * k + 1) * part] for k in range(NEAR)], axis=0)
    down = jnp.concatenate(
        [weights[(2 * k + 1) * part : (2 * k + 2) * part] for k in range(NEAR)], axis=0
    )
    act = nt(x0, up[:, :half]) + nt(x1, up[:, half:])
    back_h = nt(g0, down[:, :half]) + nt(g1, down[:, half:])
    sig = jax.nn.sigmoid(act)
    hid_ref[...] = (act * sig).astype(jnp.bfloat16)
    d_act = (back_h * sig * (1.0 + act * (1.0 - sig))).astype(jnp.bfloat16)
    da_ref[...] = d_act
    return jnp.concatenate([nn(d_act, up[:, :half]), nn(d_act, up[:, half:])], axis=0).astype(
        jnp.bfloat16
    )


def first_kernel(m_ref, w_ref, aligned_ref, da_ref, hid_ref, d_ref):
    d_ref[...] = work(m_ref[...], w_ref[...], aligned_ref, da_ref, hid_ref)


def second_kernel(m_ref, w_ref, other_ref, aligned_ref, da_ref, hid_ref, d_ref):
    mine = work(m_ref[...], w_ref[...], aligned_ref, da_ref, hid_ref)
    both = jnp.concatenate([other_ref[...], mine], axis=0)
    out, src = iota((ROWS, ROWS), 0), iota((ROWS, ROWS), 1)
    half_of, stream = (out % BLOCK) // (2 * CAP), (out // CAP) % 2
    wanted = stream * 2 * KIND_ROWS + half_of * KIND_ROWS + (out // BLOCK) * CAP + out % CAP
    d_ref[...] = nn(one_hot(src == wanted), both).astype(jnp.bfloat16)


def experts_backward(rows, weights, other=None):
    half = rows.shape[1]
    hidden = weights.shape[0] // 2
    back_rows = 2 * KIND_ROWS if other is None else ROWS
    return pl.pallas_call(
        first_kernel if other is None else second_kernel,
        out_shape=(
            jax.ShapeDtypeStruct((ROWS, half), jnp.bfloat16),
            jax.ShapeDtypeStruct((KIND_ROWS, hidden), jnp.bfloat16),
            jax.ShapeDtypeStruct((KIND_ROWS, hidden), jnp.bfloat16),
            jax.ShapeDtypeStruct((back_rows, half), jnp.bfloat16),
        ),
        in_specs=[VMEM] * (2 if other is None else 3),
        out_specs=(VMEM,) * 4,
        compiler_params=PARAMS,
        name="experts",
    )(rows, weights, *(() if other is None else (other,)))


def gradient_kernel(at_ref, la_ref, ra_ref, ld_ref, rd_ref, lh_ref, rh_ref, o_ref):
    half = la_ref.shape[1]
    hidden = ld_ref.shape[1]
    part = hidden // NEAR
    src, out = iota((hidden, 2 * hidden), 0), iota((hidden, 2 * hidden), 1)
    place = (src // part) * 2 * part + src % part
    spread = jnp.concatenate(
        [
            nn(jnp.concatenate([ld_ref[...], rd_ref[...]], axis=0), one_hot(out == place)),
            nn(jnp.concatenate([lh_ref[...], rh_ref[...]], axis=0), one_hot(out == place + part)),
        ],
        axis=0,
    ).astype(jnp.bfloat16)
    mine = at_ref[0]
    step = half // 7 if half % 7 == 0 else half
    for h in range(2):
        for start in range(0, half, step):
            cols = slice(start, start + step)
            rows = jnp.concatenate(
                [
                    ref[(2 * h + k) * KIND_ROWS : (2 * h + k + 1) * KIND_ROWS, cols]
                    for k in range(2)
                    for ref in (la_ref, ra_ref)
                ],
                axis=0,
            )
            grad = tn(rows, spread).astype(jnp.bfloat16)
            for k in range(NEAR):
                apart = mine ^ k
                slot = (apart % 2) * 2 + apart // 2
                o_ref[slot, h * half + start : h * half + start + step, :] = grad[
                    :, 2 * part * k : 2 * part * (k + 1)
                ]


def gradient(place, left, right):
    half, hidden = left[0].shape[1], left[1].shape[1]
    return pl.pallas_call(
        gradient_kernel,
        out_shape=jax.ShapeDtypeStruct((NEAR, 2 * half, 2 * hidden // NEAR), jnp.bfloat16),
        in_specs=[SMEM] + [VMEM] * 6,
        out_specs=VMEM,
        compiler_params=PARAMS,
        name="gradient",
    )(place, left[0], right[0], left[1], right[1], left[2], right[2])


def collect_kernel(m_ref, l_ref, r_ref):
    shape = (2 * BLOCK, ROWS)
    out, src = iota(shape, 0), iota(shape, 1)
    stream, half_of, expert = out // BLOCK, (out % BLOCK) // (2 * CAP), (out // CAP) % EXPERTS
    wanted = half_of * 2 * CAP + stream * CAP + out % CAP
    near = RING // EXPERTS * BLOCK
    total = nn(one_hot((src // near == expert) & (src % BLOCK == wanted)), m_ref[...])
    l_ref[...] = total[:BLOCK].astype(jnp.bfloat16)
    r_ref[...] = total[BLOCK:].astype(jnp.bfloat16)


def collect(back):
    one = jax.ShapeDtypeStruct((BLOCK, back.shape[1]), jnp.bfloat16)
    return pl.pallas_call(
        collect_kernel,
        out_shape=(one, one),
        in_specs=[VMEM],
        out_specs=(VMEM, VMEM),
        compiler_params=PARAMS,
        name="collect",
    )(back)


def finish_kernel(c_ref, e_ref, m_ref, o_ref):
    half = c_ref.shape[1] // 2
    experts = e_ref[...]
    row = iota((BLOCK, experts.shape[1]), 0)
    table = slot_table(experts, (row // CAP) % EXPERTS, row % CAP)
    for h in range(2):
        cols = slice(h * half, (h + 1) * half)
        picked = jnp.where(row // (2 * CAP) == h, table, 0.0).astype(jnp.bfloat16)
        total = c_ref[:, cols].astype(jnp.float32) + tn(picked, m_ref[...])
        o_ref[:, cols] = total.astype(jnp.bfloat16)


def finish(cot, experts, slots):
    return pl.pallas_call(
        finish_kernel,
        out_shape=jax.ShapeDtypeStruct(cot.shape, jnp.bfloat16),
        in_specs=[VMEM] * 3,
        out_specs=VMEM,
        compiler_params=PARAMS,
        name="finish",
    )(cot, experts, slots)[None]


def on_device(
    left_x,
    left_cot,
    left_experts,
    left_gates,
    right_x,
    right_cot,
    right_experts,
    right_gates,
    up_weight,
    down_weight,
):
    n_sec = lax.axis_size("section")
    n_exp = lax.axis_size("expert")
    half = left_x.shape[2] // 2
    place = lax.axis_index("expert") % NEAR
    rings = [list(range(r, n_exp, NEAR)) for r in range(NEAR)]
    chips = [list(range(z, z + NEAR)) for z in range(0, n_exp, NEAR)]

    def along_z(value):
        return lax.all_to_all(
            value, "expert", split_axis=0, concat_axis=0, tiled=True, axis_index_groups=rings
        )

    packed = jnp.concatenate([up_weight[0].T, down_weight[0].T], axis=0)
    weights = lax.all_gather(packed, "expert", axis=0, tiled=True, axis_index_groups=chips)

    copies = RING // EXPERTS
    left = prepare(left_x[0], left_cot[0], left_experts[0].T, left_gates[0].T, copies)
    right = prepare(right_x[0], right_cot[0], right_experts[0].T, right_gates[0].T, 1)
    right = send(right, "section", lambda s: n_sec - 1 - s)
    right = jnp.repeat(right.reshape(EXPERTS, 1, BLOCK, half), copies, axis=1)
    left_rows = along_z(left)
    right_rows = along_z(right.reshape(ROWS, half))

    next_cot = send(left_cot[0], "section", lambda s: s - 1)
    last_cot = send(right_cot[0], "section", lambda s: s + 1)
    next_experts = send(left_experts[0].T, "section", lambda s: s - 1)
    last_experts = send(right_experts[0].T, "section", lambda s: s + 1)

    left_work = experts_backward(left_rows, weights)
    right_work = experts_backward(right_rows, weights, left_work[3])
    back = along_z(right_work[3])

    grads = gradient(place.astype(jnp.int32)[None], left_work, right_work)
    given = send(grads[2:], "expert", lambda j: j ^ 1)
    summed = (grads[:2].astype(jnp.float32) + given.astype(jnp.float32)).astype(jnp.bfloat16)
    given = send(summed[1], "expert", lambda j: j ^ 2)
    layer_grad = (summed[0].astype(jnp.float32) + given.astype(jnp.float32)).astype(jnp.bfloat16)

    left_back, right_back = collect(back)
    next_slots = send(left_back, "section", lambda s: s - 1)
    last_slots = send(right_back, "section", lambda s: n_sec - s)
    left_grad_in = finish(next_cot, next_experts, next_slots)
    right_grad_in = finish(last_cot, last_experts, last_slots)
    return left_grad_in, right_grad_in, layer_grad[None]


def solution(mesh):
    return jax.shard_map(
        on_device,
        mesh=mesh,
        in_specs=(
            P("section", "expert", None),
            P("section", "expert", None),
            P("section", "expert", None),
            P("section", "expert", None),
            P("section", "expert", None),
            P("section", "expert", None),
            P("section", "expert", None),
            P("section", "expert", None),
            P("section", None, "expert"),
            P("section", None, "expert"),
        ),
        out_specs=(
            P("section", "expert", None),
            P("section", "expert", None),
            P("section", None, "expert"),
        ),
        check_vma=False,
    )
```

time: 182 us -> 153 us (0.84)
  the two profiles are of different devices: /device:TPU:26 before, /device:TPU:40 now
where the time goes in v2:
time: 153 us; the launch traced here: 152 us
  waiting for transfers between devices  64.6 us (42%)
  starting transfers between devices  47.3 us (31%)
  between operations  14.3 us (9%)
  Pallas kernels  10.6 us (7%)
  local copies, waits for them, and re-layouts  8.4 us (5%)
  other arithmetic  7.08 us (5%)
    ppermute x9, waiting for transfers between devices, send(): lax.ppermute(value, axis, [(a, b) for a, b in pairs if 0 <= b < size])  34.2 us
    ppermute x9, starting transfers between devices, send(): lax.ppermute(value, axis, [(a, b) for a, b in pairs if 0 <= b < size])  29.8 us
    all_to_all x3, waiting for transfers between devices, along_z(): lax.all_to_all(value, 'expert', split_axis=0, concat_axis=0, tiled=True,...  20.2 us
    all_to_all x3, starting transfers between devices, along_z(): lax.all_to_all(value, 'expert', split_axis=0, concat_axis=0, tiled=True,...  17.4 us
    all_gather x1, waiting for transfers between devices, on_device(): lax.all_gather(packed, 'expert', axis=0, tiled=True, axis_index_groups=ch...  10.2 us
    unnamed x26, local copies, waits for them, and re-layouts  4.99 us
    pallas_call x2, Pallas kernels, experts_backward(): pl.pallas_call(first_kernel if other is None else second_kernel, out_shap...  4.77 us
  transfers between devices with their start and end apart: 13, of which 8 were waited for; matrix products, arithmetic and copies ran while one was open for 3% of the time, Pallas kernels for 4%

profile of v2, /device:TPU:40, one launch (start us, length us, event | category | flops | bytes accessed | tf_op | source)
XLA Modules:
  0.0 152.2 jit_solution(15897089835093105204)
XLA Ops:
  7.2 0.0 copy-start.6
  7.2 0.0 copy-start.10
  7.2 0.0 copy-start.3
  7.2 0.0 copy-start.7
  7.2 0.0 all-gather.2.cloned.1.call-start
  7.3 2.2 %pad_maximum_fusion = bf16[128,3584]{1,0:T(8,128)(2,1)} fusion(bf16[64,3584]{1,0:T(8,128)(2,1)} %bitcast.56, bf16[64,3584]{1,0:T(8,128)(2,1)} %bitcast.57), kind=kLoop, calls=%fused_computation.6 | loop fusion | flops 1835008 | bytes 1835008 | tf_op jit(solution)/shard_map/concatenate | solution.py:275
  9.5 0.0 copy-start.4
  9.5 0.0 copy-start.5
  9.5 0.0 copy-start.8
  9.5 0.0 copy-start.9
  9.5 0.0 all-gather.2.cloned.1.call-update
  9.5 0.0 copy-done.6
  9.5 0.0 copy-done.10
  9.5 0.0 copy-done.3
  9.5 0.0 copy-done.7
  9.5 1.3 prepare.3
  10.9 10.3 %all-to-all-start.1 = ((bf16[8,24,1792]{2,1,0:T(8,128)(2,1)}), bf16[8,24,1792]{2,1,0:T(8,128)(2,1)S(1)}, u32[]{:S(2)}, u32[]{:S(2)}) async-start(bf16[8,24,1792]{2,1,0:T(8,128)(2,1)} %bitcast.20), calls=%async_computation.1 | async-start | bytes 1376256 | tf_op jit(solution)/shard_map/all_to_all | solution.py:271
  21.2 0.0 copy-done.4
  21.2 0.0 copy-done.5
  21.2 0.0 copy-done.8
  21.2 0.0 copy-done.9
  21.2 0.5 prepare.2
  21.7 4.0 %collective-permute-start.2 = (bf16[48,1792]{1,0:T(8,128)(2,1)S(1)}, bf16[48,1792]{1,0:T(8,128)(2,1)S(1)}, u32[]{:S(2)}, u32[]{:S(2)}) collective-permute-start(bf16[48,1792]{1,0:T(8,128)(2,1)S(1)} %prepare.2), channel_id=1, source_target_pairs={{0,480},{32,448},{64,416},{96,384},{128,352},{160,320},{192,288},{... | collective-permute-start | bytes 516104 | tf_op jit(solution)/shard_map/ppermute | solution.py:26
  25.6 7.8 %collective-permute-done.2 = bf16[48,1792]{1,0:T(8,128)(2,1)S(1)} collective-permute-done((bf16[48,1792]{1,0:T(8,128)(2,1)S(1)}, bf16[48,1792]{1,0:T(8,128)(2,1)S(1)}, u32[]{:S(2)}, u32[]{:S(2)}) %collective-permute-start.2) | collective-permute-done | bytes 172064 | tf_op jit(solution)/shard_map/ppermute | solution.py:26
  33.4 8.7 %all-to-all-done.1 = bf16[8,24,1792]{2,1,0:T(8,128)(2,1)S(1)} async-done(((bf16[8,24,1792]{2,1,0:T(8,128)(2,1)}), bf16[8,24,1792]{2,1,0:T(8,128)(2,1)S(1)}, u32[]{:S(2)}, u32[]{:S(2)}) %all-to-all-start.1) | async-done | bytes 688160 | tf_op jit(solution)/shard_map/all_to_all | solution.py:271
  42.2 0.9 broadcast_in_dim.15
  43.1 3.5 %all-to-all-start = ((bf16[8,24,1792]{2,1,0:T(8,128)(2,1)}), bf16[8,24,1792]{2,1,0:T(8,128)(2,1)S(1)}, u32[]{:S(2)}, u32[]{:S(2)}) async-start(bf16[8,24,1792]{2,1,0:T(8,128)(2,1)} %bitcast.10), calls=%async_computation | async-start | bytes 1376256 | tf_op jit(solution)/shard_map/all_to_all | solution.py:271
  46.6 10.2 %all-gather.2.cloned.1.call-done.w_ref = bf16[512,3584]{1,0:T(8,128)(2,1)} async-done(((bf16[128,3584]{1,0:T(8,128)(2,1)}), bf16[512,3584]{1,0:T(8,128)(2,1)}) %all-gather.2.cloned.1.call-update) | async-done | bytes 3670032 | tf_op jit(solution)/shard_map/all_gather | solution.py:276
  56.9 2.0 %copy-done = bf16[512,3584]{1,0:T(8,128)(2,1)S(1)} copy-done((bf16[512,3584]{1,0:T(8,128)(2,1)S(1)}, bf16[512,3584]{1,0:T(8,128)(2,1)}, u32[]{:S(2)}) %copy-start) | copy-done | bytes 3670040
  58.9 1.8 %experts.2 = (bf16[192,1792]{1,0:T(8,128)(2,1)S(1)}, bf16[48,256]{1,0:T(8,128)(2,1)S(1)}, bf16[48,256]{1,0:T(8,128)(2,1)S(1)}, bf16[96,1792]{1,0:T(8,128)(2,1)S(1)}) custom-call(bf16[192,1792]{1,0:T(8,128)(2,1)S(1)} %bitcast.43, bf16[512,3584]{1,0:T(8,128)(2,1)S(1)} %copy-done), custom_call_target="tpu_custom_call" | custom-call | tf_op jit(solution)/shard_map/experts/pallas_call | solution.py:143
  60.7 7.3 %all-to-all-done = bf16[8,24,1792]{2,1,0:T(8,128)(2,1)S(1)} async-done(((bf16[8,24,1792]{2,1,0:T(8,128)(2,1)}), bf16[8,24,1792]{2,1,0:T(8,128)(2,1)S(1)}, u32[]{:S(2)}, u32[]{:S(2)}) %all-to-all-start) | async-done | bytes 688160 | tf_op jit(solution)/shard_map/all_to_all | solution.py:271
  68.0 2.0 %copy-done.1 = bf16[512,3584]{1,0:T(8,128)(2,1)S(1)} copy-done((bf16[512,3584]{1,0:T(8,128)(2,1)S(1)}, bf16[512,3584]{1,0:T(8,128)(2,1)}, u32[]{:S(2)}) %copy-start.1) | copy-done | bytes 3670040
  70.0 3.0 %experts.3 = (bf16[192,1792]{1,0:T(8,128)(2,1)S(1)}, bf16[48,256]{1,0:T(8,128)(2,1)S(1)}, bf16[48,256]{1,0:T(8,128)(2,1)S(1)}, bf16[192,1792]{1,0:T(8,128)(2,1)}) custom-call(bf16[192,1792]{1,0:T(8,128)(2,1)S(1)} %bitcast.41, bf16[512,3584]{1,0:T(8,128)(2,1)S(1)} %copy-done.1, bf16[96,1792]{1,0:T(8,128)(2,1)S(1)} %get-tuple-element.13.other_ref), custom_call_target="tpu_custom_call" | custom-call | tf_op jit(solution)/shard_map/experts/pallas_call | solution.py:143
  73.0 1.4 gradient.1
  74.4 0.0 copy-start.2
  74.4 1.5 slice.17
  75.9 0.9 copy-done.2
  76.8 1.9 %collective-permute-start.7 = (bf16[2,3584,128]{2,1,0:T(8,128)(2,1)}, bf16[2,3584,128]{2,1,0:T(8,128)(2,1)}, u32[]{:S(2)}, u32[]{:S(2)}) collective-permute-start(bf16[2,3584,128]{2,1,0:T(8,128)(2,1)} %slice.17), channel_id=1, source_target_pairs={{0,1},{1,0},{2,3},{3,2},{4,5},{5,4},{6,7},{7,6},{8,9},{9,8},{10,11... | collective-permute-start | bytes 5505032 | tf_op jit(solution)/shard_map/ppermute | solution.py:26
  78.7 3.6 %all-to-all-start.2 = ((bf16[8,24,1792]{2,1,0:T(8,128)(2,1)}), bf16[8,24,1792]{2,1,0:T(8,128)(2,1)S(1)}, u32[]{:S(2)}, u32[]{:S(2)}) async-start(bf16[8,24,1792]{2,1,0:T(8,128)(2,1)} %bitcast.22), calls=%async_computation.2 | async-start | bytes 1376256 | tf_op jit(solution)/shard_map/all_to_all | solution.py:271
  82.3 0.5 collective-permute-done.7
  82.8 2.5 %add_convert_fusion = bf16[2,3584,128]{2,1,0:T(8,128)(2,1)S(1)} fusion(bf16[2,3584,128]{2,1,0:T(8,128)(2,1)} %collective-permute-done.7, bf16[4,3584,128]{2,1,0:T(8,128)(2,1)} %copy-done.2), kind=kLoop, calls=%fused_computation | loop fusion | flops 3670016 | bytes 5505024 | tf_op jit(solution)/shard_map/convert_element_type | solution.py:297
  85.3 0.0 copy-start.11
  85.3 1.0 slice_bitcast_fusion
  86.4 4.9 %collective-permute-start.8 = (bf16[3584,128]{1,0:T(8,128)(2,1)}, bf16[3584,128]{1,0:T(8,128)(2,1)}, u32[]{:S(2)}, u32[]{:S(2)}) collective-permute-start(bf16[3584,128]{1,0:T(8,128)(2,1)} %slice_bitcast_fusion), channel_id=1, source_target_pairs={{0,2},{1,3},{2,0},{3,1},{4,6},{5,7},{6,4},{7,5},{8,10},{9,11},{10,... | collective-permute-start | bytes 2752520 | tf_op jit(solution)/shard_map/ppermute | solution.py:26
  91.3 2.5 %collective-permute-start.4 = (bf16[64,3584]{1,0:T(8,128)(2,1)S(1)}, bf16[64,3584]{1,0:T(8,128)(2,1)S(1)}, u32[]{:S(2)}, u32[]{:S(2)}) collective-permute-start(bf16[64,3584]{1,0:T(8,128)(2,1)S(1)} %bitcast.47), channel_id=1, source_target_pairs={{0,32},{32,64},{64,96},{96,128},{128,160},{160,192},{192,224},{224... | collective-permute-start | bytes 1376264 | tf_op jit(solution)/shard_map/ppermute | solution.py:26
  93.8 4.2 %collective-permute-start = (bf16[64,3584]{1,0:T(8,128)(2,1)S(1)}, bf16[64,3584]{1,0:T(8,128)(2,1)S(1)}, u32[]{:S(2)}, u32[]{:S(2)}) collective-permute-start(bf16[64,3584]{1,0:T(8,128)(2,1)S(1)} %bitcast.49), channel_id=1, source_target_pairs={{32,0},{64,32},{96,64},{128,96},{160,128},{192,160},{224,192},{256... | collective-permute-start | bytes 1376264 | tf_op jit(solution)/shard_map/ppermute | solution.py:26
  98.0 0.0 copy-done.11
  98.0 1.9 %collective-permute-start.5 = (s32[8,64]{1,0:T(8,128)S(1)}, s32[8,64]{1,0:T(8,128)S(1)}, u32[]{:S(2)}, u32[]{:S(2)}) collective-permute-start(s32[8,64]{1,0:T(8,128)S(1)} %bitcast.53), channel_id=1, source_target_pairs={{0,32},{32,64},{64,96},{96,128},{128,160},{160,192},{192,224},{224... | collective-permute-start | bytes 6152 | tf_op jit(solution)/shard_map/ppermute | solution.py:26
  100.0 4.1 %all-to-all-done.2 = bf16[8,24,1792]{2,1,0:T(8,128)(2,1)S(1)} async-done(((bf16[8,24,1792]{2,1,0:T(8,128)(2,1)}), bf16[8,24,1792]{2,1,0:T(8,128)(2,1)S(1)}, u32[]{:S(2)}, u32[]{:S(2)}) %all-to-all-start.2) | async-done | bytes 688160 | tf_op jit(solution)/shard_map/all_to_all | solution.py:271
  104.1 0.2 collect.1
  104.4 3.3 %collective-permute-start.6 = (bf16[24,1792]{1,0:T(8,128)(2,1)S(1)}, bf16[24,1792]{1,0:T(8,128)(2,1)S(1)}, u32[]{:S(2)}, u32[]{:S(2)}) collective-permute-start(bf16[24,1792]{1,0:T(8,128)(2,1)S(1)} %get-tuple-element.16), channel_id=1, source_target_pairs={{32,480},{64,448},{96,416},{128,384},{160,352},{192,320},{224,288}... | collective-permute-start | bytes 258056 | tf_op jit(solution)/shard_map/ppermute | solution.py:26
  107.6 23.5 %collective-permute-done.5.e_ref = s32[8,64]{1,0:T(8,128)S(1)} collective-permute-done((s32[8,64]{1,0:T(8,128)S(1)}, s32[8,64]{1,0:T(8,128)S(1)}, u32[]{:S(2)}, u32[]{:S(2)}) %collective-permute-start.5) | collective-permute-done | bytes 2080 | tf_op jit(solution)/shard_map/ppermute | solution.py:26
  131.1 5.2 %collective-permute-start.3 = (bf16[24,1792]{1,0:T(8,128)(2,1)S(1)}, bf16[24,1792]{1,0:T(8,128)(2,1)S(1)}, u32[]{:S(2)}, u32[]{:S(2)}) collective-permute-start(bf16[24,1792]{1,0:T(8,128)(2,1)S(1)} %get-tuple-element.15), channel_id=1, source_target_pairs={{32,0},{64,32},{96,64},{128,96},{160,128},{192,160},{224,192},{256... | collective-permute-start | bytes 258056 | tf_op jit(solution)/shard_map/ppermute | solution.py:26
  136.3 0.0 collective-permute-done.4.c_ref
  136.3 1.9 %collective-permute-start.1 = (s32[8,64]{1,0:T(8,128)S(1)}, s32[8,64]{1,0:T(8,128)S(1)}, u32[]{:S(2)}, u32[]{:S(2)}) collective-permute-start(s32[8,64]{1,0:T(8,128)S(1)} %bitcast.55), channel_id=1, source_target_pairs={{32,0},{64,32},{96,64},{128,96},{160,128},{192,160},{224,192},{256... | collective-permute-start | bytes 6152 | tf_op jit(solution)/shard_map/ppermute | solution.py:26
  138.2 0.0 collective-permute-done.6.m_ref
  138.3 1.2 finish.3
  139.5 2.3 %collective-permute-done.1.e_ref = s32[8,64]{1,0:T(8,128)S(1)} collective-permute-done((s32[8,64]{1,0:T(8,128)S(1)}, s32[8,64]{1,0:T(8,128)S(1)}, u32[]{:S(2)}, u32[]{:S(2)}) %collective-permute-start.1) | collective-permute-done | bytes 2080 | tf_op jit(solution)/shard_map/ppermute | solution.py:26
  141.8 0.0 collective-permute-done.c_ref
  141.8 0.0 collective-permute-done.3.m_ref
  141.8 1.2 finish.2
  143.0 0.0 collective-permute-done.8
  143.1 0.0 copy-done.12
  143.1 2.3 %fusion.1 = bf16[1,3584,128]{2,1,0:T(8,128)(2,1)} fusion(bf16[3584,128]{1,0:T(8,128)(2,1)} %collective-permute-done.8, bf16[2,3584,128]{2,1,0:T(8,128)(2,1)S(1)} %copy-done.12), kind=kLoop, calls=%fused_computation.3 | loop fusion | flops 1835008 | bytes 2752512 | tf_op jit(solution)/shard_map/broadcast_in_dim | solution.py:306
  (3 shorter events, 0.0 us)
Async XLA Ops:
  7.2 2.3 %copy-start.6 = (bf16[1,64,3584]{2,1,0:T(8,128)(2,1)S(1)}, bf16[1,64,3584]{2,1,0:T(8,128)(2,1)}, u32[]{:S(2)}) copy-start(bf16[1,64,3584]{2,1,0:T(8,128)(2,1)} %param.11) | copy-start | bytes 1376260
  7.2 2.3 %copy-start.10 = (s32[1,64,8]{1,2,0:T(8,128)S(1)}, s32[1,64,8]{1,2,0:T(8,128)}, u32[]{:S(2)}) copy-start(s32[1,64,8]{1,2,0:T(8,128)} %param.12) | copy-start | bytes 6148
  7.2 2.3 %copy-start.3 = (bf16[1,64,3584]{2,1,0:T(8,128)(2,1)S(1)}, bf16[1,64,3584]{2,1,0:T(8,128)(2,1)}, u32[]{:S(2)}) copy-start(bf16[1,64,3584]{2,1,0:T(8,128)(2,1)} %param.10) | copy-start | bytes 1376260
  7.2 2.3 %copy-start.7 = (f32[1,64,8]{1,2,0:T(8,128)S(1)}, f32[1,64,8]{1,2,0:T(8,128)}, u32[]{:S(2)}) copy-start(f32[1,64,8]{1,2,0:T(8,128)} %param.13) | copy-start | bytes 6148
  7.2 49.6 %all-gather.2.cloned.1.call-start = ((), (), s32[]{:S(2)}) async-start(), calls=%async_computation.3 | async-start | bytes 4587520 | tf_op jit(solution)/shard_map/all_gather | solution.py:276
  9.5 11.7 %copy-start.4 = (bf16[1,64,3584]{2,1,0:T(8,128)(2,1)S(1)}, bf16[1,64,3584]{2,1,0:T(8,128)(2,1)}, u32[]{:S(2)}) copy-start(bf16[1,64,3584]{2,1,0:T(8,128)(2,1)} %param.14) | copy-start | bytes 1376260
  9.5 11.7 %copy-start.5 = (bf16[1,64,3584]{2,1,0:T(8,128)(2,1)S(1)}, bf16[1,64,3584]{2,1,0:T(8,128)(2,1)}, u32[]{:S(2)}) copy-start(bf16[1,64,3584]{2,1,0:T(8,128)(2,1)} %param.15) | copy-start | bytes 1376260
  9.5 11.7 %copy-start.8 = (f32[1,64,8]{1,2,0:T(8,128)S(1)}, f32[1,64,8]{1,2,0:T(8,128)}, u32[]{:S(2)}) copy-start(f32[1,64,8]{1,2,0:T(8,128)} %param.17) | copy-start | bytes 6148
  9.5 11.7 %copy-start.9 = (s32[1,64,8]{1,2,0:T(8,128)S(1)}, s32[1,64,8]{1,2,0:T(8,128)}, u32[]{:S(2)}) copy-start(s32[1,64,8]{1,2,0:T(8,128)} %param.16) | copy-start | bytes 6148
  10.9 31.3 %all-to-all-start.1 = ((bf16[8,24,1792]{2,1,0:T(8,128)(2,1)}), bf16[8,24,1792]{2,1,0:T(8,128)(2,1)S(1)}, u32[]{:S(2)}, u32[]{:S(2)}) async-start(bf16[8,24,1792]{2,1,0:T(8,128)(2,1)} %bitcast.20), calls=%async_computation.1 | async-start | bytes 1376256 | tf_op jit(solution)/shard_map/all_to_all | solution.py:271
  21.7 11.8 %collective-permute-start.2 = (bf16[48,1792]{1,0:T(8,128)(2,1)S(1)}, bf16[48,1792]{1,0:T(8,128)(2,1)S(1)}, u32[]{:S(2)}, u32[]{:S(2)}) collective-permute-start(bf16[48,1792]{1,0:T(8,128)(2,1)S(1)} %prepare.2), channel_id=1, source_target_pairs={{0,480},{32,448},{64,416},{96,384},{128,352},{160,320},{192,288},{... | collective-permute-start | bytes 516104 | tf_op jit(solution)/shard_map/ppermute | solution.py:26
  43.1 24.9 %all-to-all-start = ((bf16[8,24,1792]{2,1,0:T(8,128)(2,1)}), bf16[8,24,1792]{2,1,0:T(8,128)(2,1)S(1)}, u32[]{:S(2)}, u32[]{:S(2)}) async-start(bf16[8,24,1792]{2,1,0:T(8,128)(2,1)} %bitcast.10), calls=%async_computation | async-start | bytes 1376256 | tf_op jit(solution)/shard_map/all_to_all | solution.py:271
  56.8 2.0 %copy-start = (bf16[512,3584]{1,0:T(8,128)(2,1)S(1)}, bf16[512,3584]{1,0:T(8,128)(2,1)}, u32[]{:S(2)}) copy-start(bf16[512,3584]{1,0:T(8,128)(2,1)} %all-gather.2.cloned.1.call-done.w_ref) | copy-start | bytes 11010052
  68.0 2.0 %copy-start.1 = (bf16[512,3584]{1,0:T(8,128)(2,1)S(1)}, bf16[512,3584]{1,0:T(8,128)(2,1)}, u32[]{:S(2)}) copy-start(bf16[512,3584]{1,0:T(8,128)(2,1)} %all-gather.2.cloned.1.call-done.w_ref) | copy-start | bytes 11010052
  74.4 2.4 %copy-start.2 = (bf16[4,3584,128]{2,1,0:T(8,128)(2,1)}, bf16[4,3584,128]{2,1,0:T(8,128)(2,1)S(1)}, u32[]{:S(2)}) copy-start(bf16[4,3584,128]{2,1,0:T(8,128)(2,1)S(1)} %gradient.1) | copy-start | bytes 11010052
  76.8 6.0 %collective-permute-start.7 = (bf16[2,3584,128]{2,1,0:T(8,128)(2,1)}, bf16[2,3584,128]{2,1,0:T(8,128)(2,1)}, u32[]{:S(2)}, u32[]{:S(2)}) collective-permute-start(bf16[2,3584,128]{2,1,0:T(8,128)(2,1)} %slice.17), channel_id=1, source_target_pairs={{0,1},{1,0},{2,3},{3,2},{4,5},{5,4},{6,7},{7,6},{8,9},{9,8},{10,11... | collective-permute-start | bytes 5505032 | tf_op jit(solution)/shard_map/ppermute | solution.py:26
  78.7 25.4 %all-to-all-start.2 = ((bf16[8,24,1792]{2,1,0:T(8,128)(2,1)}), bf16[8,24,1792]{2,1,0:T(8,128)(2,1)S(1)}, u32[]{:S(2)}, u32[]{:S(2)}) async-start(bf16[8,24,1792]{2,1,0:T(8,128)(2,1)} %bitcast.22), calls=%async_computation.2 | async-start | bytes 1376256 | tf_op jit(solution)/shard_map/all_to_all | solution.py:271
  85.3 12.7 %copy-start.11 = (bf16[2,3584,128]{2,1,0:T(8,128)(2,1)}, bf16[2,3584,128]{2,1,0:T(8,128)(2,1)S(1)}, u32[]{:S(2)}) copy-start(bf16[2,3584,128]{2,1,0:T(8,128)(2,1)S(1)} %add_convert_fusion) | copy-start | bytes 5505028
  86.4 56.7 %collective-permute-start.8 = (bf16[3584,128]{1,0:T(8,128)(2,1)}, bf16[3584,128]{1,0:T(8,128)(2,1)}, u32[]{:S(2)}, u32[]{:S(2)}) collective-permute-start(bf16[3584,128]{1,0:T(8,128)(2,1)} %slice_bitcast_fusion), channel_id=1, source_target_pairs={{0,2},{1,3},{2,0},{3,1},{4,6},{5,7},{6,4},{7,5},{8,10},{9,11},{10,... | collective-permute-start | bytes 2752520 | tf_op jit(solution)/shard_map/ppermute | solution.py:26
  91.3 45.0 %collective-permute-start.4 = (bf16[64,3584]{1,0:T(8,128)(2,1)S(1)}, bf16[64,3584]{1,0:T(8,128)(2,1)S(1)}, u32[]{:S(2)}, u32[]{:S(2)}) collective-permute-start(bf16[64,3584]{1,0:T(8,128)(2,1)S(1)} %bitcast.47), channel_id=1, source_target_pairs={{0,32},{32,64},{64,96},{96,128},{128,160},{160,192},{192,224},{224... | collective-permute-start | bytes 1376264 | tf_op jit(solution)/shard_map/ppermute | solution.py:26
  93.8 48.0 %collective-permute-start = (bf16[64,3584]{1,0:T(8,128)(2,1)S(1)}, bf16[64,3584]{1,0:T(8,128)(2,1)S(1)}, u32[]{:S(2)}, u32[]{:S(2)}) collective-permute-start(bf16[64,3584]{1,0:T(8,128)(2,1)S(1)} %bitcast.49), channel_id=1, source_target_pairs={{32,0},{64,32},{96,64},{128,96},{160,128},{192,160},{224,192},{256... | collective-permute-start | bytes 1376264 | tf_op jit(solution)/shard_map/ppermute | solution.py:26
  98.0 33.1 %collective-permute-start.5 = (s32[8,64]{1,0:T(8,128)S(1)}, s32[8,64]{1,0:T(8,128)S(1)}, u32[]{:S(2)}, u32[]{:S(2)}) collective-permute-start(s32[8,64]{1,0:T(8,128)S(1)} %bitcast.53), channel_id=1, source_target_pairs={{0,32},{32,64},{64,96},{96,128},{128,160},{160,192},{192,224},{224... | collective-permute-start | bytes 6152 | tf_op jit(solution)/shard_map/ppermute | solution.py:26
  104.1 38.9 %copy-start.12 = (bf16[2,3584,128]{2,1,0:T(8,128)(2,1)S(1)}, bf16[2,3584,128]{2,1,0:T(8,128)(2,1)}, u32[]{:S(2)}) copy-start(bf16[2,3584,128]{2,1,0:T(8,128)(2,1)} %copy-done.11) | copy-start | bytes 5505028
  104.4 33.9 %collective-permute-start.6 = (bf16[24,1792]{1,0:T(8,128)(2,1)S(1)}, bf16[24,1792]{1,0:T(8,128)(2,1)S(1)}, u32[]{:S(2)}, u32[]{:S(2)}) collective-permute-start(bf16[24,1792]{1,0:T(8,128)(2,1)S(1)} %get-tuple-element.16), channel_id=1, source_target_pairs={{32,480},{64,448},{96,416},{128,384},{160,352},{192,320},{224,288}... | collective-permute-start | bytes 258056 | tf_op jit(solution)/shard_map/ppermute | solution.py:26
  131.1 10.7 %collective-permute-start.3 = (bf16[24,1792]{1,0:T(8,128)(2,1)S(1)}, bf16[24,1792]{1,0:T(8,128)(2,1)S(1)}, u32[]{:S(2)}, u32[]{:S(2)}) collective-permute-start(bf16[24,1792]{1,0:T(8,128)(2,1)S(1)} %get-tuple-element.15), channel_id=1, source_target_pairs={{32,0},{64,32},{96,64},{128,96},{160,128},{192,160},{224,192},{256... | collective-permute-start | bytes 258056 | tf_op jit(solution)/shard_map/ppermute | solution.py:26
  136.3 5.5 %collective-permute-start.1 = (s32[8,64]{1,0:T(8,128)S(1)}, s32[8,64]{1,0:T(8,128)S(1)}, u32[]{:S(2)}, u32[]{:S(2)}) collective-permute-start(s32[8,64]{1,0:T(8,128)S(1)} %bitcast.55), channel_id=1, source_target_pairs={{32,0},{64,32},{96,64},{128,96},{160,128},{192,160},{224,192},{256... | collective-permute-start | bytes 6152 | tf_op jit(solution)/shard_map/ppermute | solution.py:26
Sparse Core Ops, SparseCore 0:
  10.7 46.0 all-gather.1

commit v3 on v2

v3 whole, which is shorter than its diff:
```python
import functools

import jax
import jax.numpy as jnp
from jax import lax
from jax.experimental import pallas as pl
from jax.experimental.pallas import tpu as pltpu
from jax.sharding import PartitionSpec as P

EXPERTS = 2
CAP = 6
KINDS = 4
NEAR = 4
RING = 8
BLOCK = KINDS * CAP
ROWS = RING * BLOCK
KIND_ROWS = RING * CAP
TOPK = 8
TAIL = 16
ANY = pl.BlockSpec(memory_space=pl.ANY)
VMEM = pl.BlockSpec(memory_space=pltpu.VMEM)
SMEM = pl.BlockSpec(memory_space=pltpu.SMEM)

SHORT = pl.CostEstimate(flops=1, bytes_accessed=1, transcendentals=0)


def room(mib):
    return pltpu.CompilerParams(vmem_limit_bytes=mib * 1024 * 1024)


def send(value, axis, route):
    size = lax.axis_size(axis)
    pairs = [(i, route(i)) for i in range(size)]
    return lax.ppermute(value, axis, [(a, b) for a, b in pairs if 0 <= b < size])


def iota(shape, dim):
    return lax.broadcasted_iota(jnp.int32, shape, dim)


def nn(a, b):
    return jnp.dot(a, b, preferred_element_type=jnp.float32)


def nt(a, b):
    return lax.dot_general(a, b, (((1,), (1,)), ((), ())), preferred_element_type=jnp.float32)


def tn(a, b):
    return lax.dot_general(a, b, (((0,), (0,)), ((), ())), preferred_element_type=jnp.float32)


def one_hot(mask):
    return jnp.where(mask, 1.0, 0.0).astype(jnp.bfloat16)


def slot_table(experts, expert_of, slot_of):
    tokens = experts.shape[1]
    named = [
        jnp.sum(jnp.where(experts == e, 1.0, 0.0), axis=0, keepdims=True) for e in range(EXPERTS)
    ]
    named = jnp.where(expert_of == 0, named[0], named[1])
    before = one_hot(iota((tokens, tokens), 0) < iota((tokens, tokens), 1))
    rank = nn(named.astype(jnp.bfloat16), before)
    return jnp.where(rank == slot_of.astype(jnp.float32), named, 0.0)


def spread_experts(experts, width):
    tokens = experts.shape[1]
    shape = (tokens, width)
    return nn(experts.astype(jnp.bfloat16), one_hot(iota(shape, 0) == iota(shape, 1)))


def prepare_kernel(copies, x_ref, c_ref, e_ref, g_ref, o_ref):
    half = x_ref.shape[1] // 2
    experts, gates = e_ref[...], g_ref[...]
    shape = (EXPERTS * BLOCK, experts.shape[1])
    row = iota(shape, 0)
    expert_of, kind, slot_of = row // BLOCK, (row // CAP) % KINDS, row % CAP
    table = slot_table(experts, expert_of, slot_of)
    gate = [
        jnp.sum(jnp.where(experts == e, gates, 0.0), axis=0, keepdims=True) for e in range(EXPERTS)
    ]
    gate = jnp.sum(table * jnp.where(expert_of == 0, gate[0], gate[1]), axis=1, keepdims=True)
    scale = jnp.where(kind[:, :1] % 2 == 1, gate, 1.0)
    total = None
    sources = (x_ref[:, :half], c_ref[:, :half], x_ref[:, half:], c_ref[:, half:])
    for k, source in enumerate(sources):
        part = nn(jnp.where(kind == k, table, 0.0).astype(jnp.bfloat16), source)
        total = part if total is None else total + part
    total = total * scale
    if copies == 1:
        tail = spread_experts(experts.astype(jnp.float32), half)
        tail = jnp.concatenate([tail, jnp.zeros_like(tail)], axis=0)
        o_ref[...] = jnp.concatenate([total, tail], axis=0).astype(jnp.bfloat16)
    else:
        for e in range(EXPERTS):
            one = total[e * BLOCK : (e + 1) * BLOCK].astype(jnp.bfloat16)
            two = jnp.concatenate([one, one], axis=0)
            for i in range(copies // 2):
                start = (e * copies + 2 * i) * BLOCK
                o_ref[start : start + 2 * BLOCK, :] = two


def prepare(x, cot, experts, gates, copies):
    rows = EXPERTS * copies * BLOCK + (TAIL if copies == 1 else 0)
    return pl.pallas_call(
        functools.partial(prepare_kernel, copies),
        out_shape=jax.ShapeDtypeStruct((rows, x.shape[1] // 2), jnp.bfloat16),
        in_specs=[VMEM] * 4,
        out_specs=VMEM,
        compiler_params=room(8) if copies == 1 else None,
        cost_estimate=SHORT,
        name="prepare",
    )(x, cot, experts, gates)


def align(rows):
    out, src = iota((ROWS, ROWS), 0), iota((ROWS, ROWS), 1)
    within = out % KIND_ROWS
    wanted = (within // CAP) * BLOCK + (out // KIND_ROWS) * CAP + out % CAP
    return nn(one_hot(src == wanted), rows).astype(jnp.bfloat16)


def experts_kernel(l_ref, r_ref, *refs):
    pieces, (la_ref, ra_ref, da_ref, hid_ref, o_ref, w_ref, sems) = refs[:NEAR], refs[NEAR:]
    half = l_ref.shape[1]
    hidden = w_ref.shape[0]
    part = hidden // (2 * NEAR)
    copies = [
        pltpu.make_async_copy(piece, w_ref.at[pl.ds(2 * part * k, 2 * part)], sems.at[k])
        for k, piece in enumerate(pieces)
    ]
    for copy in copies:
        copy.start()
    left, right = align(l_ref[...]), align(r_ref[...])
    la_ref[...] = left
    ra_ref[...] = right
    for copy in copies:
        copy.wait()
    both = None
    for h in range(2):
        rows = jnp.concatenate(
            [
                side[(2 * h + k) * KIND_ROWS : (2 * h + k + 1) * KIND_ROWS]
                for k in range(2)
                for side in (left, right)
            ],
            axis=0,
        )
        one = nt(rows, w_ref[:, h * half : (h + 1) * half])
        both = one if both is None else both + one
    act = both[: 2 * KIND_ROWS]
    back_h = pltpu.roll(both[2 * KIND_ROWS :], hidden - part, axis=1)
    mask = (iota(act.shape, 1) // part) % 2 == 0
    sig = jax.nn.sigmoid(act)
    hid = jnp.where(mask, act * sig, 0.0)
    hid_ref[...] = pltpu.roll(hid, part, axis=1).astype(jnp.bfloat16)
    d_act = jnp.where(mask, back_h * sig * (1.0 + act * (1.0 - sig)), 0.0).astype(jnp.bfloat16)
    da_ref[...] = d_act
    back = jnp.concatenate(
        [nn(d_act, w_ref[:, :half]), nn(d_act, w_ref[:, half:])], axis=0
    ).astype(jnp.bfloat16)
    out, src = iota((ROWS, ROWS), 0), iota((ROWS, ROWS), 1)
    half_of, stream = (out % BLOCK) // (2 * CAP), (out // CAP) % 2
    wanted = (half_of * 2 + stream) * KIND_ROWS + (out // BLOCK) * CAP + out % CAP
    o_ref[...] = nn(one_hot(src == wanted), back).astype(jnp.bfloat16)


def experts_backward(left, right, weights):
    hidden = NEAR * weights[0].shape[0]
    rows = jax.ShapeDtypeStruct(left.shape, jnp.bfloat16)
    units = jax.ShapeDtypeStruct((2 * KIND_ROWS, hidden), jnp.bfloat16)
    return pl.pallas_call(
        experts_kernel,
        out_shape=(rows, rows, units, units, rows),
        in_specs=[VMEM] * 2 + [ANY] * NEAR,
        out_specs=(VMEM,) * 5,
        scratch_shapes=[
            pltpu.VMEM((hidden, weights[0].shape[1]), jnp.bfloat16),
            pltpu.SemaphoreType.DMA((NEAR,)),
        ],
        compiler_params=room(24),
        cost_estimate=SHORT,
        name="experts",
    )(left, right, *weights)


def gradient_kernel(la_ref, ra_ref, da_ref, hid_ref, kept_ref, given_ref):
    half = la_ref.shape[1]
    width = da_ref.shape[1] // NEAR
    spread = jnp.concatenate([da_ref[...], hid_ref[...]], axis=0)
    step = half // 7 if half % 7 == 0 else half
    for h in range(2):
        for start in range(0, half, step):
            rows = jnp.concatenate(
                [
                    ref[(2 * h + k) * KIND_ROWS : (2 * h + k + 1) * KIND_ROWS, start : start + step]
                    for k in range(2)
                    for ref in (la_ref, ra_ref)
                ],
                axis=0,
            )
            grad = tn(rows, spread).astype(jnp.bfloat16)
            place = slice(h * half + start, h * half + start + step)
            for k in range(NEAR):
                ref = given_ref if k % 2 else kept_ref
                ref[k // 2, place, :] = grad[:, width * k : width * (k + 1)]


def gradient(left, right, d_act, hid):
    blocks = jax.ShapeDtypeStruct((2, 2 * left.shape[1], d_act.shape[1] // NEAR), jnp.bfloat16)
    return pl.pallas_call(
        gradient_kernel,
        out_shape=(blocks, blocks),
        in_specs=[VMEM] * 4,
        out_specs=(VMEM, VMEM),
        compiler_params=room(16),
        cost_estimate=SHORT,
        name="gradient",
    )(left, right, d_act, hid)


def add_kernel(block, *refs):
    depth = refs[-1].shape[0]
    step = depth // 4
    for i in range(4):
        rows = slice(i * step, (i + 1) * step)
        total = 0.0
        for ref in refs[:-1]:
            part = ref[block, rows, :] if len(ref.shape) == 3 else ref[rows, :]
            total = total + part.astype(jnp.float32)
        refs[-1][rows, :] = total.astype(jnp.bfloat16)


def add_blocks(block, *parts):
    return pl.pallas_call(
        functools.partial(add_kernel, block),
        out_shape=jax.ShapeDtypeStruct(parts[0].shape[1:], jnp.bfloat16),
        in_specs=[VMEM] * len(parts),
        out_specs=VMEM,
        compiler_params=room(12),
        cost_estimate=SHORT,
        name="add",
    )(*parts)


def pack_kernel(up_ref, down_ref, o_ref):
    part = up_ref.shape[0]
    o_ref[:part, :] = up_ref[...]
    o_ref[part:, :] = down_ref[...]


def pack(up, down):
    return pl.pallas_call(
        pack_kernel,
        out_shape=jax.ShapeDtypeStruct((2 * up.shape[0], up.shape[1]), jnp.bfloat16),
        in_specs=[VMEM] * 2,
        out_specs=VMEM,
        compiler_params=room(8),
        cost_estimate=SHORT,
        name="pack",
    )(up, down)


def collect_kernel(m_ref, e_ref, t_ref, l_ref, r_ref):
    shape = (2 * BLOCK, ROWS)
    out, src = iota(shape, 0), iota(shape, 1)
    stream, half_of, expert = out // BLOCK, (out % BLOCK) // (2 * CAP), (out // CAP) % EXPERTS
    wanted = half_of * 2 * CAP + stream * CAP + out % CAP
    near = RING // EXPERTS * BLOCK
    total = nn(one_hot((src // near == expert) & (src % BLOCK == wanted)), m_ref[...])
    left = spread_experts(e_ref[...].astype(jnp.float32), m_ref.shape[1])
    right = t_ref[...].astype(jnp.float32)[EXPERTS * BLOCK : EXPERTS * BLOCK + TOPK]
    l_ref[...] = jnp.concatenate([total[:BLOCK], left], axis=0).astype(jnp.bfloat16)
    r_ref[...] = jnp.concatenate([total[BLOCK:], right], axis=0).astype(jnp.bfloat16)


def collect(back, left_experts, right_message):
    one = jax.ShapeDtypeStruct((BLOCK + TOPK, back.shape[1]), jnp.bfloat16)
    return pl.pallas_call(
        collect_kernel,
        out_shape=(one, one),
        in_specs=[VMEM] * 3,
        out_specs=(VMEM, VMEM),
        compiler_params=room(8),
        cost_estimate=SHORT,
        name="collect",
    )(back, left_experts, right_message)


def finish_kernel(l_ref, r_ref, lm_ref, rm_ref, lo_ref, ro_ref, c_ref, o_ref, in_sems, out_sems):
    tokens, width = l_ref.shape
    half = width // 2
    pieces = [(side, slice(h * half, (h + 1) * half)) for side in range(2) for h in range(2)]
    arrive = [
        pltpu.make_async_copy((l_ref, r_ref)[side].at[:, cols], c_ref.at[i], in_sems.at[i])
        for i, (side, cols) in enumerate(pieces)
    ]
    leave = [
        pltpu.make_async_copy(o_ref.at[i], (lo_ref, ro_ref)[side].at[:, cols], out_sems.at[i])
        for i, (side, cols) in enumerate(pieces)
    ]
    for copy in arrive:
        copy.start()
    row = iota((BLOCK + TOPK, tokens), 0)
    for side, m_ref in enumerate((lm_ref, rm_ref)):
        experts = m_ref[:, :128].astype(jnp.float32)[BLOCK:, :tokens]
        table = slot_table(experts, (row // CAP) % EXPERTS, row % CAP)
        for h in range(2):
            picked = jnp.where(row // (2 * CAP) == h, table, 0.0).astype(jnp.bfloat16)
            added = tn(picked, m_ref[...])
            i = 2 * side + h
            arrive[i].wait()
            o_ref[i] = (c_ref[i].astype(jnp.float32) + added).astype(jnp.bfloat16)
            leave[i].start()
    for copy in leave:
        copy.wait()


def finish(left_cot, right_cot, left_slots, right_slots):
    tokens, width = left_cot.shape
    shape = jax.ShapeDtypeStruct(left_cot.shape, jnp.bfloat16)
    pieces = pltpu.VMEM((4, tokens, width // 2), jnp.bfloat16)
    return pl.pallas_call(
        finish_kernel,
        out_shape=(shape, shape),
        in_specs=[ANY] * 2 + [VMEM] * 2,
        out_specs=(ANY, ANY),
        scratch_shapes=[pieces, pieces] + [pltpu.SemaphoreType.DMA((4,))] * 2,
        compiler_params=room(12),
        cost_estimate=SHORT,
        name="finish",
    )(left_cot, right_cot, left_slots, right_slots)


def on_device(
    left_x,
    left_cot,
    left_experts,
    left_gates,
    right_x,
    right_cot,
    right_experts,
    right_gates,
    up_weight,
    down_weight,
):
    n_sec = lax.axis_size("section")
    n_exp = lax.axis_size("expert")
    half = left_x.shape[2] // 2
    rings = [list(range(r, n_exp, NEAR)) for r in range(NEAR)]

    def along_z(value):
        return lax.all_to_all(
            value, "expert", split_axis=0, concat_axis=0, tiled=True, axis_index_groups=rings
        )

    copies = RING // EXPERTS
    left = prepare(left_x[0], left_cot[0], left_experts[0].T, left_gates[0].T, copies)
    left_rows = along_z(left)
    message = prepare(right_x[0], right_cot[0], right_experts[0].T, right_gates[0].T, 1)
    message = send(message, "section", lambda s: n_sec - 1 - s)
    right = message[: EXPERTS * BLOCK].reshape(EXPERTS, 1, BLOCK, half)
    right = jnp.repeat(right, copies, axis=1).reshape(ROWS, half)

    own = pack(up_weight[0].T, down_weight[0].T)
    across = send(own, "expert", lambda j: j ^ 2)
    beside = send(own, "expert", lambda j: j ^ 1)

    next_cot = send(left_cot[0], "section", lambda s: s - 1)
    last_cot = send(right_cot[0], "section", lambda s: s + 1)
    right, left_rows = lax.optimization_barrier((right, left_rows))
    right_rows = along_z(right)
    across, next_cot = lax.optimization_barrier((across, next_cot))
    corner = send(across, "expert", lambda j: j ^ 1)

    weights = (own, beside, across, corner)
    left_rows, right_rows, d_act, hid, back = experts_backward(left_rows, right_rows, weights)
    back = along_z(back)

    kept, given = gradient(left_rows, right_rows, d_act, hid)
    given, last_cot = lax.optimization_barrier((given, last_cot))
    given = send(given, "expert", lambda j: j ^ 1)
    given_far = send(add_blocks(1, kept, given), "expert", lambda j: j ^ 2)
    layer_grad = add_blocks(0, kept, given, given_far)

    left_back, right_back = collect(back, left_experts[0].T, message)
    next_slots = send(left_back, "section", lambda s: s - 1)
    last_slots = send(right_back, "section", lambda s: n_sec - s)
    next_slots, layer_grad = lax.optimization_barrier((next_slots, layer_grad))
    left_grad_in, right_grad_in = finish(next_cot, last_cot, next_slots, last_slots)
    return left_grad_in[None], right_grad_in[None], layer_grad[None]


def solution(mesh):
    return jax.shard_map(
        on_device,
        mesh=mesh,
        in_specs=(
            P("section", "expert", None),
            P("section", "expert", None),
            P("section", "expert", None),
            P("section", "expert", None),
            P("section", "expert", None),
            P("section", "expert", None),
            P("section", "expert", None),
            P("section", "expert", None),
            P("section", None, "expert"),
            P("section", None, "expert"),
        ),
        out_specs=(
            P("section", "expert", None),
            P("section", "expert", None),
            P("section", None, "expert"),
        ),
        check_vma=False,
    )
```

time: 153 us -> 121 us (0.79)
  the two profiles are of different devices: /device:TPU:40 before, /device:TPU:39 now
where the time goes in v3:
time: 121 us; the launch traced here: 120 us
  starting transfers between devices  56.7 us (47%)
  waiting for transfers between devices  39 us (32%)
  Pallas kernels  17.7 us (15%)
  local copies, waits for them, and re-layouts  6.1 us (5%)
    ppermute x10, starting transfers between devices, send(): lax.ppermute(value, axis, [(a, b) for a, b in pairs if 0 <= b < size])  35.9 us
    ppermute x10, waiting for transfers between devices, send(): lax.ppermute(value, axis, [(a, b) for a, b in pairs if 0 <= b < size])  21.7 us
    all_to_all x3, starting transfers between devices, along_z(): lax.all_to_all(value, 'expert', split_axis=0, concat_axis=0, tiled=True,...  20.9 us
    all_to_all x3, waiting for transfers between devices, along_z(): lax.all_to_all(value, 'expert', split_axis=0, concat_axis=0, tiled=True,...  17.3 us
    pallas_call x2, Pallas kernels, add_blocks(): pl.pallas_call(functools.partial(add_kernel, block), out_shape=jax.ShapeD...  5.39 us
    unnamed x28, local copies, waits for them, and re-layouts  5.19 us
    pallas_call x1, Pallas kernels, experts_backward(): pl.pallas_call(experts_kernel, out_shape=(rows, rows, units, units, rows)...  3.96 us
    pallas_call x2, Pallas kernels, prepare(): pl.pallas_call(functools.partial(prepare_kernel, copies), out_shape=jax.S...  3.02 us
  transfers between devices with their start and end apart: 13, of which 6 were waited for; matrix products, arithmetic and copies ran while one was open for 1% of the time, Pallas kernels for 10%

profile of v3, /device:TPU:39, one launch (start us, length us, event | category | flops | bytes accessed | tf_op | source)
XLA Modules:
  0.0 120.4 jit_solution(6785413839230372175)
XLA Ops:
  0.6 0.0 copy-start.7
  0.6 0.0 copy-start.8
  0.7 2.5 %prepare.3 = bf16[192,1792]{1,0:T(8,128)(2,1)} custom-call(bf16[64,3584]{1,0:T(8,128)(2,1)} %bitcast.50, bf16[64,3584]{1,0:T(8,128)(2,1)} %bitcast.4.c_ref, s32[8,64]{1,0:T(8,128)} %bitcast.42, f32[8,64]{1,0:T(8,128)} %bitcast.51), custom_call_target="tpu_custom_call" | custom-call | flops 1 | bytes 1 | tf_op jit(solution)/shard_map/prepare/pallas_call | solution.py:107
  3.2 0.0 copy-start.9
  3.2 0.0 copy-start.10
  3.2 0.0 copy-start.12
  3.2 0.0 copy-start.13
  3.2 10.2 %all-to-all-start = ((bf16[8,24,1792]{2,1,0:T(8,128)(2,1)}), bf16[8,24,1792]{2,1,0:T(8,128)(2,1)S(1)}, u32[]{:S(2)}, u32[]{:S(2)}) async-start(bf16[8,24,1792]{2,1,0:T(8,128)(2,1)} %bitcast.47), calls=%async_computation | async-start | bytes 1376256 | tf_op jit(solution)/shard_map/all_to_all | solution.py:355
  13.4 0.0 copy-done.7
  13.4 0.0 copy-done.8
  13.4 0.1 pack.1.refs_0_
  13.5 3.0 %collective-permute-start = (bf16[128,3584]{1,0:T(8,128)(2,1)S(1)}, bf16[128,3584]{1,0:T(8,128)(2,1)S(1)}, u32[]{:S(2)}, u32[]{:S(2)}) collective-permute-start(bf16[128,3584]{1,0:T(8,128)(2,1)S(1)} %pack.1.refs_0_), channel_id=1, source_target_pairs={{0,2},{1,3},{2,0},{3,1},{4,6},{5,7},{6,4},{7,5},{8,10},{9,11},{10,... | collective-permute-start | bytes 2752520 | tf_op jit(solution)/shard_map/ppermute | solution.py:34
  16.5 0.0 copy-done.9
  16.5 0.0 copy-done.10
  16.5 0.0 copy-done.12
  16.6 0.0 copy-done.13
  16.6 0.5 prepare.2
  17.0 1.9 %collective-permute-start.2 = (bf16[64,1792]{1,0:T(8,128)(2,1)S(1)}, bf16[64,1792]{1,0:T(8,128)(2,1)S(1)}, u32[]{:S(2)}, u32[]{:S(2)}) collective-permute-start(bf16[64,1792]{1,0:T(8,128)(2,1)S(1)} %prepare.2), channel_id=1, source_target_pairs={{0,480},{32,448},{64,416},{96,384},{128,352},{160,320},{192,288},{... | collective-permute-start | bytes 688136 | tf_op jit(solution)/shard_map/ppermute | solution.py:34
  19.0 3.2 %collective-permute-start.1 = (bf16[64,3584]{1,0:T(8,128)(2,1)}, bf16[64,3584]{1,0:T(8,128)(2,1)}, u32[]{:S(2)}, u32[]{:S(2)}) collective-permute-start(bf16[64,3584]{1,0:T(8,128)(2,1)} %bitcast.4.c_ref), channel_id=1, source_target_pairs={{32,0},{64,32},{96,64},{128,96},{160,128},{192,160},{224,192},{256... | collective-permute-start | bytes 1376264 | tf_op jit(solution)/shard_map/ppermute | solution.py:34
  22.2 11.2 %collective-permute-done.2.t_ref = bf16[64,1792]{1,0:T(8,128)(2,1)S(1)} collective-permute-done((bf16[64,1792]{1,0:T(8,128)(2,1)S(1)}, bf16[64,1792]{1,0:T(8,128)(2,1)S(1)}, u32[]{:S(2)}, u32[]{:S(2)}) %collective-permute-start.2) | collective-permute-done | bytes 229408 | tf_op jit(solution)/shard_map/ppermute | solution.py:34
  33.5 0.0 copy-start.4
  33.5 1.4 %all-to-all-done = bf16[8,24,1792]{2,1,0:T(8,128)(2,1)S(1)} async-done(((bf16[8,24,1792]{2,1,0:T(8,128)(2,1)}), bf16[8,24,1792]{2,1,0:T(8,128)(2,1)S(1)}, u32[]{:S(2)}, u32[]{:S(2)}) %all-to-all-start) | async-done | bytes 688160 | tf_op jit(solution)/shard_map/all_to_all | solution.py:355
  34.9 0.9 broadcast_in_dim.12
  35.8 0.0 copy-done.4
  35.8 5.2 %all-to-all-start.1 = ((bf16[8,24,1792]{2,1,0:T(8,128)(2,1)}), bf16[8,24,1792]{2,1,0:T(8,128)(2,1)S(1)}, u32[]{:S(2)}, u32[]{:S(2)}) async-start(bf16[8,24,1792]{2,1,0:T(8,128)(2,1)} %bitcast.46), calls=%async_computation.1 | async-start | bytes 1376256 | tf_op jit(solution)/shard_map/all_to_all | solution.py:355
  41.0 4.8 %collective-permute-start.3 = (bf16[128,3584]{1,0:T(8,128)(2,1)S(1)}, bf16[128,3584]{1,0:T(8,128)(2,1)S(1)}, u32[]{:S(2)}, u32[]{:S(2)}) collective-permute-start(bf16[128,3584]{1,0:T(8,128)(2,1)S(1)} %pack.1.refs_0_), channel_id=1, source_target_pairs={{0,1},{1,0},{2,3},{3,2},{4,5},{5,4},{6,7},{7,6},{8,9},{9,8},{10,11... | collective-permute-start | bytes 2752520 | tf_op jit(solution)/shard_map/ppermute | solution.py:34
  45.9 4.2 %collective-permute-done.1.l_ref = bf16[64,3584]{1,0:T(8,128)(2,1)} collective-permute-done((bf16[64,3584]{1,0:T(8,128)(2,1)}, bf16[64,3584]{1,0:T(8,128)(2,1)}, u32[]{:S(2)}, u32[]{:S(2)}) %collective-permute-start.1) | collective-permute-done | bytes 458784 | tf_op jit(solution)/shard_map/ppermute | solution.py:34
  50.1 0.0 collective-permute-done.refs_2_
  50.1 3.8 %collective-permute-start.4 = (bf16[128,3584]{1,0:T(8,128)(2,1)S(1)}, bf16[128,3584]{1,0:T(8,128)(2,1)S(1)}, u32[]{:S(2)}, u32[]{:S(2)}) collective-permute-start(bf16[128,3584]{1,0:T(8,128)(2,1)S(1)} %collective-permute-done.refs_2_), channel_id=1, source_target_pairs={{0,1},{1,0},{2,3},{3,2},{4,5},{5,4},{6,7},{7,6},{8,9},{9,8},{10,11... | collective-permute-start | bytes 2752520 | tf_op jit(solution)/shard_map/ppermute | solution.py:34
  53.8 5.0 %collective-permute-start.5 = (bf16[64,3584]{1,0:T(8,128)(2,1)}, bf16[64,3584]{1,0:T(8,128)(2,1)}, u32[]{:S(2)}, u32[]{:S(2)}) collective-permute-start(bf16[64,3584]{1,0:T(8,128)(2,1)} %bitcast.40), channel_id=1, source_target_pairs={{0,32},{32,64},{64,96},{96,128},{128,160},{160,192},{192,224},{224... | collective-permute-start | bytes 1376264 | tf_op jit(solution)/shard_map/ppermute | solution.py:34
  58.9 0.0 collective-permute-done.3.refs_1_
  58.9 0.0 copy-start
  58.9 0.9 copy-done
  59.8 0.0 collective-permute-done.4.refs_3_
  59.8 0.0 copy-start.2
  59.8 0.9 copy-done.2
  60.7 0.0 all-to-all-done.1
  60.8 0.0 copy-start.1
  60.8 1.2 copy-done.1
  61.9 0.0 copy-start.3
  61.9 1.2 copy-done.3
  63.1 4.0 %experts.1 = (bf16[192,1792]{1,0:T(8,128)(2,1)S(1)}, bf16[192,1792]{1,0:T(8,128)(2,1)S(1)}, bf16[96,512]{1,0:T(8,128)(2,1)S(1)}, bf16[96,512]{1,0:T(8,128)(2,1)S(1)}, bf16[192,1792]{1,0:T(8,128)(2,1)S(1)}) custom-call(bf16[192,1792]{1,0:T(8,128)(2,1)S(1)} %bitcast.33, bf16[192,1792]{1,0:T(8,128)(2,1)S(1)} %bitcast.34, bf16[128,3584]{1,0:T(8,128)(2,1)S(1)} %pack.1.refs_0_, ...), custom_call_target="tpu_custom_call" | custom-call | flops 1 | bytes 1 | tf_op jit(solution)/shard_map/experts/pallas_call | solution.py:174
  67.1 0.0 copy-start.6
  67.1 2.4 %gradient.1 = (bf16[2,3584,128]{2,1,0:T(8,128)(2,1)S(1)}, bf16[2,3584,128]{2,1,0:T(8,128)(2,1)}) custom-call(bf16[192,1792]{1,0:T(8,128)(2,1)S(1)} %get-tuple-element.26.la_ref, bf16[192,1792]{1,0:T(8,128)(2,1)S(1)} %get-tuple-element.27.ra_ref, bf16[96,512]{1,0:T(8,128)(2,1)S(1)} %get-tuple-element.28.da_ref, bf16[96,512]{1,0:T(8,128)(2,1)S(1)} %get-tuple-element.29.hid_ref), custom_call_target="tpu_custom_call" | custom-call | flops 1 | bytes 1 | tf_op jit(solution)/shard_map/gradient/pallas_call | solution.py:213
  69.5 0.5 collective-permute-done.5.r_ref
  69.9 3.7 %collective-permute-start.7 = (bf16[2,3584,128]{2,1,0:T(8,128)(2,1)}, bf16[2,3584,128]{2,1,0:T(8,128)(2,1)}, u32[]{:S(2)}, u32[]{:S(2)}) collective-permute-start(bf16[2,3584,128]{2,1,0:T(8,128)(2,1)} %get-tuple-element.35), channel_id=1, source_target_pairs={{0,1},{1,0},{2,3},{3,2},{4,5},{5,4},{6,7},{7,6},{8,9},{9,8},{10,11... | collective-permute-start | bytes 5505032 | tf_op jit(solution)/shard_map/ppermute | solution.py:34
  73.7 0.0 copy-done.6
  73.7 5.4 %all-to-all-start.2 = ((bf16[8,24,1792]{2,1,0:T(8,128)(2,1)}), bf16[8,24,1792]{2,1,0:T(8,128)(2,1)S(1)}, u32[]{:S(2)}, u32[]{:S(2)}) async-start(bf16[8,24,1792]{2,1,0:T(8,128)(2,1)} %bitcast.36), calls=%async_computation.2 | async-start | bytes 1376256 | tf_op jit(solution)/shard_map/all_to_all | solution.py:355
  79.1 0.0 collective-permute-done.7.refs_1_
  79.1 0.0 copy-start.11
  79.1 2.6 %add.2 = bf16[3584,128]{1,0:T(8,128)(2,1)} custom-call(bf16[2,3584,128]{2,1,0:T(8,128)(2,1)S(1)} %get-tuple-element.34.refs_0_, bf16[2,3584,128]{2,1,0:T(8,128)(2,1)} %collective-permute-done.7.refs_1_), custom_call_target="tpu_custom_call" | custom-call | flops 1 | bytes 1 | tf_op jit(solution)/shard_map/add/pallas_call | solution.py:237
  81.8 2.9 %collective-permute-start.8 = (bf16[3584,128]{1,0:T(8,128)(2,1)}, bf16[3584,128]{1,0:T(8,128)(2,1)S(1)}, u32[]{:S(2)}, u32[]{:S(2)}) collective-permute-start(bf16[3584,128]{1,0:T(8,128)(2,1)} %add.2), channel_id=1, source_target_pairs={{0,2},{1,3},{2,0},{3,1},{4,6},{5,7},{6,4},{7,5},{8,10},{9,11},{10,... | collective-permute-start | bytes 2752520 | tf_op jit(solution)/shard_map/ppermute | solution.py:34
  84.7 15.9 %all-to-all-done.2 = bf16[8,24,1792]{2,1,0:T(8,128)(2,1)S(1)} async-done(((bf16[8,24,1792]{2,1,0:T(8,128)(2,1)}), bf16[8,24,1792]{2,1,0:T(8,128)(2,1)S(1)}, u32[]{:S(2)}, u32[]{:S(2)}) %all-to-all-start.2) | async-done | bytes 688160 | tf_op jit(solution)/shard_map/all_to_all | solution.py:355
  100.6 0.0 copy-done.11
  100.6 0.0 copy-start.5
  100.6 0.9 copy-done.5
  101.5 0.3 collect.1
  101.8 5.5 %collective-permute-start.6 = (bf16[32,1792]{1,0:T(8,128)(2,1)S(1)}, bf16[32,1792]{1,0:T(8,128)(2,1)S(1)}, u32[]{:S(2)}, u32[]{:S(2)}) collective-permute-start(bf16[32,1792]{1,0:T(8,128)(2,1)S(1)} %get-tuple-element.33), channel_id=1, source_target_pairs={{32,0},{64,32},{96,64},{128,96},{160,128},{192,160},{224,192},{256... | collective-permute-start | bytes 344072 | tf_op jit(solution)/shard_map/ppermute | solution.py:34
  107.3 1.9 %collective-permute-start.9 = (bf16[32,1792]{1,0:T(8,128)(2,1)S(1)}, bf16[32,1792]{1,0:T(8,128)(2,1)S(1)}, u32[]{:S(2)}, u32[]{:S(2)}) collective-permute-start(bf16[32,1792]{1,0:T(8,128)(2,1)S(1)} %get-tuple-element.37), channel_id=1, source_target_pairs={{32,480},{64,448},{96,416},{128,384},{160,352},{192,320},{224,288}... | collective-permute-start | bytes 344072 | tf_op jit(solution)/shard_map/ppermute | solution.py:34
  109.2 0.0 collective-permute-done.8.refs_2_
  109.2 2.8 %add.3 = bf16[3584,128]{1,0:T(8,128)(2,1)} custom-call(bf16[2,3584,128]{2,1,0:T(8,128)(2,1)S(1)} %get-tuple-element.34.refs_0_, bf16[2,3584,128]{2,1,0:T(8,128)(2,1)} %collective-permute-done.7.refs_1_, bf16[3584,128]{1,0:T(8,128)(2,1)S(1)} %collective-permute-done.8.refs_2_), custom_call_target="tpu_custom_call" | custom-call | flops 1 | bytes 1 | tf_op jit(solution)/shard_map/add/pallas_call | solution.py:237
  112.0 0.0 collective-permute-done.6.lm_ref
  112.0 5.7 %collective-permute-done.9.rm_ref = bf16[32,1792]{1,0:T(8,128)(2,1)S(1)} collective-permute-done((bf16[32,1792]{1,0:T(8,128)(2,1)S(1)}, bf16[32,1792]{1,0:T(8,128)(2,1)S(1)}, u32[]{:S(2)}, u32[]{:S(2)}) %collective-permute-start.9) | collective-permute-done | bytes 114720 | tf_op jit(solution)/shard_map/ppermute | solution.py:34
  117.7 2.6 %finish.1 = (bf16[64,3584]{1,0:T(8,128)(2,1)}, bf16[64,3584]{1,0:T(8,128)(2,1)}) custom-call(bf16[64,3584]{1,0:T(8,128)(2,1)} %collective-permute-done.1.l_ref, bf16[64,3584]{1,0:T(8,128)(2,1)} %collective-permute-done.5.r_ref, bf16[32,1792]{1,0:T(8,128)(2,1)S(1)} %collective-permute-done.6.lm_ref, bf16[32,1792]{1,0:T(8,128)(2,1)S(1)} %collective-permute-done.9.rm_ref), custom_call_target="tpu_custom_call" | custom-call | flops 1 | bytes 1 | tf_op jit(solution)/shard_map/finish/pallas_call | solution.py:325
  (1 shorter events, 0.0 us)
Async XLA Ops:
  0.6 12.8 %copy-start.7 = (bf16[1,3584,64]{1,2,0:T(8,128)(2,1)S(1)}, bf16[1,3584,64]{1,2,0:T(8,128)(2,1)}, u32[]{:S(2)}) copy-start(bf16[1,3584,64]{1,2,0:T(8,128)(2,1)} %param.18) | copy-start | bytes 1376260
  0.6 12.8 %copy-start.8 = (bf16[1,3584,64]{1,2,0:T(8,128)(2,1)S(1)}, bf16[1,3584,64]{1,2,0:T(8,128)(2,1)}, u32[]{:S(2)}) copy-start(bf16[1,3584,64]{1,2,0:T(8,128)(2,1)} %param.19) | copy-start | bytes 1376260
  3.2 13.3 %copy-start.9 = (bf16[1,64,3584]{2,1,0:T(8,128)(2,1)S(1)}, bf16[1,64,3584]{2,1,0:T(8,128)(2,1)}, u32[]{:S(2)}) copy-start(bf16[1,64,3584]{2,1,0:T(8,128)(2,1)} %param.14) | copy-start | bytes 1376260
  3.2 13.3 %copy-start.10 = (bf16[1,64,3584]{2,1,0:T(8,128)(2,1)S(1)}, bf16[1,64,3584]{2,1,0:T(8,128)(2,1)}, u32[]{:S(2)}) copy-start(bf16[1,64,3584]{2,1,0:T(8,128)(2,1)} %param.15) | copy-start | bytes 1376260
  3.2 13.3 %copy-start.12 = (s32[1,64,8]{1,2,0:T(8,128)S(1)}, s32[1,64,8]{1,2,0:T(8,128)}, u32[]{:S(2)}) copy-start(s32[1,64,8]{1,2,0:T(8,128)} %param.16) | copy-start | bytes 6148
  3.2 13.4 %copy-start.13 = (f32[1,64,8]{1,2,0:T(8,128)S(1)}, f32[1,64,8]{1,2,0:T(8,128)}, u32[]{:S(2)}) copy-start(f32[1,64,8]{1,2,0:T(8,128)} %param.17) | copy-start | bytes 6148
  3.2 31.6 %all-to-all-start = ((bf16[8,24,1792]{2,1,0:T(8,128)(2,1)}), bf16[8,24,1792]{2,1,0:T(8,128)(2,1)S(1)}, u32[]{:S(2)}, u32[]{:S(2)}) async-start(bf16[8,24,1792]{2,1,0:T(8,128)(2,1)} %bitcast.47), calls=%async_computation | async-start | bytes 1376256 | tf_op jit(solution)/shard_map/all_to_all | solution.py:355
  13.5 36.6 %collective-permute-start = (bf16[128,3584]{1,0:T(8,128)(2,1)S(1)}, bf16[128,3584]{1,0:T(8,128)(2,1)S(1)}, u32[]{:S(2)}, u32[]{:S(2)}) collective-permute-start(bf16[128,3584]{1,0:T(8,128)(2,1)S(1)} %pack.1.refs_0_), channel_id=1, source_target_pairs={{0,2},{1,3},{2,0},{3,1},{4,6},{5,7},{6,4},{7,5},{8,10},{9,11},{10,... | collective-permute-start | bytes 2752520 | tf_op jit(solution)/shard_map/ppermute | solution.py:34
  17.0 16.4 %collective-permute-start.2 = (bf16[64,1792]{1,0:T(8,128)(2,1)S(1)}, bf16[64,1792]{1,0:T(8,128)(2,1)S(1)}, u32[]{:S(2)}, u32[]{:S(2)}) collective-permute-start(bf16[64,1792]{1,0:T(8,128)(2,1)S(1)} %prepare.2), channel_id=1, source_target_pairs={{0,480},{32,448},{64,416},{96,384},{128,352},{160,320},{192,288},{... | collective-permute-start | bytes 688136 | tf_op jit(solution)/shard_map/ppermute | solution.py:34
  19.0 31.1 %collective-permute-start.1 = (bf16[64,3584]{1,0:T(8,128)(2,1)}, bf16[64,3584]{1,0:T(8,128)(2,1)}, u32[]{:S(2)}, u32[]{:S(2)}) collective-permute-start(bf16[64,3584]{1,0:T(8,128)(2,1)} %bitcast.4.c_ref), channel_id=1, source_target_pairs={{32,0},{64,32},{96,64},{128,96},{160,128},{192,160},{224,192},{256... | collective-permute-start | bytes 1376264 | tf_op jit(solution)/shard_map/ppermute | solution.py:34
  33.5 2.3 %copy-start.4 = (bf16[64,1792]{1,0:T(8,128)(2,1)}, bf16[64,1792]{1,0:T(8,128)(2,1)S(1)}, u32[]{:S(2)}) copy-start(bf16[64,1792]{1,0:T(8,128)(2,1)S(1)} %collective-permute-done.2.t_ref) | copy-start | bytes 688132
  35.8 25.0 %all-to-all-start.1 = ((bf16[8,24,1792]{2,1,0:T(8,128)(2,1)}), bf16[8,24,1792]{2,1,0:T(8,128)(2,1)S(1)}, u32[]{:S(2)}, u32[]{:S(2)}) async-start(bf16[8,24,1792]{2,1,0:T(8,128)(2,1)} %bitcast.46), calls=%async_computation.1 | async-start | bytes 1376256 | tf_op jit(solution)/shard_map/all_to_all | solution.py:355
  41.0 17.9 %collective-permute-start.3 = (bf16[128,3584]{1,0:T(8,128)(2,1)S(1)}, bf16[128,3584]{1,0:T(8,128)(2,1)S(1)}, u32[]{:S(2)}, u32[]{:S(2)}) collective-permute-start(bf16[128,3584]{1,0:T(8,128)(2,1)S(1)} %pack.1.refs_0_), channel_id=1, source_target_pairs={{0,1},{1,0},{2,3},{3,2},{4,5},{5,4},{6,7},{7,6},{8,9},{9,8},{10,11... | collective-permute-start | bytes 2752520 | tf_op jit(solution)/shard_map/ppermute | solution.py:34
  50.1 9.7 %collective-permute-start.4 = (bf16[128,3584]{1,0:T(8,128)(2,1)S(1)}, bf16[128,3584]{1,0:T(8,128)(2,1)S(1)}, u32[]{:S(2)}, u32[]{:S(2)}) collective-permute-start(bf16[128,3584]{1,0:T(8,128)(2,1)S(1)} %collective-permute-done.refs_2_), channel_id=1, source_target_pairs={{0,1},{1,0},{2,3},{3,2},{4,5},{5,4},{6,7},{7,6},{8,9},{9,8},{10,11... | collective-permute-start | bytes 2752520 | tf_op jit(solution)/shard_map/ppermute | solution.py:34
  53.8 16.1 %collective-permute-start.5 = (bf16[64,3584]{1,0:T(8,128)(2,1)}, bf16[64,3584]{1,0:T(8,128)(2,1)}, u32[]{:S(2)}, u32[]{:S(2)}) collective-permute-start(bf16[64,3584]{1,0:T(8,128)(2,1)} %bitcast.40), channel_id=1, source_target_pairs={{0,32},{32,64},{64,96},{96,128},{128,160},{160,192},{192,224},{224... | collective-permute-start | bytes 1376264 | tf_op jit(solution)/shard_map/ppermute | solution.py:34
  58.9 0.9 copy-start
  59.8 0.9 copy-start.2
  60.8 1.2 copy-start.1
  61.9 1.2 copy-start.3
  67.1 6.6 %copy-start.6 = (bf16[192,1792]{1,0:T(8,128)(2,1)}, bf16[192,1792]{1,0:T(8,128)(2,1)S(1)}, u32[]{:S(2)}) copy-start(bf16[192,1792]{1,0:T(8,128)(2,1)S(1)} %get-tuple-element.32) | copy-start | bytes 2064388
  69.9 9.2 %collective-permute-start.7 = (bf16[2,3584,128]{2,1,0:T(8,128)(2,1)}, bf16[2,3584,128]{2,1,0:T(8,128)(2,1)}, u32[]{:S(2)}, u32[]{:S(2)}) collective-permute-start(bf16[2,3584,128]{2,1,0:T(8,128)(2,1)} %get-tuple-element.35), channel_id=1, source_target_pairs={{0,1},{1,0},{2,3},{3,2},{4,5},{5,4},{6,7},{7,6},{8,9},{9,8},{10,11... | collective-permute-start | bytes 5505032 | tf_op jit(solution)/shard_map/ppermute | solution.py:34
  73.7 26.9 %all-to-all-start.2 = ((bf16[8,24,1792]{2,1,0:T(8,128)(2,1)}), bf16[8,24,1792]{2,1,0:T(8,128)(2,1)S(1)}, u32[]{:S(2)}, u32[]{:S(2)}) async-start(bf16[8,24,1792]{2,1,0:T(8,128)(2,1)} %bitcast.36), calls=%async_computation.2 | async-start | bytes 1376256 | tf_op jit(solution)/shard_map/all_to_all | solution.py:355
  79.1 21.5 %copy-start.11 = (s32[1,64,8]{1,2,0:T(8,128)S(1)}, s32[1,64,8]{1,2,0:T(8,128)}, u32[]{:S(2)}) copy-start(s32[1,64,8]{1,2,0:T(8,128)} %param.12) | copy-start | bytes 6148
  81.8 27.5 %collective-permute-start.8 = (bf16[3584,128]{1,0:T(8,128)(2,1)}, bf16[3584,128]{1,0:T(8,128)(2,1)S(1)}, u32[]{:S(2)}, u32[]{:S(2)}) collective-permute-start(bf16[3584,128]{1,0:T(8,128)(2,1)} %add.2), channel_id=1, source_target_pairs={{0,2},{1,3},{2,0},{3,1},{4,6},{5,7},{6,4},{7,5},{8,10},{9,11},{10,... | collective-permute-start | bytes 2752520 | tf_op jit(solution)/shard_map/ppermute | solution.py:34
  100.6 0.9 copy-start.5
  101.8 10.2 %collective-permute-start.6 = (bf16[32,1792]{1,0:T(8,128)(2,1)S(1)}, bf16[32,1792]{1,0:T(8,128)(2,1)S(1)}, u32[]{:S(2)}, u32[]{:S(2)}) collective-permute-start(bf16[32,1792]{1,0:T(8,128)(2,1)S(1)} %get-tuple-element.33), channel_id=1, source_target_pairs={{32,0},{64,32},{96,64},{128,96},{160,128},{192,160},{224,192},{256... | collective-permute-start | bytes 344072 | tf_op jit(solution)/shard_map/ppermute | solution.py:34
  107.3 10.4 %collective-permute-start.9 = (bf16[32,1792]{1,0:T(8,128)(2,1)S(1)}, bf16[32,1792]{1,0:T(8,128)(2,1)S(1)}, u32[]{:S(2)}, u32[]{:S(2)}) collective-permute-start(bf16[32,1792]{1,0:T(8,128)(2,1)S(1)} %get-tuple-element.37), channel_id=1, source_target_pairs={{32,480},{64,448},{96,416},{128,384},{160,352},{192,320},{224,288}... | collective-permute-start | bytes 344072 | tf_op jit(solution)/shard_map/ppermute | solution.py:34

commit v4 on v3

--- a/solution.py
+++ b/solution.py
@@ -15,8 +15,8 @@
 BLOCK = KINDS * CAP
 ROWS = RING * BLOCK
 KIND_ROWS = RING * CAP
+PIECES = 4
 TOPK = 8
-TAIL = 16
 ANY = pl.BlockSpec(memory_space=pl.ANY)
 VMEM = pl.BlockSpec(memory_space=pltpu.VMEM)
 SMEM = pl.BlockSpec(memory_space=pltpu.SMEM)
@@ -71,9 +71,7 @@
     return nn(experts.astype(jnp.bfloat16), one_hot(iota(shape, 0) == iota(shape, 1)))
 
 
-def prepare_kernel(copies, x_ref, c_ref, e_ref, g_ref, o_ref):
-    half = x_ref.shape[1] // 2
-    experts, gates = e_ref[...], g_ref[...]
+def dispatch_rows(experts, gates, sources):
     shape = (EXPERTS * BLOCK, experts.shape[1])
     row = iota(shape, 0)
     expert_of, kind, slot_of = row // BLOCK, (row // CAP) % KINDS, row % CAP
@@ -83,19 +81,26 @@
     ]
     gate = jnp.sum(table * jnp.where(expert_of == 0, gate[0], gate[1]), axis=1, keepdims=True)
     scale = jnp.where(kind[:, :1] % 2 == 1, gate, 1.0)
+    picks = [jnp.where(kind == k, table, 0.0).astype(jnp.bfloat16) for k in range(KINDS)]
     total = None
-    sources = (x_ref[:, :half], c_ref[:, :half], x_ref[:, half:], c_ref[:, half:])
-    for k, source in enumerate(sources):
-        part = nn(jnp.where(kind == k, table, 0.0).astype(jnp.bfloat16), source)
+    for pick, source in zip(picks, sources()):
+        part = nn(pick, source)
         total = part if total is None else total + part
-    total = total * scale
+    return (total * scale).astype(jnp.bfloat16)
+
+
+def prepare_kernel(copies, x_ref, c_ref, e_ref, g_ref, o_ref):
+    half = x_ref.shape[1] // 2
+
+    def sources():
+        return x_ref[:, :half], c_ref[:, :half], x_ref[:, half:], c_ref[:, half:]
+
+    rows = dispatch_rows(e_ref[...], g_ref[...], sources)
     if copies == 1:
-        tail = spread_experts(experts.astype(jnp.float32), half)
-        tail = jnp.concatenate([tail, jnp.zeros_like(tail)], axis=0)
-        o_ref[...] = jnp.concatenate([total, tail], axis=0).astype(jnp.bfloat16)
+        o_ref[...] = rows
     else:
         for e in range(EXPERTS):
-            one = total[e * BLOCK : (e + 1) * BLOCK].astype(jnp.bfloat16)
+            one = rows[e * BLOCK : (e + 1) * BLOCK]
             two = jnp.concatenate([one, one], axis=0)
             for i in range(copies // 2):
                 start = (e * copies + 2 * i) * BLOCK
@@ -103,10 +108,9 @@
 
 
 def prepare(x, cot, experts, gates, copies):
-    rows = EXPERTS * copies * BLOCK + (TAIL if copies == 1 else 0)
     return pl.pallas_call(
         functools.partial(prepare_kernel, copies),
-        out_shape=jax.ShapeDtypeStruct((rows, x.shape[1] // 2), jnp.bfloat16),
+        out_shape=jax.ShapeDtypeStruct((EXPERTS * copies * BLOCK, x.shape[1] // 2), jnp.bfloat16),
         in_specs=[VMEM] * 4,
         out_specs=VMEM,
         compiler_params=room(8) if copies == 1 else None,
@@ -180,7 +184,7 @@
             pltpu.VMEM((hidden, weights[0].shape[1]), jnp.bfloat16),
             pltpu.SemaphoreType.DMA((NEAR,)),
         ],
-        compiler_params=room(24),
+        compiler_params=room(48),
         cost_estimate=SHORT,
         name="experts",
     )(left, right, *weights)
@@ -221,28 +225,24 @@
     )(left, right, d_act, hid)
 
 
-def add_kernel(block, *refs):
-    depth = refs[-1].shape[0]
-    step = depth // 4
-    for i in range(4):
+def add_kernel(a_ref, b_ref, o_ref, *, block):
+    step = o_ref.shape[0] // PIECES
+    for i in range(PIECES):
         rows = slice(i * step, (i + 1) * step)
-        total = 0.0
-        for ref in refs[:-1]:
-            part = ref[block, rows, :] if len(ref.shape) == 3 else ref[rows, :]
-            total = total + part.astype(jnp.float32)
-        refs[-1][rows, :] = total.astype(jnp.bfloat16)
-
-
-def add_blocks(block, *parts):
-    return pl.pallas_call(
-        functools.partial(add_kernel, block),
-        out_shape=jax.ShapeDtypeStruct(parts[0].shape[1:], jnp.bfloat16),
-        in_specs=[VMEM] * len(parts),
+        a, b = (ref[rows, :] if block is None else ref[block, rows, :] for ref in (a_ref, b_ref))
+        o_ref[rows, :] = (a.astype(jnp.float32) + b.astype(jnp.float32)).astype(jnp.bfloat16)
+
+
+def add_blocks(a, b, block=None):
+    return pl.pallas_call(
+        functools.partial(add_kernel, block=block),
+        out_shape=jax.ShapeDtypeStruct(a.shape[-2:], jnp.bfloat16),
+        in_specs=[VMEM] * 2,
         out_specs=VMEM,
         compiler_params=room(12),
         cost_estimate=SHORT,
         name="add",
-    )(*parts)
+    )(a, b)
 
 
 def pack_kernel(up_ref, down_ref, o_ref):
@@ -263,20 +263,20 @@
     )(up, down)
 
 
-def collect_kernel(m_ref, e_ref, t_ref, l_ref, r_ref):
+def collect_kernel(m_ref, le_ref, re_ref, l_ref, r_ref):
     shape = (2 * BLOCK, ROWS)
     out, src = iota(shape, 0), iota(shape, 1)
     stream, half_of, expert = out // BLOCK, (out % BLOCK) // (2 * CAP), (out // CAP) % EXPERTS
     wanted = half_of * 2 * CAP + stream * CAP + out % CAP
     near = RING // EXPERTS * BLOCK
     total = nn(one_hot((src // near == expert) & (src % BLOCK == wanted)), m_ref[...])
-    left = spread_experts(e_ref[...].astype(jnp.float32), m_ref.shape[1])
-    right = t_ref[...].astype(jnp.float32)[EXPERTS * BLOCK : EXPERTS * BLOCK + TOPK]
-    l_ref[...] = jnp.concatenate([total[:BLOCK], left], axis=0).astype(jnp.bfloat16)
-    r_ref[...] = jnp.concatenate([total[BLOCK:], right], axis=0).astype(jnp.bfloat16)
-
-
-def collect(back, left_experts, right_message):
+    for i, (e_ref, o_ref) in enumerate(((le_ref, l_ref), (re_ref, r_ref))):
+        table = spread_experts(e_ref[...].astype(jnp.float32), m_ref.shape[1])
+        sums = total[i * BLOCK : (i + 1) * BLOCK]
+        o_ref[...] = jnp.concatenate([sums, table], axis=0).astype(jnp.bfloat16)
+
+
+def collect(back, left_experts, right_experts):
     one = jax.ShapeDtypeStruct((BLOCK + TOPK, back.shape[1]), jnp.bfloat16)
     return pl.pallas_call(
         collect_kernel,
@@ -286,7 +286,7 @@
         compiler_params=room(8),
         cost_estimate=SHORT,
         name="collect",
-    )(back, left_experts, right_message)
+    )(back, left_experts, right_experts)
 
 
 def finish_kernel(l_ref, r_ref, lm_ref, rm_ref, lo_ref, ro_ref, c_ref, o_ref, in_sems, out_sems):
@@ -361,7 +361,8 @@
     left_rows = along_z(left)
     message = prepare(right_x[0], right_cot[0], right_experts[0].T, right_gates[0].T, 1)
     message = send(message, "section", lambda s: n_sec - 1 - s)
-    right = message[: EXPERTS * BLOCK].reshape(EXPERTS, 1, BLOCK, half)
+    mirrored = send(right_experts[0].T, "section", lambda s: n_sec - 1 - s)
+    right = message.reshape(EXPERTS, 1, BLOCK, half)
     right = jnp.repeat(right, copies, axis=1).reshape(ROWS, half)
 
     own = pack(up_weight[0].T, down_weight[0].T)
@@ -372,7 +373,7 @@
     last_cot = send(right_cot[0], "section", lambda s: s + 1)
     right, left_rows = lax.optimization_barrier((right, left_rows))
     right_rows = along_z(right)
-    across, next_cot = lax.optimization_barrier((across, next_cot))
+    across, next_cot, mirrored = lax.optimization_barrier((across, next_cot, mirrored))
     corner = send(across, "expert", lambda j: j ^ 1)
 
     weights = (own, beside, across, corner)
@@ -382,10 +383,10 @@
     kept, given = gradient(left_rows, right_rows, d_act, hid)
     given, last_cot = lax.optimization_barrier((given, last_cot))
     given = send(given, "expert", lambda j: j ^ 1)
-    given_far = send(add_blocks(1, kept, given), "expert", lambda j: j ^ 2)
-    layer_grad = add_blocks(0, kept, given, given_far)
-
-    left_back, right_back = collect(back, left_experts[0].T, message)
+    far = send(add_blocks(kept, given, 1), "expert", lambda j: j ^ 2)
+    layer_grad = add_blocks(add_blocks(kept, given, 0), far)
+
+    left_back, right_back = collect(back, left_experts[0].T, mirrored)
     next_slots = send(left_back, "section", lambda s: s - 1)
     last_slots = send(right_back, "section", lambda s: n_sec - s)
     next_slots, layer_grad = lax.optimization_barrier((next_slots, layer_grad))

time: 121 us -> 119 us (0.983)
  local copies, waits for them, and re-layouts: 6.1 us -> 0.93 us
  waiting for transfers between devices: 39 us -> 42.1 us
    unnamed x28 -> x16, local copies, waits for them, and re-layouts: 5.19 us -> 0.03 us
    all_to_all x3, waiting for transfers between devices: 17.3 us -> 21.3 us  [along_z(): lax.all_to_all(value, 'expert', split_axis=0, concat_axis=0, tiled=True,...]
    ppermute x10 -> x11, waiting for transfers between devices: 21.7 us -> 20.8 us  [send(): lax.ppermute(value, axis, [(a, b) for a, b in pairs if 0 <= b < size])]
    ppermute x10 -> x11, starting transfers between devices: 35.9 us -> 35.5 us  [send(): lax.ppermute(value, axis, [(a, b) for a, b in pairs if 0 <= b < size])]
    pallas_call x2 -> x3, Pallas kernels: 5.39 us -> 5.51 us  [add_blocks(): pl.pallas_call(functools.partial(add_kernel, block=block), out_shape=jax....]
  transfers between devices with their start and end apart: 13 -> 14, of which waited for: 6 -> 8; matrix products, arithmetic and copies ran while one was open for 1% -> 1% of each run, Pallas kernels for 10% -> 11%
where the time goes in v4:
time: 119 us; the launch traced here: 118 us
  starting transfers between devices  55.9 us (47%)
  waiting for transfers between devices  42.1 us (35%)
  Pallas kernels  18.6 us (16%)
    ppermute x11, starting transfers between devices, send(): lax.ppermute(value, axis, [(a, b) for a, b in pairs if 0 <= b < size])  35.5 us
    all_to_all x3, waiting for transfers between devices, along_z(): lax.all_to_all(value, 'expert', split_axis=0, concat_axis=0, tiled=True,...  21.3 us
    ppermute x11, waiting for transfers between devices, send(): lax.ppermute(value, axis, [(a, b) for a, b in pairs if 0 <= b < size])  20.8 us
    all_to_all x3, starting transfers between devices, along_z(): lax.all_to_all(value, 'expert', split_axis=0, concat_axis=0, tiled=True,...  20.4 us
    pallas_call x3, Pallas kernels, add_blocks(): pl.pallas_call(functools.partial(add_kernel, block=block), out_shape=jax....  5.51 us
    pallas_call x1, Pallas kernels, experts_backward(): pl.pallas_call(experts_kernel, out_shape=(rows, rows, units, units, rows)...  4.76 us
    pallas_call x2, Pallas kernels, prepare(): pl.pallas_call(functools.partial(prepare_kernel, copies), out_shape=jax.S...  3 us
    pallas_call x1, Pallas kernels, finish(): pl.pallas_call(finish_kernel, out_shape=(shape, shape), in_specs=[ANY] *...  2.64 us
  transfers between devices with their start and end apart: 14, of which 8 were waited for; matrix products, arithmetic and copies ran while one was open for 1% of the time, Pallas kernels for 11%

profile of v4, /device:TPU:39, one launch (start us, length us, event | category | flops | bytes accessed | tf_op | source)
XLA Modules:
  0.0 118.4 jit_solution(1690173304880610290)
XLA Ops:
  0.6 0.0 copy-start.1
  0.6 0.0 copy-start.2
  0.7 2.5 %prepare.3 = bf16[192,1792]{1,0:T(8,128)(2,1)} custom-call(bf16[64,3584]{1,0:T(8,128)(2,1)} %bitcast.49, bf16[64,3584]{1,0:T(8,128)(2,1)} %bitcast.4.c_ref, s32[8,64]{1,0:T(8,128)} %bitcast.42, f32[8,64]{1,0:T(8,128)} %bitcast.51), custom_call_target="tpu_custom_call" | custom-call | flops 1 | bytes 1 | tf_op jit(solution)/shard_map/prepare/pallas_call | solution.py:111
  3.2 0.0 copy-start.3
  3.2 0.0 copy-start.4
  3.2 0.0 copy-start.6
  3.2 0.0 copy-start.7
  3.2 10.2 %all-to-all-start = ((bf16[8,24,1792]{2,1,0:T(8,128)(2,1)}), bf16[8,24,1792]{2,1,0:T(8,128)(2,1)S(1)}, u32[]{:S(2)}, u32[]{:S(2)}) async-start(bf16[8,24,1792]{2,1,0:T(8,128)(2,1)} %bitcast.47), calls=%async_computation | async-start | bytes 1376256 | tf_op jit(solution)/shard_map/all_to_all | solution.py:355
  13.4 0.0 copy-done.1
  13.4 0.0 copy-done.2
  13.4 0.1 pack.1.refs_0_
  13.5 3.0 %collective-permute-start = (bf16[128,3584]{1,0:T(8,128)(2,1)S(1)}, bf16[128,3584]{1,0:T(8,128)(2,1)}, u32[]{:S(2)}, u32[]{:S(2)}) collective-permute-start(bf16[128,3584]{1,0:T(8,128)(2,1)S(1)} %pack.1.refs_0_), channel_id=1, source_target_pairs={{0,2},{1,3},{2,0},{3,1},{4,6},{5,7},{6,4},{7,5},{8,10},{9,11},{10,... | collective-permute-start | bytes 2752520 | tf_op jit(solution)/shard_map/ppermute | solution.py:34
  16.5 0.0 copy-done.3
  16.5 0.0 copy-done.4
  16.5 0.0 copy-done.6
  16.6 0.0 copy-done.7
  16.6 0.5 prepare.2
  17.0 1.9 %collective-permute-start.3 = (bf16[48,1792]{1,0:T(8,128)(2,1)S(1)}, bf16[48,1792]{1,0:T(8,128)(2,1)S(1)}, u32[]{:S(2)}, u32[]{:S(2)}) collective-permute-start(bf16[48,1792]{1,0:T(8,128)(2,1)S(1)} %prepare.2), channel_id=1, source_target_pairs={{0,480},{32,448},{64,416},{96,384},{128,352},{160,320},{192,288},{... | collective-permute-start | bytes 516104 | tf_op jit(solution)/shard_map/ppermute | solution.py:34
  19.0 3.3 %collective-permute-start.1 = (bf16[64,3584]{1,0:T(8,128)(2,1)}, bf16[64,3584]{1,0:T(8,128)(2,1)}, u32[]{:S(2)}, u32[]{:S(2)}) collective-permute-start(bf16[64,3584]{1,0:T(8,128)(2,1)} %bitcast.4.c_ref), channel_id=1, source_target_pairs={{32,0},{64,32},{96,64},{128,96},{160,128},{192,160},{224,192},{256... | collective-permute-start | bytes 1376264 | tf_op jit(solution)/shard_map/ppermute | solution.py:34
  22.2 8.6 %collective-permute-done.3 = bf16[48,1792]{1,0:T(8,128)(2,1)S(1)} collective-permute-done((bf16[48,1792]{1,0:T(8,128)(2,1)S(1)}, bf16[48,1792]{1,0:T(8,128)(2,1)S(1)}, u32[]{:S(2)}, u32[]{:S(2)}) %collective-permute-start.3) | collective-permute-done | bytes 172064 | tf_op jit(solution)/shard_map/ppermute | solution.py:34
  30.8 4.1 %all-to-all-done = bf16[8,24,1792]{2,1,0:T(8,128)(2,1)S(1)} async-done(((bf16[8,24,1792]{2,1,0:T(8,128)(2,1)}), bf16[8,24,1792]{2,1,0:T(8,128)(2,1)S(1)}, u32[]{:S(2)}, u32[]{:S(2)}) %all-to-all-start) | async-done | bytes 688160 | tf_op jit(solution)/shard_map/all_to_all | solution.py:355
  34.9 0.9 broadcast_in_dim.12
  35.8 3.5 %all-to-all-start.1 = ((bf16[8,24,1792]{2,1,0:T(8,128)(2,1)}), bf16[8,24,1792]{2,1,0:T(8,128)(2,1)S(1)}, u32[]{:S(2)}, u32[]{:S(2)}) async-start(bf16[8,24,1792]{2,1,0:T(8,128)(2,1)} %bitcast.21), calls=%async_computation.1 | async-start | bytes 1376256 | tf_op jit(solution)/shard_map/all_to_all | solution.py:355
  39.3 2.3 %collective-permute-start.2 = (s32[8,64]{1,0:T(8,128)S(1)}, s32[8,64]{1,0:T(8,128)S(1)}, u32[]{:S(2)}, u32[]{:S(2)}) collective-permute-start(s32[8,64]{1,0:T(8,128)S(1)} %bitcast.46), channel_id=1, source_target_pairs={{0,480},{32,448},{64,416},{96,384},{128,352},{160,320},{192,288},{... | collective-permute-start | bytes 6152 | tf_op jit(solution)/shard_map/ppermute | solution.py:34
  41.7 3.3 %collective-permute-start.4 = (bf16[128,3584]{1,0:T(8,128)(2,1)S(1)}, bf16[128,3584]{1,0:T(8,128)(2,1)S(1)}, u32[]{:S(2)}, u32[]{:S(2)}) collective-permute-start(bf16[128,3584]{1,0:T(8,128)(2,1)S(1)} %pack.1.refs_0_), channel_id=1, source_target_pairs={{0,1},{1,0},{2,3},{3,2},{4,5},{5,4},{6,7},{7,6},{8,9},{9,8},{10,11... | collective-permute-start | bytes 2752520 | tf_op jit(solution)/shard_map/ppermute | solution.py:34
  45.0 0.9 collective-permute-done.2.re_ref
  45.9 3.1 %collective-permute-done.1.l_ref = bf16[64,3584]{1,0:T(8,128)(2,1)} collective-permute-done((bf16[64,3584]{1,0:T(8,128)(2,1)}, bf16[64,3584]{1,0:T(8,128)(2,1)}, u32[]{:S(2)}, u32[]{:S(2)}) %collective-permute-start.1) | collective-permute-done | bytes 458784 | tf_op jit(solution)/shard_map/ppermute | solution.py:34
  48.9 0.0 collective-permute-done.refs_2_
  48.9 3.8 %collective-permute-start.5 = (bf16[128,3584]{1,0:T(8,128)(2,1)}, bf16[128,3584]{1,0:T(8,128)(2,1)}, u32[]{:S(2)}, u32[]{:S(2)}) collective-permute-start(bf16[128,3584]{1,0:T(8,128)(2,1)} %collective-permute-done.refs_2_), channel_id=1, source_target_pairs={{0,1},{1,0},{2,3},{3,2},{4,5},{5,4},{6,7},{7,6},{8,9},{9,8},{10,11... | collective-permute-start | bytes 2752520 | tf_op jit(solution)/shard_map/ppermute | solution.py:34
  52.7 5.1 %collective-permute-start.6 = (bf16[64,3584]{1,0:T(8,128)(2,1)}, bf16[64,3584]{1,0:T(8,128)(2,1)}, u32[]{:S(2)}, u32[]{:S(2)}) collective-permute-start(bf16[64,3584]{1,0:T(8,128)(2,1)} %bitcast.40), channel_id=1, source_target_pairs={{0,32},{32,64},{64,96},{96,128},{128,160},{160,192},{192,224},{224... | collective-permute-start | bytes 1376264 | tf_op jit(solution)/shard_map/ppermute | solution.py:34
  57.8 0.0 collective-permute-done.4.refs_1_
  57.8 0.0 collective-permute-done.5.refs_3_
  57.9 1.2 all-to-all-done.1
  59.0 4.8 %experts.1 = (bf16[192,1792]{1,0:T(8,128)(2,1)S(1)}, bf16[192,1792]{1,0:T(8,128)(2,1)S(1)}, bf16[96,512]{1,0:T(8,128)(2,1)S(1)}, bf16[96,512]{1,0:T(8,128)(2,1)S(1)}, bf16[192,1792]{1,0:T(8,128)(2,1)S(1)}) custom-call(bf16[192,1792]{1,0:T(8,128)(2,1)S(1)} %bitcast.33, bf16[192,1792]{1,0:T(8,128)(2,1)S(1)} %bitcast.34, bf16[128,3584]{1,0:T(8,128)(2,1)S(1)} %pack.1.refs_0_, ...), custom_call_target="tpu_custom_call" | custom-call | flops 1 | bytes 1 | tf_op jit(solution)/shard_map/experts/pallas_call | solution.py:178
  63.8 0.0 copy-start
  63.8 2.4 %gradient.1 = (bf16[2,3584,128]{2,1,0:T(8,128)(2,1)S(1)}, bf16[2,3584,128]{2,1,0:T(8,128)(2,1)}) custom-call(bf16[192,1792]{1,0:T(8,128)(2,1)S(1)} %get-tuple-element.27.la_ref, bf16[192,1792]{1,0:T(8,128)(2,1)S(1)} %get-tuple-element.28.ra_ref, bf16[96,512]{1,0:T(8,128)(2,1)S(1)} %get-tuple-element.29.da_ref, bf16[96,512]{1,0:T(8,128)(2,1)S(1)} %get-tuple-element.30.hid_ref), custom_call_target="tpu_custom_call" | custom-call | flops 1 | bytes 1 | tf_op jit(solution)/shard_map/gradient/pallas_call | solution.py:217
  66.2 2.7 %collective-permute-done.6.r_ref = bf16[64,3584]{1,0:T(8,128)(2,1)} collective-permute-done((bf16[64,3584]{1,0:T(8,128)(2,1)}, bf16[64,3584]{1,0:T(8,128)(2,1)}, u32[]{:S(2)}, u32[]{:S(2)}) %collective-permute-start.6) | collective-permute-done | bytes 458784 | tf_op jit(solution)/shard_map/ppermute | solution.py:34
  68.9 2.5 %collective-permute-start.8 = (bf16[2,3584,128]{2,1,0:T(8,128)(2,1)}, bf16[2,3584,128]{2,1,0:T(8,128)(2,1)}, u32[]{:S(2)}, u32[]{:S(2)}) collective-permute-start(bf16[2,3584,128]{2,1,0:T(8,128)(2,1)} %get-tuple-element.37), channel_id=1, source_target_pairs={{0,1},{1,0},{2,3},{3,2},{4,5},{5,4},{6,7},{7,6},{8,9},{9,8},{10,11... | collective-permute-start | bytes 5505032 | tf_op jit(solution)/shard_map/ppermute | solution.py:34
  71.4 0.0 copy-done
  71.4 6.7 %all-to-all-start.2 = ((bf16[8,24,1792]{2,1,0:T(8,128)(2,1)}), bf16[8,24,1792]{2,1,0:T(8,128)(2,1)S(1)}, u32[]{:S(2)}, u32[]{:S(2)}) async-start(bf16[8,24,1792]{2,1,0:T(8,128)(2,1)} %bitcast.36), calls=%async_computation.2 | async-start | bytes 1376256 | tf_op jit(solution)/shard_map/all_to_all | solution.py:355
  78.1 0.0 collective-permute-done.8.b_ref
  78.1 0.0 copy-start.5
  78.1 2.6 %add.4 = bf16[3584,128]{1,0:T(8,128)(2,1)} custom-call(bf16[2,3584,128]{2,1,0:T(8,128)(2,1)S(1)} %get-tuple-element.36.a_ref, bf16[2,3584,128]{2,1,0:T(8,128)(2,1)} %collective-permute-done.8.b_ref), custom_call_target="tpu_custom_call" | custom-call | flops 1 | bytes 1 | tf_op jit(solution)/shard_map/add/pallas_call | solution.py:237
  80.7 2.8 %collective-permute-start.9 = (bf16[3584,128]{1,0:T(8,128)(2,1)}, bf16[3584,128]{1,0:T(8,128)(2,1)S(1)}, u32[]{:S(2)}, u32[]{:S(2)}) collective-permute-start(bf16[3584,128]{1,0:T(8,128)(2,1)} %add.4), channel_id=1, source_target_pairs={{0,2},{1,3},{2,0},{3,1},{4,6},{5,7},{6,4},{7,5},{8,10},{9,11},{10,... | collective-permute-start | bytes 2752520 | tf_op jit(solution)/shard_map/ppermute | solution.py:34
  83.5 16.0 %all-to-all-done.2 = bf16[8,24,1792]{2,1,0:T(8,128)(2,1)S(1)} async-done(((bf16[8,24,1792]{2,1,0:T(8,128)(2,1)}), bf16[8,24,1792]{2,1,0:T(8,128)(2,1)S(1)}, u32[]{:S(2)}, u32[]{:S(2)}) %all-to-all-start.2) | async-done | bytes 688160 | tf_op jit(solution)/shard_map/all_to_all | solution.py:355
  99.6 0.0 copy-done.5
  99.6 0.3 collect.1
  99.8 5.5 %collective-permute-start.7 = (bf16[32,1792]{1,0:T(8,128)(2,1)S(1)}, bf16[32,1792]{1,0:T(8,128)(2,1)S(1)}, u32[]{:S(2)}, u32[]{:S(2)}) collective-permute-start(bf16[32,1792]{1,0:T(8,128)(2,1)S(1)} %get-tuple-element.35), channel_id=1, source_target_pairs={{32,0},{64,32},{96,64},{128,96},{160,128},{192,160},{224,192},{256... | collective-permute-start | bytes 344072 | tf_op jit(solution)/shard_map/ppermute | solution.py:34
  105.3 1.9 %collective-permute-start.10 = (bf16[32,1792]{1,0:T(8,128)(2,1)S(1)}, bf16[32,1792]{1,0:T(8,128)(2,1)S(1)}, u32[]{:S(2)}, u32[]{:S(2)}) collective-permute-start(bf16[32,1792]{1,0:T(8,128)(2,1)S(1)} %get-tuple-element.39), channel_id=1, source_target_pairs={{32,480},{64,448},{96,416},{128,384},{160,352},{192,320},{224,288}... | collective-permute-start | bytes 344072 | tf_op jit(solution)/shard_map/ppermute | solution.py:34
  107.3 1.7 %add.3.a_ref = bf16[3584,128]{1,0:T(8,128)(2,1)S(1)} custom-call(bf16[2,3584,128]{2,1,0:T(8,128)(2,1)S(1)} %get-tuple-element.36.a_ref, bf16[2,3584,128]{2,1,0:T(8,128)(2,1)} %collective-permute-done.8.b_ref), custom_call_target="tpu_custom_call" | custom-call | flops 1 | bytes 1 | tf_op jit(solution)/shard_map/add/pallas_call | solution.py:237
  109.0 0.0 collective-permute-done.9.b_ref
  109.0 1.2 add.5
  110.1 0.0 collective-permute-done.7.lm_ref
  110.1 5.6 %collective-permute-done.10.rm_ref = bf16[32,1792]{1,0:T(8,128)(2,1)S(1)} collective-permute-done((bf16[32,1792]{1,0:T(8,128)(2,1)S(1)}, bf16[32,1792]{1,0:T(8,128)(2,1)S(1)}, u32[]{:S(2)}, u32[]{:S(2)}) %collective-permute-start.10) | collective-permute-done | bytes 114720 | tf_op jit(solution)/shard_map/ppermute | solution.py:34
  115.8 2.6 %finish.1 = (bf16[64,3584]{1,0:T(8,128)(2,1)}, bf16[64,3584]{1,0:T(8,128)(2,1)}) custom-call(bf16[64,3584]{1,0:T(8,128)(2,1)} %collective-permute-done.1.l_ref, bf16[64,3584]{1,0:T(8,128)(2,1)} %collective-permute-done.6.r_ref, bf16[32,1792]{1,0:T(8,128)(2,1)S(1)} %collective-permute-done.7.lm_ref, bf16[32,1792]{1,0:T(8,128)(2,1)S(1)} %collective-permute-done.10.rm_ref), custom_call_target="tpu_custom_call" | custom-call | flops 1 | bytes 1 | tf_op jit(solution)/shard_map/finish/pallas_call | solution.py:325
Async XLA Ops:
  0.6 12.8 %copy-start.1 = (bf16[1,3584,64]{1,2,0:T(8,128)(2,1)S(1)}, bf16[1,3584,64]{1,2,0:T(8,128)(2,1)}, u32[]{:S(2)}) copy-start(bf16[1,3584,64]{1,2,0:T(8,128)(2,1)} %param.18) | copy-start | bytes 1376260
  0.6 12.8 %copy-start.2 = (bf16[1,3584,64]{1,2,0:T(8,128)(2,1)S(1)}, bf16[1,3584,64]{1,2,0:T(8,128)(2,1)}, u32[]{:S(2)}) copy-start(bf16[1,3584,64]{1,2,0:T(8,128)(2,1)} %param.19) | copy-start | bytes 1376260
  3.2 13.3 %copy-start.3 = (bf16[1,64,3584]{2,1,0:T(8,128)(2,1)S(1)}, bf16[1,64,3584]{2,1,0:T(8,128)(2,1)}, u32[]{:S(2)}) copy-start(bf16[1,64,3584]{2,1,0:T(8,128)(2,1)} %param.14) | copy-start | bytes 1376260
  3.2 13.3 %copy-start.4 = (bf16[1,64,3584]{2,1,0:T(8,128)(2,1)S(1)}, bf16[1,64,3584]{2,1,0:T(8,128)(2,1)}, u32[]{:S(2)}) copy-start(bf16[1,64,3584]{2,1,0:T(8,128)(2,1)} %param.15) | copy-start | bytes 1376260
  3.2 13.3 %copy-start.6 = (f32[1,64,8]{1,2,0:T(8,128)S(1)}, f32[1,64,8]{1,2,0:T(8,128)}, u32[]{:S(2)}) copy-start(f32[1,64,8]{1,2,0:T(8,128)} %param.17) | copy-start | bytes 6148
  3.2 13.4 %copy-start.7 = (s32[1,64,8]{1,2,0:T(8,128)S(1)}, s32[1,64,8]{1,2,0:T(8,128)}, u32[]{:S(2)}) copy-start(s32[1,64,8]{1,2,0:T(8,128)} %param.16) | copy-start | bytes 6148
  3.2 31.6 %all-to-all-start = ((bf16[8,24,1792]{2,1,0:T(8,128)(2,1)}), bf16[8,24,1792]{2,1,0:T(8,128)(2,1)S(1)}, u32[]{:S(2)}, u32[]{:S(2)}) async-start(bf16[8,24,1792]{2,1,0:T(8,128)(2,1)} %bitcast.47), calls=%async_computation | async-start | bytes 1376256 | tf_op jit(solution)/shard_map/all_to_all | solution.py:355
  13.5 35.4 %collective-permute-start = (bf16[128,3584]{1,0:T(8,128)(2,1)S(1)}, bf16[128,3584]{1,0:T(8,128)(2,1)}, u32[]{:S(2)}, u32[]{:S(2)}) collective-permute-start(bf16[128,3584]{1,0:T(8,128)(2,1)S(1)} %pack.1.refs_0_), channel_id=1, source_target_pairs={{0,2},{1,3},{2,0},{3,1},{4,6},{5,7},{6,4},{7,5},{8,10},{9,11},{10,... | collective-permute-start | bytes 2752520 | tf_op jit(solution)/shard_map/ppermute | solution.py:34
  17.0 13.7 %collective-permute-start.3 = (bf16[48,1792]{1,0:T(8,128)(2,1)S(1)}, bf16[48,1792]{1,0:T(8,128)(2,1)S(1)}, u32[]{:S(2)}, u32[]{:S(2)}) collective-permute-start(bf16[48,1792]{1,0:T(8,128)(2,1)S(1)} %prepare.2), channel_id=1, source_target_pairs={{0,480},{32,448},{64,416},{96,384},{128,352},{160,320},{192,288},{... | collective-permute-start | bytes 516104 | tf_op jit(solution)/shard_map/ppermute | solution.py:34
  19.0 30.0 %collective-permute-start.1 = (bf16[64,3584]{1,0:T(8,128)(2,1)}, bf16[64,3584]{1,0:T(8,128)(2,1)}, u32[]{:S(2)}, u32[]{:S(2)}) collective-permute-start(bf16[64,3584]{1,0:T(8,128)(2,1)} %bitcast.4.c_ref), channel_id=1, source_target_pairs={{32,0},{64,32},{96,64},{128,96},{160,128},{192,160},{224,192},{256... | collective-permute-start | bytes 1376264 | tf_op jit(solution)/shard_map/ppermute | solution.py:34
  35.8 23.3 %all-to-all-start.1 = ((bf16[8,24,1792]{2,1,0:T(8,128)(2,1)}), bf16[8,24,1792]{2,1,0:T(8,128)(2,1)S(1)}, u32[]{:S(2)}, u32[]{:S(2)}) async-start(bf16[8,24,1792]{2,1,0:T(8,128)(2,1)} %bitcast.21), calls=%async_computation.1 | async-start | bytes 1376256 | tf_op jit(solution)/shard_map/all_to_all | solution.py:355
  39.3 6.6 %collective-permute-start.2 = (s32[8,64]{1,0:T(8,128)S(1)}, s32[8,64]{1,0:T(8,128)S(1)}, u32[]{:S(2)}, u32[]{:S(2)}) collective-permute-start(s32[8,64]{1,0:T(8,128)S(1)} %bitcast.46), channel_id=1, source_target_pairs={{0,480},{32,448},{64,416},{96,384},{128,352},{160,320},{192,288},{... | collective-permute-start | bytes 6152 | tf_op jit(solution)/shard_map/ppermute | solution.py:34
  41.7 16.2 %collective-permute-start.4 = (bf16[128,3584]{1,0:T(8,128)(2,1)S(1)}, bf16[128,3584]{1,0:T(8,128)(2,1)S(1)}, u32[]{:S(2)}, u32[]{:S(2)}) collective-permute-start(bf16[128,3584]{1,0:T(8,128)(2,1)S(1)} %pack.1.refs_0_), channel_id=1, source_target_pairs={{0,1},{1,0},{2,3},{3,2},{4,5},{5,4},{6,7},{7,6},{8,9},{9,8},{10,11... | collective-permute-start | bytes 2752520 | tf_op jit(solution)/shard_map/ppermute | solution.py:34
  48.9 8.9 %collective-permute-start.5 = (bf16[128,3584]{1,0:T(8,128)(2,1)}, bf16[128,3584]{1,0:T(8,128)(2,1)}, u32[]{:S(2)}, u32[]{:S(2)}) collective-permute-start(bf16[128,3584]{1,0:T(8,128)(2,1)} %collective-permute-done.refs_2_), channel_id=1, source_target_pairs={{0,1},{1,0},{2,3},{3,2},{4,5},{5,4},{6,7},{7,6},{8,9},{9,8},{10,11... | collective-permute-start | bytes 2752520 | tf_op jit(solution)/shard_map/ppermute | solution.py:34
  52.7 16.2 %collective-permute-start.6 = (bf16[64,3584]{1,0:T(8,128)(2,1)}, bf16[64,3584]{1,0:T(8,128)(2,1)}, u32[]{:S(2)}, u32[]{:S(2)}) collective-permute-start(bf16[64,3584]{1,0:T(8,128)(2,1)} %bitcast.40), channel_id=1, source_target_pairs={{0,32},{32,64},{64,96},{96,128},{128,160},{160,192},{192,224},{224... | collective-permute-start | bytes 1376264 | tf_op jit(solution)/shard_map/ppermute | solution.py:34
  63.8 7.6 %copy-start = (bf16[192,1792]{1,0:T(8,128)(2,1)}, bf16[192,1792]{1,0:T(8,128)(2,1)S(1)}, u32[]{:S(2)}) copy-start(bf16[192,1792]{1,0:T(8,128)(2,1)S(1)} %get-tuple-element.33) | copy-start | bytes 2064388
  68.9 9.2 %collective-permute-start.8 = (bf16[2,3584,128]{2,1,0:T(8,128)(2,1)}, bf16[2,3584,128]{2,1,0:T(8,128)(2,1)}, u32[]{:S(2)}, u32[]{:S(2)}) collective-permute-start(bf16[2,3584,128]{2,1,0:T(8,128)(2,1)} %get-tuple-element.37), channel_id=1, source_target_pairs={{0,1},{1,0},{2,3},{3,2},{4,5},{5,4},{6,7},{7,6},{8,9},{9,8},{10,11... | collective-permute-start | bytes 5505032 | tf_op jit(solution)/shard_map/ppermute | solution.py:34
  71.4 28.1 %all-to-all-start.2 = ((bf16[8,24,1792]{2,1,0:T(8,128)(2,1)}), bf16[8,24,1792]{2,1,0:T(8,128)(2,1)S(1)}, u32[]{:S(2)}, u32[]{:S(2)}) async-start(bf16[8,24,1792]{2,1,0:T(8,128)(2,1)} %bitcast.36), calls=%async_computation.2 | async-start | bytes 1376256 | tf_op jit(solution)/shard_map/all_to_all | solution.py:355
  78.1 21.5 %copy-start.5 = (s32[1,64,8]{1,2,0:T(8,128)S(1)}, s32[1,64,8]{1,2,0:T(8,128)}, u32[]{:S(2)}) copy-start(s32[1,64,8]{1,2,0:T(8,128)} %param.12) | copy-start | bytes 6148
  80.7 28.2 %collective-permute-start.9 = (bf16[3584,128]{1,0:T(8,128)(2,1)}, bf16[3584,128]{1,0:T(8,128)(2,1)S(1)}, u32[]{:S(2)}, u32[]{:S(2)}) collective-permute-start(bf16[3584,128]{1,0:T(8,128)(2,1)} %add.4), channel_id=1, source_target_pairs={{0,2},{1,3},{2,0},{3,1},{4,6},{5,7},{6,4},{7,5},{8,10},{9,11},{10,... | collective-permute-start | bytes 2752520 | tf_op jit(solution)/shard_map/ppermute | solution.py:34
  99.8 10.3 %collective-permute-start.7 = (bf16[32,1792]{1,0:T(8,128)(2,1)S(1)}, bf16[32,1792]{1,0:T(8,128)(2,1)S(1)}, u32[]{:S(2)}, u32[]{:S(2)}) collective-permute-start(bf16[32,1792]{1,0:T(8,128)(2,1)S(1)} %get-tuple-element.35), channel_id=1, source_target_pairs={{32,0},{64,32},{96,64},{128,96},{160,128},{192,160},{224,192},{256... | collective-permute-start | bytes 344072 | tf_op jit(solution)/shard_map/ppermute | solution.py:34
  105.3 10.4 %collective-permute-start.10 = (bf16[32,1792]{1,0:T(8,128)(2,1)S(1)}, bf16[32,1792]{1,0:T(8,128)(2,1)S(1)}, u32[]{:S(2)}, u32[]{:S(2)}) collective-permute-start(bf16[32,1792]{1,0:T(8,128)(2,1)S(1)} %get-tuple-element.39), channel_id=1, source_target_pairs={{32,480},{64,448},{96,416},{128,384},{160,352},{192,320},{224,288}... | collective-permute-start | bytes 344072 | tf_op jit(solution)/shard_map/ppermute | solution.py:34

commit v5 on v4

--- a/solution.py
+++ b/solution.py
@@ -225,20 +225,37 @@
     )(left, right, d_act, hid)
 
 
-def add_kernel(a_ref, b_ref, o_ref, *, block):
+def add_kernel(a_ref, b_ref, o_ref, in_ref=None, sems=None, *, block):
     step = o_ref.shape[0] // PIECES
+    copies = []
+    if block is not None:
+        for i in range(PIECES):
+            source = b_ref.at[block, pl.ds(i * step, step)]
+            copies.append(pltpu.make_async_copy(source, in_ref.at[i], sems.at[i]))
+            copies[i].start()
     for i in range(PIECES):
         rows = slice(i * step, (i + 1) * step)
-        a, b = (ref[rows, :] if block is None else ref[block, rows, :] for ref in (a_ref, b_ref))
+        if block is None:
+            a, b = a_ref[rows, :], b_ref[rows, :]
+        else:
+            a = a_ref[block, rows, :]
+            copies[i].wait()
+            b = in_ref[i]
         o_ref[rows, :] = (a.astype(jnp.float32) + b.astype(jnp.float32)).astype(jnp.bfloat16)
 
 
 def add_blocks(a, b, block=None):
+    depth, width = a.shape[-2:]
+    scratch = [
+        pltpu.VMEM((PIECES, depth // PIECES, width), jnp.bfloat16),
+        pltpu.SemaphoreType.DMA((PIECES,)),
+    ]
     return pl.pallas_call(
         functools.partial(add_kernel, block=block),
-        out_shape=jax.ShapeDtypeStruct(a.shape[-2:], jnp.bfloat16),
-        in_specs=[VMEM] * 2,
+        out_shape=jax.ShapeDtypeStruct((depth, width), jnp.bfloat16),
+        in_specs=[VMEM, VMEM if block is None else ANY],
         out_specs=VMEM,
+        scratch_shapes=[] if block is None else scratch,
         compiler_params=room(12),
         cost_estimate=SHORT,
         name="add",

time: 119 us -> 119 us (level)
  no operation moved by 1% of the time
where the time goes in v5:
time: 119 us; the launch traced here: 118 us
  starting transfers between devices  55.9 us (47%)
  waiting for transfers between devices  42.7 us (36%)
  Pallas kernels  18 us (15%)
    ppermute x11, starting transfers between devices, send(): lax.ppermute(value, axis, [(a, b) for a, b in pairs if 0 <= b < size])  35.5 us
    all_to_all x3, waiting for transfers between devices, along_z(): lax.all_to_all(value, 'expert', split_axis=0, concat_axis=0, tiled=True,...  21.6 us
    ppermute x11, waiting for transfers between devices, send(): lax.ppermute(value, axis, [(a, b) for a, b in pairs if 0 <= b < size])  21.1 us
    all_to_all x3, starting transfers between devices, along_z(): lax.all_to_all(value, 'expert', split_axis=0, concat_axis=0, tiled=True,...  20.4 us
    pallas_call x3, Pallas kernels, add_blocks(): pl.pallas_call(functools.partial(add_kernel, block=block), out_shape=jax....  4.82 us
    pallas_call x1, Pallas kernels, experts_backward(): pl.pallas_call(experts_kernel, out_shape=(rows, rows, units, units, rows)...  4.76 us
    pallas_call x2, Pallas kernels, prepare(): pl.pallas_call(functools.partial(prepare_kernel, copies), out_shape=jax.S...  3 us
    pallas_call x1, Pallas kernels, finish(): pl.pallas_call(finish_kernel, out_shape=(shape, shape), in_specs=[ANY] *...  2.64 us
  transfers between devices with their start and end apart: 14, of which 8 were waited for; matrix products, arithmetic and copies ran while one was open for 1% of the time, Pallas kernels for 11%

profile of v5, /device:TPU:39, one launch (start us, length us, event | category | flops | bytes accessed | tf_op | source)
XLA Modules:
  0.0 118.4 jit_solution(8663164293895468754)
XLA Ops:
  0.6 0.0 copy-start.1
  0.6 0.0 copy-start.2
  0.7 2.5 %prepare.3 = bf16[192,1792]{1,0:T(8,128)(2,1)} custom-call(bf16[64,3584]{1,0:T(8,128)(2,1)} %bitcast.49, bf16[64,3584]{1,0:T(8,128)(2,1)} %bitcast.4.c_ref, s32[8,64]{1,0:T(8,128)} %bitcast.42, f32[8,64]{1,0:T(8,128)} %bitcast.51), custom_call_target="tpu_custom_call" | custom-call | flops 1 | bytes 1 | tf_op jit(solution)/shard_map/prepare/pallas_call | solution.py:111
  3.2 0.0 copy-start.3
  3.2 0.0 copy-start.4
  3.2 0.0 copy-start.6
  3.2 0.0 copy-start.7
  3.2 10.2 %all-to-all-start = ((bf16[8,24,1792]{2,1,0:T(8,128)(2,1)}), bf16[8,24,1792]{2,1,0:T(8,128)(2,1)S(1)}, u32[]{:S(2)}, u32[]{:S(2)}) async-start(bf16[8,24,1792]{2,1,0:T(8,128)(2,1)} %bitcast.47), calls=%async_computation | async-start | bytes 1376256 | tf_op jit(solution)/shard_map/all_to_all | solution.py:372
  13.4 0.0 copy-done.1
  13.4 0.0 copy-done.2
  13.4 0.1 pack.1.refs_0_
  13.5 3.0 %collective-permute-start = (bf16[128,3584]{1,0:T(8,128)(2,1)S(1)}, bf16[128,3584]{1,0:T(8,128)(2,1)}, u32[]{:S(2)}, u32[]{:S(2)}) collective-permute-start(bf16[128,3584]{1,0:T(8,128)(2,1)S(1)} %pack.1.refs_0_), channel_id=1, source_target_pairs={{0,2},{1,3},{2,0},{3,1},{4,6},{5,7},{6,4},{7,5},{8,10},{9,11},{10,... | collective-permute-start | bytes 2752520 | tf_op jit(solution)/shard_map/ppermute | solution.py:34
  16.5 0.0 copy-done.3
  16.5 0.0 copy-done.4
  16.5 0.0 copy-done.6
  16.6 0.0 copy-done.7
  16.6 0.5 prepare.2
  17.0 1.9 %collective-permute-start.3 = (bf16[48,1792]{1,0:T(8,128)(2,1)S(1)}, bf16[48,1792]{1,0:T(8,128)(2,1)S(1)}, u32[]{:S(2)}, u32[]{:S(2)}) collective-permute-start(bf16[48,1792]{1,0:T(8,128)(2,1)S(1)} %prepare.2), channel_id=1, source_target_pairs={{0,480},{32,448},{64,416},{96,384},{128,352},{160,320},{192,288},{... | collective-permute-start | bytes 516104 | tf_op jit(solution)/shard_map/ppermute | solution.py:34
  19.0 3.3 %collective-permute-start.1 = (bf16[64,3584]{1,0:T(8,128)(2,1)}, bf16[64,3584]{1,0:T(8,128)(2,1)}, u32[]{:S(2)}, u32[]{:S(2)}) collective-permute-start(bf16[64,3584]{1,0:T(8,128)(2,1)} %bitcast.4.c_ref), channel_id=1, source_target_pairs={{32,0},{64,32},{96,64},{128,96},{160,128},{192,160},{224,192},{256... | collective-permute-start | bytes 1376264 | tf_op jit(solution)/shard_map/ppermute | solution.py:34
  22.2 8.6 %collective-permute-done.3 = bf16[48,1792]{1,0:T(8,128)(2,1)S(1)} collective-permute-done((bf16[48,1792]{1,0:T(8,128)(2,1)S(1)}, bf16[48,1792]{1,0:T(8,128)(2,1)S(1)}, u32[]{:S(2)}, u32[]{:S(2)}) %collective-permute-start.3) | collective-permute-done | bytes 172064 | tf_op jit(solution)/shard_map/ppermute | solution.py:34
  30.8 4.1 %all-to-all-done = bf16[8,24,1792]{2,1,0:T(8,128)(2,1)S(1)} async-done(((bf16[8,24,1792]{2,1,0:T(8,128)(2,1)}), bf16[8,24,1792]{2,1,0:T(8,128)(2,1)S(1)}, u32[]{:S(2)}, u32[]{:S(2)}) %all-to-all-start) | async-done | bytes 688160 | tf_op jit(solution)/shard_map/all_to_all | solution.py:372
  34.9 0.9 broadcast_in_dim.12
  35.8 3.5 %all-to-all-start.1 = ((bf16[8,24,1792]{2,1,0:T(8,128)(2,1)}), bf16[8,24,1792]{2,1,0:T(8,128)(2,1)S(1)}, u32[]{:S(2)}, u32[]{:S(2)}) async-start(bf16[8,24,1792]{2,1,0:T(8,128)(2,1)} %bitcast.21), calls=%async_computation.1 | async-start | bytes 1376256 | tf_op jit(solution)/shard_map/all_to_all | solution.py:372
  39.3 2.3 %collective-permute-start.2 = (s32[8,64]{1,0:T(8,128)S(1)}, s32[8,64]{1,0:T(8,128)S(1)}, u32[]{:S(2)}, u32[]{:S(2)}) collective-permute-start(s32[8,64]{1,0:T(8,128)S(1)} %bitcast.46), channel_id=1, source_target_pairs={{0,480},{32,448},{64,416},{96,384},{128,352},{160,320},{192,288},{... | collective-permute-start | bytes 6152 | tf_op jit(solution)/shard_map/ppermute | solution.py:34
  41.7 3.3 %collective-permute-start.4 = (bf16[128,3584]{1,0:T(8,128)(2,1)S(1)}, bf16[128,3584]{1,0:T(8,128)(2,1)S(1)}, u32[]{:S(2)}, u32[]{:S(2)}) collective-permute-start(bf16[128,3584]{1,0:T(8,128)(2,1)S(1)} %pack.1.refs_0_), channel_id=1, source_target_pairs={{0,1},{1,0},{2,3},{3,2},{4,5},{5,4},{6,7},{7,6},{8,9},{9,8},{10,11... | collective-permute-start | bytes 2752520 | tf_op jit(solution)/shard_map/ppermute | solution.py:34
  45.0 0.9 collective-permute-done.2.re_ref
  45.9 3.1 %collective-permute-done.1.l_ref = bf16[64,3584]{1,0:T(8,128)(2,1)} collective-permute-done((bf16[64,3584]{1,0:T(8,128)(2,1)}, bf16[64,3584]{1,0:T(8,128)(2,1)}, u32[]{:S(2)}, u32[]{:S(2)}) %collective-permute-start.1) | collective-permute-done | bytes 458784 | tf_op jit(solution)/shard_map/ppermute | solution.py:34
  48.9 0.0 collective-permute-done.refs_2_
  48.9 3.8 %collective-permute-start.5 = (bf16[128,3584]{1,0:T(8,128)(2,1)}, bf16[128,3584]{1,0:T(8,128)(2,1)}, u32[]{:S(2)}, u32[]{:S(2)}) collective-permute-start(bf16[128,3584]{1,0:T(8,128)(2,1)} %collective-permute-done.refs_2_), channel_id=1, source_target_pairs={{0,1},{1,0},{2,3},{3,2},{4,5},{5,4},{6,7},{7,6},{8,9},{9,8},{10,11... | collective-permute-start | bytes 2752520 | tf_op jit(solution)/shard_map/ppermute | solution.py:34
  52.7 5.1 %collective-permute-start.6 = (bf16[64,3584]{1,0:T(8,128)(2,1)}, bf16[64,3584]{1,0:T(8,128)(2,1)}, u32[]{:S(2)}, u32[]{:S(2)}) collective-permute-start(bf16[64,3584]{1,0:T(8,128)(2,1)} %bitcast.40), channel_id=1, source_target_pairs={{0,32},{32,64},{64,96},{96,128},{128,160},{160,192},{192,224},{224... | collective-permute-start | bytes 1376264 | tf_op jit(solution)/shard_map/ppermute | solution.py:34
  57.8 0.0 collective-permute-done.4.refs_1_
  57.8 0.0 collective-permute-done.5.refs_3_
  57.9 1.2 all-to-all-done.1
  59.0 4.8 %experts.1 = (bf16[192,1792]{1,0:T(8,128)(2,1)S(1)}, bf16[192,1792]{1,0:T(8,128)(2,1)S(1)}, bf16[96,512]{1,0:T(8,128)(2,1)S(1)}, bf16[96,512]{1,0:T(8,128)(2,1)S(1)}, bf16[192,1792]{1,0:T(8,128)(2,1)S(1)}) custom-call(bf16[192,1792]{1,0:T(8,128)(2,1)S(1)} %bitcast.33, bf16[192,1792]{1,0:T(8,128)(2,1)S(1)} %bitcast.34, bf16[128,3584]{1,0:T(8,128)(2,1)S(1)} %pack.1.refs_0_, ...), custom_call_target="tpu_custom_call" | custom-call | flops 1 | bytes 1 | tf_op jit(solution)/shard_map/experts/pallas_call | solution.py:178
  63.8 0.0 copy-start
  63.8 2.4 %gradient.1 = (bf16[2,3584,128]{2,1,0:T(8,128)(2,1)S(1)}, bf16[2,3584,128]{2,1,0:T(8,128)(2,1)}) custom-call(bf16[192,1792]{1,0:T(8,128)(2,1)S(1)} %get-tuple-element.27.la_ref, bf16[192,1792]{1,0:T(8,128)(2,1)S(1)} %get-tuple-element.28.ra_ref, bf16[96,512]{1,0:T(8,128)(2,1)S(1)} %get-tuple-element.29.da_ref, bf16[96,512]{1,0:T(8,128)(2,1)S(1)} %get-tuple-element.30.hid_ref), custom_call_target="tpu_custom_call" | custom-call | flops 1 | bytes 1 | tf_op jit(solution)/shard_map/gradient/pallas_call | solution.py:217
  66.2 2.7 %collective-permute-done.6.r_ref = bf16[64,3584]{1,0:T(8,128)(2,1)} collective-permute-done((bf16[64,3584]{1,0:T(8,128)(2,1)}, bf16[64,3584]{1,0:T(8,128)(2,1)}, u32[]{:S(2)}, u32[]{:S(2)}) %collective-permute-start.6) | collective-permute-done | bytes 458784 | tf_op jit(solution)/shard_map/ppermute | solution.py:34
  68.9 2.5 %collective-permute-start.8 = (bf16[2,3584,128]{2,1,0:T(8,128)(2,1)}, bf16[2,3584,128]{2,1,0:T(8,128)(2,1)}, u32[]{:S(2)}, u32[]{:S(2)}) collective-permute-start(bf16[2,3584,128]{2,1,0:T(8,128)(2,1)} %get-tuple-element.37), channel_id=1, source_target_pairs={{0,1},{1,0},{2,3},{3,2},{4,5},{5,4},{6,7},{7,6},{8,9},{9,8},{10,11... | collective-permute-start | bytes 5505032 | tf_op jit(solution)/shard_map/ppermute | solution.py:34
  71.4 0.0 copy-done
  71.4 6.7 %all-to-all-start.2 = ((bf16[8,24,1792]{2,1,0:T(8,128)(2,1)}), bf16[8,24,1792]{2,1,0:T(8,128)(2,1)S(1)}, u32[]{:S(2)}, u32[]{:S(2)}) async-start(bf16[8,24,1792]{2,1,0:T(8,128)(2,1)} %bitcast.36), calls=%async_computation.2 | async-start | bytes 1376256 | tf_op jit(solution)/shard_map/all_to_all | solution.py:372
  78.1 0.0 collective-permute-done.8.b_ref
  78.1 0.0 copy-start.5
  78.1 2.3 %add.4 = bf16[3584,128]{1,0:T(8,128)(2,1)} custom-call(bf16[2,3584,128]{2,1,0:T(8,128)(2,1)S(1)} %get-tuple-element.36.a_ref, bf16[2,3584,128]{2,1,0:T(8,128)(2,1)} %collective-permute-done.8.b_ref), custom_call_target="tpu_custom_call" | custom-call | flops 1 | bytes 1 | tf_op jit(solution)/shard_map/add/pallas_call | solution.py:253
  80.4 2.8 %collective-permute-start.9 = (bf16[3584,128]{1,0:T(8,128)(2,1)}, bf16[3584,128]{1,0:T(8,128)(2,1)S(1)}, u32[]{:S(2)}, u32[]{:S(2)}) collective-permute-start(bf16[3584,128]{1,0:T(8,128)(2,1)} %add.4), channel_id=1, source_target_pairs={{0,2},{1,3},{2,0},{3,1},{4,6},{5,7},{6,4},{7,5},{8,10},{9,11},{10,... | collective-permute-start | bytes 2752520 | tf_op jit(solution)/shard_map/ppermute | solution.py:34
  83.2 16.3 %all-to-all-done.2 = bf16[8,24,1792]{2,1,0:T(8,128)(2,1)S(1)} async-done(((bf16[8,24,1792]{2,1,0:T(8,128)(2,1)}), bf16[8,24,1792]{2,1,0:T(8,128)(2,1)S(1)}, u32[]{:S(2)}, u32[]{:S(2)}) %all-to-all-start.2) | async-done | bytes 688160 | tf_op jit(solution)/shard_map/all_to_all | solution.py:372
  99.6 0.0 copy-done.5
  99.6 0.3 collect.1
  99.8 5.5 %collective-permute-start.7 = (bf16[32,1792]{1,0:T(8,128)(2,1)S(1)}, bf16[32,1792]{1,0:T(8,128)(2,1)S(1)}, u32[]{:S(2)}, u32[]{:S(2)}) collective-permute-start(bf16[32,1792]{1,0:T(8,128)(2,1)S(1)} %get-tuple-element.35), channel_id=1, source_target_pairs={{32,0},{64,32},{96,64},{128,96},{160,128},{192,160},{224,192},{256... | collective-permute-start | bytes 344072 | tf_op jit(solution)/shard_map/ppermute | solution.py:34
  105.3 1.9 %collective-permute-start.10 = (bf16[32,1792]{1,0:T(8,128)(2,1)S(1)}, bf16[32,1792]{1,0:T(8,128)(2,1)S(1)}, u32[]{:S(2)}, u32[]{:S(2)}) collective-permute-start(bf16[32,1792]{1,0:T(8,128)(2,1)S(1)} %get-tuple-element.39), channel_id=1, source_target_pairs={{32,480},{64,448},{96,416},{128,384},{160,352},{192,320},{224,288}... | collective-permute-start | bytes 344072 | tf_op jit(solution)/shard_map/ppermute | solution.py:34
  107.3 1.4 %add.3.a_ref = bf16[3584,128]{1,0:T(8,128)(2,1)S(1)} custom-call(bf16[2,3584,128]{2,1,0:T(8,128)(2,1)S(1)} %get-tuple-element.36.a_ref, bf16[2,3584,128]{2,1,0:T(8,128)(2,1)} %collective-permute-done.8.b_ref), custom_call_target="tpu_custom_call" | custom-call | flops 1 | bytes 1 | tf_op jit(solution)/shard_map/add/pallas_call | solution.py:253
  108.6 0.0 collective-permute-done.9.b_ref
  108.6 1.2 add.5
  109.8 0.0 collective-permute-done.7.lm_ref
  109.8 5.9 %collective-permute-done.10.rm_ref = bf16[32,1792]{1,0:T(8,128)(2,1)S(1)} collective-permute-done((bf16[32,1792]{1,0:T(8,128)(2,1)S(1)}, bf16[32,1792]{1,0:T(8,128)(2,1)S(1)}, u32[]{:S(2)}, u32[]{:S(2)}) %collective-permute-start.10) | collective-permute-done | bytes 114720 | tf_op jit(solution)/shard_map/ppermute | solution.py:34
  115.8 2.6 %finish.1 = (bf16[64,3584]{1,0:T(8,128)(2,1)}, bf16[64,3584]{1,0:T(8,128)(2,1)}) custom-call(bf16[64,3584]{1,0:T(8,128)(2,1)} %collective-permute-done.1.l_ref, bf16[64,3584]{1,0:T(8,128)(2,1)} %collective-permute-done.6.r_ref, bf16[32,1792]{1,0:T(8,128)(2,1)S(1)} %collective-permute-done.7.lm_ref, bf16[32,1792]{1,0:T(8,128)(2,1)S(1)} %collective-permute-done.10.rm_ref), custom_call_target="tpu_custom_call" | custom-call | flops 1 | bytes 1 | tf_op jit(solution)/shard_map/finish/pallas_call | solution.py:342
Async XLA Ops:
  0.6 12.8 %copy-start.1 = (bf16[1,3584,64]{1,2,0:T(8,128)(2,1)S(1)}, bf16[1,3584,64]{1,2,0:T(8,128)(2,1)}, u32[]{:S(2)}) copy-start(bf16[1,3584,64]{1,2,0:T(8,128)(2,1)} %param.18) | copy-start | bytes 1376260
  0.6 12.8 %copy-start.2 = (bf16[1,3584,64]{1,2,0:T(8,128)(2,1)S(1)}, bf16[1,3584,64]{1,2,0:T(8,128)(2,1)}, u32[]{:S(2)}) copy-start(bf16[1,3584,64]{1,2,0:T(8,128)(2,1)} %param.19) | copy-start | bytes 1376260
  3.2 13.3 %copy-start.3 = (bf16[1,64,3584]{2,1,0:T(8,128)(2,1)S(1)}, bf16[1,64,3584]{2,1,0:T(8,128)(2,1)}, u32[]{:S(2)}) copy-start(bf16[1,64,3584]{2,1,0:T(8,128)(2,1)} %param.14) | copy-start | bytes 1376260
  3.2 13.3 %copy-start.4 = (bf16[1,64,3584]{2,1,0:T(8,128)(2,1)S(1)}, bf16[1,64,3584]{2,1,0:T(8,128)(2,1)}, u32[]{:S(2)}) copy-start(bf16[1,64,3584]{2,1,0:T(8,128)(2,1)} %param.15) | copy-start | bytes 1376260
  3.2 13.3 %copy-start.6 = (f32[1,64,8]{1,2,0:T(8,128)S(1)}, f32[1,64,8]{1,2,0:T(8,128)}, u32[]{:S(2)}) copy-start(f32[1,64,8]{1,2,0:T(8,128)} %param.17) | copy-start | bytes 6148
  3.2 13.4 %copy-start.7 = (s32[1,64,8]{1,2,0:T(8,128)S(1)}, s32[1,64,8]{1,2,0:T(8,128)}, u32[]{:S(2)}) copy-start(s32[1,64,8]{1,2,0:T(8,128)} %param.16) | copy-start | bytes 6148
  3.2 31.6 %all-to-all-start = ((bf16[8,24,1792]{2,1,0:T(8,128)(2,1)}), bf16[8,24,1792]{2,1,0:T(8,128)(2,1)S(1)}, u32[]{:S(2)}, u32[]{:S(2)}) async-start(bf16[8,24,1792]{2,1,0:T(8,128)(2,1)} %bitcast.47), calls=%async_computation | async-start | bytes 1376256 | tf_op jit(solution)/shard_map/all_to_all | solution.py:372
  13.5 35.4 %collective-permute-start = (bf16[128,3584]{1,0:T(8,128)(2,1)S(1)}, bf16[128,3584]{1,0:T(8,128)(2,1)}, u32[]{:S(2)}, u32[]{:S(2)}) collective-permute-start(bf16[128,3584]{1,0:T(8,128)(2,1)S(1)} %pack.1.refs_0_), channel_id=1, source_target_pairs={{0,2},{1,3},{2,0},{3,1},{4,6},{5,7},{6,4},{7,5},{8,10},{9,11},{10,... | collective-permute-start | bytes 2752520 | tf_op jit(solution)/shard_map/ppermute | solution.py:34
  17.0 13.7 %collective-permute-start.3 = (bf16[48,1792]{1,0:T(8,128)(2,1)S(1)}, bf16[48,1792]{1,0:T(8,128)(2,1)S(1)}, u32[]{:S(2)}, u32[]{:S(2)}) collective-permute-start(bf16[48,1792]{1,0:T(8,128)(2,1)S(1)} %prepare.2), channel_id=1, source_target_pairs={{0,480},{32,448},{64,416},{96,384},{128,352},{160,320},{192,288},{... | collective-permute-start | bytes 516104 | tf_op jit(solution)/shard_map/ppermute | solution.py:34
  19.0 30.0 %collective-permute-start.1 = (bf16[64,3584]{1,0:T(8,128)(2,1)}, bf16[64,3584]{1,0:T(8,128)(2,1)}, u32[]{:S(2)}, u32[]{:S(2)}) collective-permute-start(bf16[64,3584]{1,0:T(8,128)(2,1)} %bitcast.4.c_ref), channel_id=1, source_target_pairs={{32,0},{64,32},{96,64},{128,96},{160,128},{192,160},{224,192},{256... | collective-permute-start | bytes 1376264 | tf_op jit(solution)/shard_map/ppermute | solution.py:34
  35.8 23.3 %all-to-all-start.1 = ((bf16[8,24,1792]{2,1,0:T(8,128)(2,1)}), bf16[8,24,1792]{2,1,0:T(8,128)(2,1)S(1)}, u32[]{:S(2)}, u32[]{:S(2)}) async-start(bf16[8,24,1792]{2,1,0:T(8,128)(2,1)} %bitcast.21), calls=%async_computation.1 | async-start | bytes 1376256 | tf_op jit(solution)/shard_map/all_to_all | solution.py:372
  39.3 6.6 %collective-permute-start.2 = (s32[8,64]{1,0:T(8,128)S(1)}, s32[8,64]{1,0:T(8,128)S(1)}, u32[]{:S(2)}, u32[]{:S(2)}) collective-permute-start(s32[8,64]{1,0:T(8,128)S(1)} %bitcast.46), channel_id=1, source_target_pairs={{0,480},{32,448},{64,416},{96,384},{128,352},{160,320},{192,288},{... | collective-permute-start | bytes 6152 | tf_op jit(solution)/shard_map/ppermute | solution.py:34
  41.7 16.2 %collective-permute-start.4 = (bf16[128,3584]{1,0:T(8,128)(2,1)S(1)}, bf16[128,3584]{1,0:T(8,128)(2,1)S(1)}, u32[]{:S(2)}, u32[]{:S(2)}) collective-permute-start(bf16[128,3584]{1,0:T(8,128)(2,1)S(1)} %pack.1.refs_0_), channel_id=1, source_target_pairs={{0,1},{1,0},{2,3},{3,2},{4,5},{5,4},{6,7},{7,6},{8,9},{9,8},{10,11... | collective-permute-start | bytes 2752520 | tf_op jit(solution)/shard_map/ppermute | solution.py:34
  48.9 8.9 %collective-permute-start.5 = (bf16[128,3584]{1,0:T(8,128)(2,1)}, bf16[128,3584]{1,0:T(8,128)(2,1)}, u32[]{:S(2)}, u32[]{:S(2)}) collective-permute-start(bf16[128,3584]{1,0:T(8,128)(2,1)} %collective-permute-done.refs_2_), channel_id=1, source_target_pairs={{0,1},{1,0},{2,3},{3,2},{4,5},{5,4},{6,7},{7,6},{8,9},{9,8},{10,11... | collective-permute-start | bytes 2752520 | tf_op jit(solution)/shard_map/ppermute | solution.py:34
  52.7 16.2 %collective-permute-start.6 = (bf16[64,3584]{1,0:T(8,128)(2,1)}, bf16[64,3584]{1,0:T(8,128)(2,1)}, u32[]{:S(2)}, u32[]{:S(2)}) collective-permute-start(bf16[64,3584]{1,0:T(8,128)(2,1)} %bitcast.40), channel_id=1, source_target_pairs={{0,32},{32,64},{64,96},{96,128},{128,160},{160,192},{192,224},{224... | collective-permute-start | bytes 1376264 | tf_op jit(solution)/shard_map/ppermute | solution.py:34
  63.8 7.6 %copy-start = (bf16[192,1792]{1,0:T(8,128)(2,1)}, bf16[192,1792]{1,0:T(8,128)(2,1)S(1)}, u32[]{:S(2)}) copy-start(bf16[192,1792]{1,0:T(8,128)(2,1)S(1)} %get-tuple-element.33) | copy-start | bytes 2064388
  68.9 9.2 %collective-permute-start.8 = (bf16[2,3584,128]{2,1,0:T(8,128)(2,1)}, bf16[2,3584,128]{2,1,0:T(8,128)(2,1)}, u32[]{:S(2)}, u32[]{:S(2)}) collective-permute-start(bf16[2,3584,128]{2,1,0:T(8,128)(2,1)} %get-tuple-element.37), channel_id=1, source_target_pairs={{0,1},{1,0},{2,3},{3,2},{4,5},{5,4},{6,7},{7,6},{8,9},{9,8},{10,11... | collective-permute-start | bytes 5505032 | tf_op jit(solution)/shard_map/ppermute | solution.py:34
  71.4 28.1 %all-to-all-start.2 = ((bf16[8,24,1792]{2,1,0:T(8,128)(2,1)}), bf16[8,24,1792]{2,1,0:T(8,128)(2,1)S(1)}, u32[]{:S(2)}, u32[]{:S(2)}) async-start(bf16[8,24,1792]{2,1,0:T(8,128)(2,1)} %bitcast.36), calls=%async_computation.2 | async-start | bytes 1376256 | tf_op jit(solution)/shard_map/all_to_all | solution.py:372
  78.1 21.5 %copy-start.5 = (s32[1,64,8]{1,2,0:T(8,128)S(1)}, s32[1,64,8]{1,2,0:T(8,128)}, u32[]{:S(2)}) copy-start(s32[1,64,8]{1,2,0:T(8,128)} %param.12) | copy-start | bytes 6148
  80.4 28.2 %collective-permute-start.9 = (bf16[3584,128]{1,0:T(8,128)(2,1)}, bf16[3584,128]{1,0:T(8,128)(2,1)S(1)}, u32[]{:S(2)}, u32[]{:S(2)}) collective-permute-start(bf16[3584,128]{1,0:T(8,128)(2,1)} %add.4), channel_id=1, source_target_pairs={{0,2},{1,3},{2,0},{3,1},{4,6},{5,7},{6,4},{7,5},{8,10},{9,11},{10,... | collective-permute-start | bytes 2752520 | tf_op jit(solution)/shard_map/ppermute | solution.py:34
  99.8 10.0 %collective-permute-start.7 = (bf16[32,1792]{1,0:T(8,128)(2,1)S(1)}, bf16[32,1792]{1,0:T(8,128)(2,1)S(1)}, u32[]{:S(2)}, u32[]{:S(2)}) collective-permute-start(bf16[32,1792]{1,0:T(8,128)(2,1)S(1)} %get-tuple-element.35), channel_id=1, source_target_pairs={{32,0},{64,32},{96,64},{128,96},{160,128},{192,160},{224,192},{256... | collective-permute-start | bytes 344072 | tf_op jit(solution)/shard_map/ppermute | solution.py:34
  105.3 10.4 %collective-permute-start.10 = (bf16[32,1792]{1,0:T(8,128)(2,1)S(1)}, bf16[32,1792]{1,0:T(8,128)(2,1)S(1)}, u32[]{:S(2)}, u32[]{:S(2)}) collective-permute-start(bf16[32,1792]{1,0:T(8,128)(2,1)S(1)} %get-tuple-element.39), channel_id=1, source_target_pairs={{32,480},{64,448},{96,416},{128,384},{160,352},{192,320},{224,288}... | collective-permute-start | bytes 344072 | tf_op jit(solution)/shard_map/ppermute | solution.py:34
